TPU v7x, 512 devices: a whole 4x4x16 slice. The times are simulated.
512 devices in a mesh: gx: 16 (over z), gy: 32 (over x, y, core).
Axes of the slice: x: 4, y: 4, z: 16, core: 2. Of those that a mesh axis runs over, the one named last changes fastest.
Arguments:
- samples: bfloat16 [524288, 32], P(('gx', 'gy')), may hold values from -6 to 6
- site_order: int32 [524288], P(('gx', 'gy')), may hold values from 0 to 1023, as said below
- leaf_basis: bfloat16 [64, 128, 64, 32], P('gx', 'gy'), may hold values from -0.75 to 0.75
- near_blocks: bfloat16 [64, 128, 9, 64, 64], P('gx', 'gy'), may hold values from -0.25 to 0.25
- transfer: bfloat16 [2, 4, 32, 32], replicated, may hold values from -0.75 to 0.75
- coupling: bfloat16 [3, 40, 32, 32], replicated, may hold values from -0.21875 to 0.21875
Outputs:
- covariance_product: bfloat16 [524288, 32], P(('gx', 'gy'))
Inputs may be any that keep to these rules, and one draw needn't show every extreme that they name: `site_order`: each device's block of 1024 consecutive entries, devices ordered by gx then gy, is a permutation of 0 to 1023.
All inputs are finite; a program needn't handle non-finite values.
Results may differ from a plain program's by a relative error of at most 0.0065.
Values may be sent and summed in bfloat16 or wider, within the bound.
No kernel may reach another device: no remote copies, remote signals or barrier semaphores. Data moves between devices by JAX's collectives and lax.ppermute only.
A program may use at most 64 MiB of HBM per device.

v0:
```python
import jax
import jax.numpy as jnp
from jax import lax
from jax.sharding import PartitionSpec as P

LEVELS = 3


OFFSETS = [
    (shift_row, shift_column)
    for shift_row in range(-3, 4)
    for shift_column in range(-3, 4)
    if max(abs(shift_row), abs(shift_column)) >= 2
]


def shifted(block, axis, distance):
    devices = range(lax.axis_size(axis))
    route = [(i - distance, i) for i in devices if i - distance in devices]
    return lax.ppermute(block, axis, route)


def with_halo(block, sides, width):
    for axis, dim in sides:
        count = lax.axis_size(axis)
        forward = [(i, i + 1) for i in range(count - 1)]
        backward = [(target, source) for source, target in forward]
        low = lax.ppermute(
            lax.slice_in_dim(block, block.shape[dim] - width, None, axis=dim), axis, forward
        )
        high = lax.ppermute(lax.slice_in_dim(block, 0, width, axis=dim), axis, backward)
        block = jnp.concatenate([low, block, high], axis=dim)
    return block


def allowed(parity, offset):
    parent_step = jnp.floor_divide(parity + offset, 2)
    return (parent_step >= -1) & (parent_step <= 1)


def lift_level(expansions, matrices):
    row_count, column_count = (expansions.shape[0], expansions.shape[1])
    grouped = expansions.reshape(
        row_count // 2, 2, column_count // 2, 2, expansions.shape[2], expansions.shape[3]
    )
    blocks = matrices.reshape(2, 2, matrices.shape[1], matrices.shape[2])
    return jnp.einsum("xiyjkv,ijkm->xymv", grouped, blocks, preferred_element_type=jnp.float32)


def lower_level(downward, matrices):
    row_count, column_count = (downward.shape[0], downward.shape[1])
    blocks = matrices.reshape(2, 2, matrices.shape[1], matrices.shape[2])
    spread = jnp.einsum("ijkm,xymv->xiyjkv", blocks, downward, preferred_element_type=jnp.float32)
    return spread.reshape(2 * row_count, 2 * column_count, downward.shape[2], downward.shape[3])


def shift_rows(portion, offset):
    return shifted(portion, "gx", offset)


def shift_columns(portion, offset):
    return shifted(portion, "gy", offset)


def assemble(expansion, along, received, device_reach):
    extent = expansion.shape[along]
    pieces = []
    for distance in range(-device_reach, device_reach + 1):
        if distance == 0:
            pieces.append(expansion)
        else:
            pieces.append(received[distance])
    joined = jnp.concatenate(pieces, along)
    first_row = device_reach * extent - 3
    return lax.slice_in_dim(joined, first_row, first_row + extent + 6, axis=along)


def surround(expansion, along, shifter):
    extent = expansion.shape[along]
    device_reach = -(-3 // extent)
    received = {}
    for distance in range(-device_reach, device_reach + 1):
        if distance != 0:
            received[distance] = shifter(expansion, -distance)
    return assemble(expansion, along, received, device_reach)


def far_sum(padded, matrices, row_parity, column_parity):
    row_count = padded.shape[0] - 6
    column_count = padded.shape[1] - 6
    windows = []
    for position, (shift_row, shift_column) in enumerate(OFFSETS):
        window = padded[
            3 + shift_row : 3 + shift_row + row_count,
            3 + shift_column : 3 + shift_column + column_count,
        ]
        inside = (
            allowed(row_parity, shift_row)[:, None] & allowed(column_parity, shift_column)[None, :]
        ).astype(window.dtype)
        windows.append(window * inside[:, :, None, None])
    stacked = jnp.stack(windows, 0)
    return jnp.einsum("nabjv,nij->abiv", stacked, matrices, preferred_element_type=jnp.float32)


def level_far(expansions, matrices, padded_flat):
    row_count, column_count, basis_rank, vectors = expansions.shape
    padded = padded_flat.reshape(row_count + 6, column_count + 6, basis_rank, vectors)
    row_parity = (lax.axis_index("gx") * row_count + jnp.arange(row_count, dtype=jnp.int32)) % 2
    column_parity = (
        lax.axis_index("gy") * column_count + jnp.arange(column_count, dtype=jnp.int32)
    ) % 2
    return far_sum(padded, matrices, row_parity, column_parity)


def local(samples, site_order, leaf_basis, near_blocks, transfer, coupling):
    boxes_x, boxes_y, leaf_sites, basis_rank = leaf_basis.shape
    vectors = samples.shape[1]
    row_total = samples.shape[0]
    selector = (site_order[:, None] == jnp.arange(row_total, dtype=jnp.int32)[None, :]).astype(
        jnp.bfloat16
    )
    x_leaf = jnp.dot(selector, samples, preferred_element_type=jnp.float32).astype(jnp.bfloat16)
    x_leaf = x_leaf.reshape(boxes_x, boxes_y, leaf_sites, vectors)
    extended = with_halo(
        x_leaf.reshape(boxes_x, boxes_y, leaf_sites * vectors), (("gx", 0), ("gy", 1)), 1
    )
    extended = extended.reshape(boxes_x + 2, boxes_y + 2, leaf_sites, vectors)
    near_field = jnp.zeros((boxes_x, boxes_y, leaf_sites, vectors), jnp.float32)
    for position in range(9):
        shift_row = position // 3 - 1
        shift_column = position % 3 - 1
        window = extended[
            1 + shift_row : 1 + shift_row + boxes_x, 1 + shift_column : 1 + shift_column + boxes_y
        ]
        near_field = near_field + jnp.einsum(
            "abpq,abqv->abpv",
            near_blocks[:, :, position],
            window,
            preferred_element_type=jnp.float32,
        )
    expansions = [
        jnp.einsum(
            "abpk,abpv->abkv", leaf_basis, x_leaf, preferred_element_type=jnp.float32
        ).astype(jnp.bfloat16)
    ]
    for level_index in range(LEVELS - 1):
        expansions.append(lift_level(expansions[-1], transfer[level_index]).astype(jnp.bfloat16))
    flats = [
        current.reshape(current.shape[0], current.shape[1], basis_rank * vectors)
        for current in expansions
    ]
    shifted_count = LEVELS
    padded_list = [
        surround(surround(flats[level_index], 0, shift_rows), 1, shift_columns)
        for level_index in range(shifted_count)
    ]
    far_terms = [
        level_far(expansions[level_index], coupling[level_index], padded_list[level_index])
        for level_index in range(LEVELS)
    ]
    downward = far_terms[-1].astype(jnp.bfloat16)
    for level_index in reversed(range(LEVELS - 1)):
        downward = (far_terms[level_index] + lower_level(downward, transfer[level_index])).astype(
            jnp.bfloat16
        )
    combined = (
        jnp.einsum("abpk,abkv->abpv", leaf_basis, downward, preferred_element_type=jnp.float32)
        + near_field
    )
    combined = combined.astype(jnp.bfloat16).reshape(boxes_x * boxes_y * leaf_sites, vectors)
    placed = jnp.einsum("rs,rv->sv", selector, combined, preferred_element_type=jnp.float32)
    return placed.astype(jnp.bfloat16)


def solution(mesh):
    return jax.shard_map(
        local,
        mesh=mesh,
        in_specs=(
            P(("gx", "gy"), None),
            P(("gx", "gy")),
            P("gx", "gy", None, None),
            P("gx", "gy", None, None, None),
            P(),
            P(),
        ),
        out_specs=P(("gx", "gy"), None),
        check_vma=False,
    )
```

profile of v0, /device:TPU:38, one launch (start us, length us, event | category | flops | bytes accessed | tf_op | source)
XLA Modules:
  0.0 152.4 jit_solution(13420081963414768921)
XLA Ops:
  0.0 1.9 %fusion.18 = bf16[1024,32]{0,1:T(8,128)(2,1)S(1)} fusion(bf16[1024,32]{0,1:T(8,128)(2,1)} %param.6, s32[1024]{0:T(1024)} %param.7), kind=kOutput, calls=%fused_computation.22 | convolution fusion | flops 68190208 | bytes 135168 | tf_op jit(solution)/shard_map/dot_general | solution.py:122
  2.0 0.8 fusion.189
  3.5 5.2 %collective-permute-start.4 = (bf16[2,2,1024]{2,1,0:T(2,128)(2,1)S(1)}, bf16[2,2,1024]{2,1,0:T(2,128)(2,1)S(1)}, u32[]{:S(2)}, u32[]{:S(2)}) collective-permute-start(bf16[2,2,1024]{2,1,0:T(2,128)(2,1)S(1)} %reshape.3275), channel_id=1, source_target_pairs={{0,64},{32,96},{64,128},{96,160},{128,192},{160,224},{192,256},{22... | collective-permute-start | bytes 24584 | tf_op jit(solution)/shard_map/ppermute | solution.py:20
  8.7 5.0 %collective-permute-start.5 = (bf16[2,2,1024]{2,1,0:T(2,128)(2,1)S(1)}, bf16[2,2,1024]{2,1,0:T(2,128)(2,1)S(1)}, u32[]{:S(2)}, u32[]{:S(2)}) collective-permute-start(bf16[2,2,1024]{2,1,0:T(2,128)(2,1)S(1)} %reshape.3275), channel_id=1, source_target_pairs={{0,32},{32,64},{64,96},{96,128},{128,160},{160,192},{192,224},{224... | collective-permute-start | bytes 24584 | tf_op jit(solution)/shard_map/ppermute | solution.py:20
  13.8 1.9 %collective-permute-start.6 = (bf16[2,2,1024]{2,1,0:T(2,128)(2,1)S(1)}, bf16[2,2,1024]{2,1,0:T(2,128)(2,1)S(1)}, u32[]{:S(2)}, u32[]{:S(2)}) collective-permute-start(bf16[2,2,1024]{2,1,0:T(2,128)(2,1)S(1)} %reshape.3275), channel_id=1, source_target_pairs={{32,0},{64,32},{96,64},{128,96},{160,128},{192,160},{224,192},{256... | collective-permute-start | bytes 24584 | tf_op jit(solution)/shard_map/ppermute | solution.py:20
  15.7 1.3 collective-permute-start.7
  17.4 8.5 %collective-permute-start.12 = (bf16[1,1,1024]{2,1,0:T(2,128)(2,1)S(1)}, bf16[1,1,1024]{2,1,0:T(2,128)(2,1)S(1)}, u32[]{:S(2)}, u32[]{:S(2)}) collective-permute-start(bf16[1,1,1024]{2,1,0:T(2,128)(2,1)S(1)} %reshape.3277), channel_id=1, source_target_pairs={{0,96},{32,128},{64,160},{96,192},{128,224},{160,256},{192,288},{2... | collective-permute-start | bytes 6152 | tf_op jit(solution)/shard_map/ppermute | solution.py:20
  27.2 1.3 copy.48
  29.3 0.9 and_convert_fusion.40
  30.7 0.7 copy.57
  32.1 5.2 %collective-permute-start.13 = (bf16[1,1,1024]{2,1,0:T(2,128)(2,1)S(1)}, bf16[1,1,1024]{2,1,0:T(2,128)(2,1)S(1)}, u32[]{:S(2)}, u32[]{:S(2)}) collective-permute-start(bf16[1,1,1024]{2,1,0:T(2,128)(2,1)S(1)} %reshape.3277), channel_id=1, source_target_pairs={{0,64},{32,96},{64,128},{96,160},{128,192},{160,224},{192,256},{22... | collective-permute-start | bytes 6152 | tf_op jit(solution)/shard_map/ppermute | solution.py:20
  37.3 1.3 collective-permute-done.13
  38.6 3.6 %collective-permute-start.14 = (bf16[1,1,1024]{2,1,0:T(2,128)(2,1)S(1)}, bf16[1,1,1024]{2,1,0:T(2,128)(2,1)S(1)}, u32[]{:S(2)}, u32[]{:S(2)}) collective-permute-start(bf16[1,1,1024]{2,1,0:T(2,128)(2,1)S(1)} %reshape.3277), channel_id=1, source_target_pairs={{0,32},{32,64},{64,96},{96,128},{128,160},{160,192},{192,224},{224... | collective-permute-start | bytes 6152 | tf_op jit(solution)/shard_map/ppermute | solution.py:20
  42.3 1.8 %collective-permute-done.14 = bf16[1,1,1024]{2,1,0:T(2,128)(2,1)S(1)} collective-permute-done((bf16[1,1,1024]{2,1,0:T(2,128)(2,1)S(1)}, bf16[1,1,1024]{2,1,0:T(2,128)(2,1)S(1)}, u32[]{:S(2)}, u32[]{:S(2)}) %collective-permute-start.14) | collective-permute-done | bytes 2080 | tf_op jit(solution)/shard_map/ppermute | solution.py:20
  44.1 1.9 %collective-permute-start.15 = (bf16[1,1,1024]{2,1,0:T(2,128)(2,1)S(1)}, bf16[1,1,1024]{2,1,0:T(2,128)(2,1)S(1)}, u32[]{:S(2)}, u32[]{:S(2)}) collective-permute-start(bf16[1,1,1024]{2,1,0:T(2,128)(2,1)S(1)} %reshape.3277), channel_id=1, source_target_pairs={{32,0},{64,32},{96,64},{128,96},{160,128},{192,160},{224,192},{256... | collective-permute-start | bytes 6152 | tf_op jit(solution)/shard_map/ppermute | solution.py:20
  46.1 3.9 %collective-permute-done.15 = bf16[1,1,1024]{2,1,0:T(2,128)(2,1)S(1)} collective-permute-done((bf16[1,1,1024]{2,1,0:T(2,128)(2,1)S(1)}, bf16[1,1,1024]{2,1,0:T(2,128)(2,1)S(1)}, u32[]{:S(2)}, u32[]{:S(2)}) %collective-permute-start.15) | collective-permute-done | bytes 2080 | tf_op jit(solution)/shard_map/ppermute | solution.py:20
  50.0 1.3 collective-permute-start.16
  51.3 7.1 %collective-permute-done.16 = bf16[1,1,1024]{2,1,0:T(2,128)(2,1)S(1)} collective-permute-done((bf16[1,1,1024]{2,1,0:T(2,128)(2,1)S(1)}, bf16[1,1,1024]{2,1,0:T(2,128)(2,1)S(1)}, u32[]{:S(2)}, u32[]{:S(2)}) %collective-permute-start.16) | collective-permute-done | bytes 2080 | tf_op jit(solution)/shard_map/ppermute | solution.py:20
  58.4 1.3 collective-permute-start.17
  59.7 7.2 %collective-permute-done.17 = bf16[1,1,1024]{2,1,0:T(2,128)(2,1)S(1)} collective-permute-done((bf16[1,1,1024]{2,1,0:T(2,128)(2,1)S(1)}, bf16[1,1,1024]{2,1,0:T(2,128)(2,1)S(1)}, u32[]{:S(2)}, u32[]{:S(2)}) %collective-permute-start.17) | collective-permute-done | bytes 2080 | tf_op jit(solution)/shard_map/ppermute | solution.py:20
  66.9 3.7 %collective-permute-start.24 = (bf16[1,4,2048]{2,1,0:T(4,128)(2,1)S(1)}, bf16[1,4,2048]{2,1,0:T(4,128)(2,1)S(1)}, u32[]{:S(2)}, u32[]{:S(2)}) collective-permute-start(bf16[1,4,2048]{2,1,0:T(4,128)(2,1)S(1)} %slice.591), channel_id=1, source_target_pairs={{0,32},{32,64},{64,96},{96,128},{128,160},{160,192},{192,224},{224... | collective-permute-start | bytes 49160 | tf_op jit(solution)/shard_map/ppermute | solution.py:28
  70.6 2.2 %collective-permute-start.25 = (bf16[1,4,2048]{2,1,0:T(4,128)(2,1)S(1)}, bf16[1,4,2048]{2,1,0:T(4,128)(2,1)S(1)}, u32[]{:S(2)}, u32[]{:S(2)}) collective-permute-start(bf16[1,4,2048]{2,1,0:T(4,128)(2,1)S(1)} %slice.593), channel_id=1, source_target_pairs={{32,0},{64,32},{96,64},{128,96},{160,128},{192,160},{224,192},{256... | collective-permute-start | bytes 49160 | tf_op jit(solution)/shard_map/ppermute | solution.py:31
  72.8 1.9 %collective-permute-start.18 = (bf16[7,1,1024]{2,1,0:T(2,128)(2,1)S(1)}, bf16[7,1,1024]{2,1,0:T(2,128)(2,1)S(1)}, u32[]{:S(2)}, u32[]{:S(2)}) collective-permute-start(bf16[7,1,1024]{2,1,0:T(2,128)(2,1)S(1)} %constant_dynamic-update-slice_fusion.85), channel_id=1, source_target_pairs={{0,3},{1,4},{2,5},{3,6},{4,7},{5,8},{6,9},{7,10},{8,11},{9,12},{10... | collective-permute-start | bytes 43016 | tf_op jit(solution)/shard_map/ppermute | solution.py:20
  74.8 3.5 %collective-permute-start.19 = (bf16[7,1,1024]{2,1,0:T(2,128)(2,1)S(1)}, bf16[7,1,1024]{2,1,0:T(2,128)(2,1)S(1)}, u32[]{:S(2)}, u32[]{:S(2)}) collective-permute-start(bf16[7,1,1024]{2,1,0:T(2,128)(2,1)S(1)} %constant_dynamic-update-slice_fusion.85), channel_id=1, source_target_pairs={{0,2},{1,3},{2,4},{3,5},{4,6},{5,7},{6,8},{7,9},{8,10},{9,11},{10,... | collective-permute-start | bytes 43016 | tf_op jit(solution)/shard_map/ppermute | solution.py:20
  78.3 4.0 %collective-permute-start.20 = (bf16[7,1,1024]{2,1,0:T(2,128)(2,1)S(1)}, bf16[7,1,1024]{2,1,0:T(2,128)(2,1)S(1)}, u32[]{:S(2)}, u32[]{:S(2)}) collective-permute-start(bf16[7,1,1024]{2,1,0:T(2,128)(2,1)S(1)} %constant_dynamic-update-slice_fusion.85), channel_id=1, source_target_pairs={{0,1},{1,2},{2,3},{3,4},{4,5},{5,6},{6,7},{7,8},{8,9},{9,10},{10,1... | collective-permute-start | bytes 43016 | tf_op jit(solution)/shard_map/ppermute | solution.py:20
  82.4 5.0 %collective-permute-start.21 = (bf16[7,1,1024]{2,1,0:T(2,128)(2,1)S(1)}, bf16[7,1,1024]{2,1,0:T(2,128)(2,1)S(1)}, u32[]{:S(2)}, u32[]{:S(2)}) collective-permute-start(bf16[7,1,1024]{2,1,0:T(2,128)(2,1)S(1)} %constant_dynamic-update-slice_fusion.85), channel_id=1, source_target_pairs={{1,0},{2,1},{3,2},{4,3},{5,4},{6,5},{7,6},{8,7},{9,8},{10,9},{11,1... | collective-permute-start | bytes 43016 | tf_op jit(solution)/shard_map/ppermute | solution.py:20
  87.4 2.3 %collective-permute-start.22 = (bf16[7,1,1024]{2,1,0:T(2,128)(2,1)S(1)}, bf16[7,1,1024]{2,1,0:T(2,128)(2,1)S(1)}, u32[]{:S(2)}, u32[]{:S(2)}) collective-permute-start(bf16[7,1,1024]{2,1,0:T(2,128)(2,1)S(1)} %constant_dynamic-update-slice_fusion.85), channel_id=1, source_target_pairs={{2,0},{3,1},{4,2},{5,3},{6,4},{7,5},{8,6},{9,7},{10,8},{11,9},{12,... | collective-permute-start | bytes 43016 | tf_op jit(solution)/shard_map/ppermute | solution.py:20
  89.7 1.9 %collective-permute-start.23 = (bf16[7,1,1024]{2,1,0:T(2,128)(2,1)S(1)}, bf16[7,1,1024]{2,1,0:T(2,128)(2,1)S(1)}, u32[]{:S(2)}, u32[]{:S(2)}) collective-permute-start(bf16[7,1,1024]{2,1,0:T(2,128)(2,1)S(1)} %constant_dynamic-update-slice_fusion.85), channel_id=1, source_target_pairs={{3,0},{4,1},{5,2},{6,3},{7,4},{8,5},{9,6},{10,7},{11,8},{12,9},{13... | collective-permute-start | bytes 43016 | tf_op jit(solution)/shard_map/ppermute | solution.py:20
  91.7 4.6 %collective-permute-start = (bf16[4,4,1024]{2,1,0:T(4,128)(2,1)S(1)}, bf16[4,4,1024]{2,1,0:T(4,128)(2,1)S(1)}, u32[]{:S(2)}, u32[]{:S(2)}) collective-permute-start(bf16[4,4,1024]{2,1,0:T(4,128)(2,1)S(1)} %reshape.3272), channel_id=1, source_target_pairs={{0,32},{32,64},{64,96},{96,128},{128,160},{160,192},{192,224},{224... | collective-permute-start | bytes 98312 | tf_op jit(solution)/shard_map/ppermute | solution.py:20
  96.4 1.9 %collective-permute-start.1 = (bf16[4,4,1024]{2,1,0:T(4,128)(2,1)S(1)}, bf16[4,4,1024]{2,1,0:T(4,128)(2,1)S(1)}, u32[]{:S(2)}, u32[]{:S(2)}) collective-permute-start(bf16[4,4,1024]{2,1,0:T(4,128)(2,1)S(1)} %reshape.3272), channel_id=1, source_target_pairs={{32,0},{64,32},{96,64},{128,96},{160,128},{192,160},{224,192},{256... | collective-permute-start | bytes 98312 | tf_op jit(solution)/shard_map/ppermute | solution.py:20
  98.3 2.4 %collective-permute-start.10 = (bf16[8,2,1024]{2,1,0:T(2,128)(2,1)S(1)}, bf16[8,2,1024]{2,1,0:T(2,128)(2,1)}, u32[]{:S(2)}, u32[]{:S(2)}) collective-permute-start(bf16[8,2,1024]{2,1,0:T(2,128)(2,1)S(1)} %slice.654), channel_id=1, source_target_pairs={{1,0},{2,1},{3,2},{4,3},{5,4},{6,5},{7,6},{8,7},{9,8},{10,9},{11,1... | collective-permute-start | bytes 98312 | tf_op jit(solution)/shard_map/ppermute | solution.py:20
  100.7 5.4 %collective-permute-start.11 = (bf16[8,2,1024]{2,1,0:T(2,128)(2,1)S(1)}, bf16[8,2,1024]{2,1,0:T(2,128)(2,1)}, u32[]{:S(2)}, u32[]{:S(2)}) collective-permute-start(bf16[8,2,1024]{2,1,0:T(2,128)(2,1)S(1)} %slice.654), channel_id=1, source_target_pairs={{2,0},{3,1},{4,2},{5,3},{6,4},{7,5},{8,6},{9,7},{10,8},{11,9},{12,... | collective-permute-start | bytes 98312 | tf_op jit(solution)/shard_map/ppermute | solution.py:20
  106.7 1.9 %collective-permute-start.8 = (bf16[8,2,1024]{2,1,0:T(2,128)(2,1)S(1)}, bf16[8,2,1024]{2,1,0:T(2,128)(2,1)}, u32[]{:S(2)}, u32[]{:S(2)}) collective-permute-start(bf16[8,2,1024]{2,1,0:T(2,128)(2,1)S(1)} %slice.654), channel_id=1, source_target_pairs={{0,2},{1,3},{2,4},{3,5},{4,6},{5,7},{6,8},{7,9},{8,10},{9,11},{10,... | collective-permute-start | bytes 98312 | tf_op jit(solution)/shard_map/ppermute | solution.py:20
  109.3 0.9 fusion.25
  110.2 1.9 %collective-permute-start.26 = (bf16[6,1,2048]{2,1,0:T(2,128)(2,1)S(1)}, bf16[6,1,2048]{2,1,0:T(2,128)(2,1)S(1)}, u32[]{:S(2)}, u32[]{:S(2)}) collective-permute-start(bf16[6,1,2048]{2,1,0:T(2,128)(2,1)S(1)} %get-tuple-element.8), channel_id=1, source_target_pairs={{0,1},{1,2},{2,3},{3,4},{4,5},{5,6},{6,7},{7,8},{8,9},{9,10},{10,1... | collective-permute-start | bytes 73736 | tf_op jit(solution)/shard_map/ppermute | solution.py:28
  112.1 5.8 %collective-permute-start.27 = (bf16[6,1,2048]{2,1,0:T(2,128)(2,1)S(1)}, bf16[6,1,2048]{2,1,0:T(2,128)(2,1)S(1)}, u32[]{:S(2)}, u32[]{:S(2)}) collective-permute-start(bf16[6,1,2048]{2,1,0:T(2,128)(2,1)S(1)} %get-tuple-element.9), channel_id=1, source_target_pairs={{1,0},{2,1},{3,2},{4,3},{5,4},{6,5},{7,6},{8,7},{9,8},{10,9},{11,1... | collective-permute-start | bytes 73736 | tf_op jit(solution)/shard_map/ppermute | solution.py:31
  118.0 1.9 %collective-permute-start.9 = (bf16[8,2,1024]{2,1,0:T(2,128)(2,1)S(1)}, bf16[8,2,1024]{2,1,0:T(2,128)(2,1)S(1)}, u32[]{:S(2)}, u32[]{:S(2)}) collective-permute-start(bf16[8,2,1024]{2,1,0:T(2,128)(2,1)S(1)} %slice.654), channel_id=1, source_target_pairs={{0,1},{1,2},{2,3},{3,4},{4,5},{5,6},{6,7},{7,8},{8,9},{9,10},{10,1... | collective-permute-start | bytes 98312 | tf_op jit(solution)/shard_map/ppermute | solution.py:20
  119.9 1.9 %collective-permute-start.2 = (bf16[10,4,1024]{2,1,0:T(4,128)(2,1)S(1)}, bf16[10,4,1024]{2,1,0:T(4,128)(2,1)}, u32[]{:S(2)}, u32[]{:S(2)}) collective-permute-start(bf16[10,4,1024]{2,1,0:T(4,128)(2,1)S(1)} %pad_maximum_fusion.3), channel_id=1, source_target_pairs={{0,1},{1,2},{2,3},{3,4},{4,5},{5,6},{6,7},{7,8},{8,9},{9,10},{10,1... | collective-permute-start | bytes 245768 | tf_op jit(solution)/shard_map/ppermute | solution.py:20
  122.4 1.4 fusion.28
  125.4 1.0 fusion.38
  126.4 1.0 fusion.40
  127.4 1.0 fusion.42
  128.5 5.9 %collective-permute-start.3 = (bf16[10,4,1024]{2,1,0:T(4,128)(2,1)S(1)}, bf16[10,4,1024]{2,1,0:T(4,128)(2,1)S(1)}, u32[]{:S(2)}, u32[]{:S(2)}) collective-permute-start(bf16[10,4,1024]{2,1,0:T(4,128)(2,1)S(1)} %pad_maximum_fusion.3), channel_id=1, source_target_pairs={{1,0},{2,1},{3,2},{4,3},{5,4},{6,5},{7,6},{8,7},{9,8},{10,9},{11,1... | collective-permute-start | bytes 245768 | tf_op jit(solution)/shard_map/ppermute | solution.py:20
  134.4 1.8 %concatenate.27 = bf16[8,10,1024]{2,1,0:T(8,128)(2,1)S(1)} concatenate(bf16[8,2,1024]{2,1,0:T(2,128)(2,1)} %collective-permute-done.8, bf16[8,2,1024]{2,1,0:T(2,128)(2,1)S(1)} %collective-permute-done.9, bf16[8,2,1024]{2,1,0:T(2,128)(2,1)S(1)} %copy-done.9, bf16[8,2,1024]{2,1,0:T(2,128)(2,1)} %collective-permute-done.10, bf16[8,2,1024]{2,1,0:T(2,128)(2,1)} %collective-permute-done.11), dimensions={1} | concatenate | bytes 327680 | tf_op jit(solution)/shard_map/concatenate | solution.py:73
  141.2 1.1 pad_maximum_fusion
  148.1 1.0 fusion
  149.4 1.3 fusion.17
  150.9 1.4 fusion.19
  (315 shorter events, 17.5 us)
Async XLA Ops:
  0.0 2.8 %copy-start = (bf16[4,4,64,32]{2,3,1,0:T(8,128)(2,1)S(1)}, bf16[4,4,64,32]{2,3,1,0:T(8,128)(2,1)}, u32[]{:S(2)}) copy-start(bf16[4,4,64,32]{2,3,1,0:T(8,128)(2,1)} %param.8) | copy-start | bytes 196612
  0.0 27.1 %copy-start.1 = (bf16[3,40,32,32]{1,3,2,0:T(8,128)(2,1)S(1)}, bf16[3,40,32,32]{1,3,2,0:T(8,128)(2,1)}, u32[]{:S(2)}) copy-start(bf16[3,40,32,32]{1,3,2,0:T(8,128)(2,1)} %param.11) | copy-start | bytes 737284
  2.8 23.8 %copy-start.6 = (bf16[1,4,32,32]{3,2,1,0:T(8,128)(2,1)}, bf16[1,4,32,32]{3,2,1,0:T(8,128)(2,1)S(1)}, u32[]{:S(2)}) copy-start(bf16[1,4,32,32]{3,2,1,0:T(8,128)(2,1)S(1)} %get-tuple-element.13) | copy-start | bytes 24580
  3.5 67.1 %collective-permute-start.4 = (bf16[2,2,1024]{2,1,0:T(2,128)(2,1)S(1)}, bf16[2,2,1024]{2,1,0:T(2,128)(2,1)S(1)}, u32[]{:S(2)}, u32[]{:S(2)}) collective-permute-start(bf16[2,2,1024]{2,1,0:T(2,128)(2,1)S(1)} %reshape.3275), channel_id=1, source_target_pairs={{0,64},{32,96},{64,128},{96,160},{128,192},{160,224},{192,256},{22... | collective-permute-start | bytes 24584 | tf_op jit(solution)/shard_map/ppermute | solution.py:20
  8.7 64.1 %collective-permute-start.5 = (bf16[2,2,1024]{2,1,0:T(2,128)(2,1)S(1)}, bf16[2,2,1024]{2,1,0:T(2,128)(2,1)S(1)}, u32[]{:S(2)}, u32[]{:S(2)}) collective-permute-start(bf16[2,2,1024]{2,1,0:T(2,128)(2,1)S(1)} %reshape.3275), channel_id=1, source_target_pairs={{0,32},{32,64},{64,96},{96,128},{128,160},{160,192},{192,224},{224... | collective-permute-start | bytes 24584 | tf_op jit(solution)/shard_map/ppermute | solution.py:20
  13.8 61.0 %collective-permute-start.6 = (bf16[2,2,1024]{2,1,0:T(2,128)(2,1)S(1)}, bf16[2,2,1024]{2,1,0:T(2,128)(2,1)S(1)}, u32[]{:S(2)}, u32[]{:S(2)}) collective-permute-start(bf16[2,2,1024]{2,1,0:T(2,128)(2,1)S(1)} %reshape.3275), channel_id=1, source_target_pairs={{32,0},{64,32},{96,64},{128,96},{160,128},{192,160},{224,192},{256... | collective-permute-start | bytes 24584 | tf_op jit(solution)/shard_map/ppermute | solution.py:20
  15.7 62.6 %collective-permute-start.7 = (bf16[2,2,1024]{2,1,0:T(2,128)(2,1)S(1)}, bf16[2,2,1024]{2,1,0:T(2,128)(2,1)S(1)}, u32[]{:S(2)}, u32[]{:S(2)}) collective-permute-start(bf16[2,2,1024]{2,1,0:T(2,128)(2,1)S(1)} %reshape.3275), channel_id=1, source_target_pairs={{64,0},{96,32},{128,64},{160,96},{192,128},{224,160},{256,192},{28... | collective-permute-start | bytes 24584 | tf_op jit(solution)/shard_map/ppermute | solution.py:20
  17.4 14.7 %collective-permute-start.12 = (bf16[1,1,1024]{2,1,0:T(2,128)(2,1)S(1)}, bf16[1,1,1024]{2,1,0:T(2,128)(2,1)S(1)}, u32[]{:S(2)}, u32[]{:S(2)}) collective-permute-start(bf16[1,1,1024]{2,1,0:T(2,128)(2,1)S(1)} %reshape.3277), channel_id=1, source_target_pairs={{0,96},{32,128},{64,160},{96,192},{128,224},{160,256},{192,288},{2... | collective-permute-start | bytes 6152 | tf_op jit(solution)/shard_map/ppermute | solution.py:20
  32.1 6.5 %collective-permute-start.13 = (bf16[1,1,1024]{2,1,0:T(2,128)(2,1)S(1)}, bf16[1,1,1024]{2,1,0:T(2,128)(2,1)S(1)}, u32[]{:S(2)}, u32[]{:S(2)}) collective-permute-start(bf16[1,1,1024]{2,1,0:T(2,128)(2,1)S(1)} %reshape.3277), channel_id=1, source_target_pairs={{0,64},{32,96},{64,128},{96,160},{128,192},{160,224},{192,256},{22... | collective-permute-start | bytes 6152 | tf_op jit(solution)/shard_map/ppermute | solution.py:20
  38.6 5.5 %collective-permute-start.14 = (bf16[1,1,1024]{2,1,0:T(2,128)(2,1)S(1)}, bf16[1,1,1024]{2,1,0:T(2,128)(2,1)S(1)}, u32[]{:S(2)}, u32[]{:S(2)}) collective-permute-start(bf16[1,1,1024]{2,1,0:T(2,128)(2,1)S(1)} %reshape.3277), channel_id=1, source_target_pairs={{0,32},{32,64},{64,96},{96,128},{128,160},{160,192},{192,224},{224... | collective-permute-start | bytes 6152 | tf_op jit(solution)/shard_map/ppermute | solution.py:20
  44.1 5.9 %collective-permute-start.15 = (bf16[1,1,1024]{2,1,0:T(2,128)(2,1)S(1)}, bf16[1,1,1024]{2,1,0:T(2,128)(2,1)S(1)}, u32[]{:S(2)}, u32[]{:S(2)}) collective-permute-start(bf16[1,1,1024]{2,1,0:T(2,128)(2,1)S(1)} %reshape.3277), channel_id=1, source_target_pairs={{32,0},{64,32},{96,64},{128,96},{160,128},{192,160},{224,192},{256... | collective-permute-start | bytes 6152 | tf_op jit(solution)/shard_map/ppermute | solution.py:20
  50.0 8.4 %collective-permute-start.16 = (bf16[1,1,1024]{2,1,0:T(2,128)(2,1)S(1)}, bf16[1,1,1024]{2,1,0:T(2,128)(2,1)S(1)}, u32[]{:S(2)}, u32[]{:S(2)}) collective-permute-start(bf16[1,1,1024]{2,1,0:T(2,128)(2,1)S(1)} %reshape.3277), channel_id=1, source_target_pairs={{64,0},{96,32},{128,64},{160,96},{192,128},{224,160},{256,192},{28... | collective-permute-start | bytes 6152 | tf_op jit(solution)/shard_map/ppermute | solution.py:20
  58.4 8.5 %collective-permute-start.17 = (bf16[1,1,1024]{2,1,0:T(2,128)(2,1)S(1)}, bf16[1,1,1024]{2,1,0:T(2,128)(2,1)S(1)}, u32[]{:S(2)}, u32[]{:S(2)}) collective-permute-start(bf16[1,1,1024]{2,1,0:T(2,128)(2,1)S(1)} %reshape.3277), channel_id=1, source_target_pairs={{96,0},{128,32},{160,64},{192,96},{224,128},{256,160},{288,192},{3... | collective-permute-start | bytes 6152 | tf_op jit(solution)/shard_map/ppermute | solution.py:20
  66.9 15.5 %collective-permute-start.24 = (bf16[1,4,2048]{2,1,0:T(4,128)(2,1)S(1)}, bf16[1,4,2048]{2,1,0:T(4,128)(2,1)S(1)}, u32[]{:S(2)}, u32[]{:S(2)}) collective-permute-start(bf16[1,4,2048]{2,1,0:T(4,128)(2,1)S(1)} %slice.591), channel_id=1, source_target_pairs={{0,32},{32,64},{64,96},{96,128},{128,160},{160,192},{192,224},{224... | collective-permute-start | bytes 49160 | tf_op jit(solution)/shard_map/ppermute | solution.py:28
  70.6 36.1 %collective-permute-start.25 = (bf16[1,4,2048]{2,1,0:T(4,128)(2,1)S(1)}, bf16[1,4,2048]{2,1,0:T(4,128)(2,1)S(1)}, u32[]{:S(2)}, u32[]{:S(2)}) collective-permute-start(bf16[1,4,2048]{2,1,0:T(4,128)(2,1)S(1)} %slice.593), channel_id=1, source_target_pairs={{32,0},{64,32},{96,64},{128,96},{160,128},{192,160},{224,192},{256... | collective-permute-start | bytes 49160 | tf_op jit(solution)/shard_map/ppermute | solution.py:31
  72.8 14.6 %collective-permute-start.18 = (bf16[7,1,1024]{2,1,0:T(2,128)(2,1)S(1)}, bf16[7,1,1024]{2,1,0:T(2,128)(2,1)S(1)}, u32[]{:S(2)}, u32[]{:S(2)}) collective-permute-start(bf16[7,1,1024]{2,1,0:T(2,128)(2,1)S(1)} %constant_dynamic-update-slice_fusion.85), channel_id=1, source_target_pairs={{0,3},{1,4},{2,5},{3,6},{4,7},{5,8},{6,9},{7,10},{8,11},{9,12},{10... | collective-permute-start | bytes 43016 | tf_op jit(solution)/shard_map/ppermute | solution.py:20
  74.8 15.0 %collective-permute-start.19 = (bf16[7,1,1024]{2,1,0:T(2,128)(2,1)S(1)}, bf16[7,1,1024]{2,1,0:T(2,128)(2,1)S(1)}, u32[]{:S(2)}, u32[]{:S(2)}) collective-permute-start(bf16[7,1,1024]{2,1,0:T(2,128)(2,1)S(1)} %constant_dynamic-update-slice_fusion.85), channel_id=1, source_target_pairs={{0,2},{1,3},{2,4},{3,5},{4,6},{5,7},{6,8},{7,9},{8,10},{9,11},{10,... | collective-permute-start | bytes 43016 | tf_op jit(solution)/shard_map/ppermute | solution.py:20
  78.3 13.4 %collective-permute-start.20 = (bf16[7,1,1024]{2,1,0:T(2,128)(2,1)S(1)}, bf16[7,1,1024]{2,1,0:T(2,128)(2,1)S(1)}, u32[]{:S(2)}, u32[]{:S(2)}) collective-permute-start(bf16[7,1,1024]{2,1,0:T(2,128)(2,1)S(1)} %constant_dynamic-update-slice_fusion.85), channel_id=1, source_target_pairs={{0,1},{1,2},{2,3},{3,4},{4,5},{5,6},{6,7},{7,8},{8,9},{9,10},{10,1... | collective-permute-start | bytes 43016 | tf_op jit(solution)/shard_map/ppermute | solution.py:20
  82.4 41.5 %copy-start.8 = (bf16[8,2,1024]{2,1,0:T(2,128)(2,1)}, bf16[8,2,1024]{2,1,0:T(2,128)(2,1)S(1)}, u32[]{:S(2)}) copy-start(bf16[8,2,1024]{2,1,0:T(2,128)(2,1)S(1)} %slice.654) | copy-start | bytes 98308
  82.4 14.0 %collective-permute-start.21 = (bf16[7,1,1024]{2,1,0:T(2,128)(2,1)S(1)}, bf16[7,1,1024]{2,1,0:T(2,128)(2,1)S(1)}, u32[]{:S(2)}, u32[]{:S(2)}) collective-permute-start(bf16[7,1,1024]{2,1,0:T(2,128)(2,1)S(1)} %constant_dynamic-update-slice_fusion.85), channel_id=1, source_target_pairs={{1,0},{2,1},{3,2},{4,3},{5,4},{6,5},{7,6},{8,7},{9,8},{10,9},{11,1... | collective-permute-start | bytes 43016 | tf_op jit(solution)/shard_map/ppermute | solution.py:20
  87.4 10.9 %collective-permute-start.22 = (bf16[7,1,1024]{2,1,0:T(2,128)(2,1)S(1)}, bf16[7,1,1024]{2,1,0:T(2,128)(2,1)S(1)}, u32[]{:S(2)}, u32[]{:S(2)}) collective-permute-start(bf16[7,1,1024]{2,1,0:T(2,128)(2,1)S(1)} %constant_dynamic-update-slice_fusion.85), channel_id=1, source_target_pairs={{2,0},{3,1},{4,2},{5,3},{6,4},{7,5},{8,6},{9,7},{10,8},{11,9},{12,... | collective-permute-start | bytes 43016 | tf_op jit(solution)/shard_map/ppermute | solution.py:20
  89.7 11.0 %collective-permute-start.23 = (bf16[7,1,1024]{2,1,0:T(2,128)(2,1)S(1)}, bf16[7,1,1024]{2,1,0:T(2,128)(2,1)S(1)}, u32[]{:S(2)}, u32[]{:S(2)}) collective-permute-start(bf16[7,1,1024]{2,1,0:T(2,128)(2,1)S(1)} %constant_dynamic-update-slice_fusion.85), channel_id=1, source_target_pairs={{3,0},{4,1},{5,2},{6,3},{7,4},{8,5},{9,6},{10,7},{11,8},{12,9},{13... | collective-permute-start | bytes 43016 | tf_op jit(solution)/shard_map/ppermute | solution.py:20
  91.7 18.5 %collective-permute-start = (bf16[4,4,1024]{2,1,0:T(4,128)(2,1)S(1)}, bf16[4,4,1024]{2,1,0:T(4,128)(2,1)S(1)}, u32[]{:S(2)}, u32[]{:S(2)}) collective-permute-start(bf16[4,4,1024]{2,1,0:T(4,128)(2,1)S(1)} %reshape.3272), channel_id=1, source_target_pairs={{0,32},{32,64},{64,96},{96,128},{128,160},{160,192},{192,224},{224... | collective-permute-start | bytes 98312 | tf_op jit(solution)/shard_map/ppermute | solution.py:20
  96.4 15.8 %collective-permute-start.1 = (bf16[4,4,1024]{2,1,0:T(4,128)(2,1)S(1)}, bf16[4,4,1024]{2,1,0:T(4,128)(2,1)S(1)}, u32[]{:S(2)}, u32[]{:S(2)}) collective-permute-start(bf16[4,4,1024]{2,1,0:T(4,128)(2,1)S(1)} %reshape.3272), channel_id=1, source_target_pairs={{32,0},{64,32},{96,64},{128,96},{160,128},{192,160},{224,192},{256... | collective-permute-start | bytes 98312 | tf_op jit(solution)/shard_map/ppermute | solution.py:20
  98.3 30.1 %collective-permute-start.10 = (bf16[8,2,1024]{2,1,0:T(2,128)(2,1)S(1)}, bf16[8,2,1024]{2,1,0:T(2,128)(2,1)}, u32[]{:S(2)}, u32[]{:S(2)}) collective-permute-start(bf16[8,2,1024]{2,1,0:T(2,128)(2,1)S(1)} %slice.654), channel_id=1, source_target_pairs={{1,0},{2,1},{3,2},{4,3},{5,4},{6,5},{7,6},{8,7},{9,8},{10,9},{11,1... | collective-permute-start | bytes 98312 | tf_op jit(solution)/shard_map/ppermute | solution.py:20
  100.7 33.7 %collective-permute-start.11 = (bf16[8,2,1024]{2,1,0:T(2,128)(2,1)S(1)}, bf16[8,2,1024]{2,1,0:T(2,128)(2,1)}, u32[]{:S(2)}, u32[]{:S(2)}) collective-permute-start(bf16[8,2,1024]{2,1,0:T(2,128)(2,1)S(1)} %slice.654), channel_id=1, source_target_pairs={{2,0},{3,1},{4,2},{5,3},{6,4},{7,5},{8,6},{9,7},{10,8},{11,9},{12,... | collective-permute-start | bytes 98312 | tf_op jit(solution)/shard_map/ppermute | solution.py:20
  106.7 27.7 %collective-permute-start.8 = (bf16[8,2,1024]{2,1,0:T(2,128)(2,1)S(1)}, bf16[8,2,1024]{2,1,0:T(2,128)(2,1)}, u32[]{:S(2)}, u32[]{:S(2)}) collective-permute-start(bf16[8,2,1024]{2,1,0:T(2,128)(2,1)S(1)} %slice.654), channel_id=1, source_target_pairs={{0,2},{1,3},{2,4},{3,5},{4,6},{5,7},{6,8},{7,9},{8,10},{9,11},{10,... | collective-permute-start | bytes 98312 | tf_op jit(solution)/shard_map/ppermute | solution.py:20
  110.2 7.8 %collective-permute-start.26 = (bf16[6,1,2048]{2,1,0:T(2,128)(2,1)S(1)}, bf16[6,1,2048]{2,1,0:T(2,128)(2,1)S(1)}, u32[]{:S(2)}, u32[]{:S(2)}) collective-permute-start(bf16[6,1,2048]{2,1,0:T(2,128)(2,1)S(1)} %get-tuple-element.8), channel_id=1, source_target_pairs={{0,1},{1,2},{2,3},{3,4},{4,5},{5,6},{6,7},{7,8},{8,9},{9,10},{10,1... | collective-permute-start | bytes 73736 | tf_op jit(solution)/shard_map/ppermute | solution.py:28
  112.1 7.8 %collective-permute-start.27 = (bf16[6,1,2048]{2,1,0:T(2,128)(2,1)S(1)}, bf16[6,1,2048]{2,1,0:T(2,128)(2,1)S(1)}, u32[]{:S(2)}, u32[]{:S(2)}) collective-permute-start(bf16[6,1,2048]{2,1,0:T(2,128)(2,1)S(1)} %get-tuple-element.9), channel_id=1, source_target_pairs={{1,0},{2,1},{3,2},{4,3},{5,4},{6,5},{7,6},{8,7},{9,8},{10,9},{11,1... | collective-permute-start | bytes 73736 | tf_op jit(solution)/shard_map/ppermute | solution.py:31
  118.0 16.4 %collective-permute-start.9 = (bf16[8,2,1024]{2,1,0:T(2,128)(2,1)S(1)}, bf16[8,2,1024]{2,1,0:T(2,128)(2,1)S(1)}, u32[]{:S(2)}, u32[]{:S(2)}) collective-permute-start(bf16[8,2,1024]{2,1,0:T(2,128)(2,1)S(1)} %slice.654), channel_id=1, source_target_pairs={{0,1},{1,2},{2,3},{3,4},{4,5},{5,6},{6,7},{7,8},{8,9},{9,10},{10,1... | collective-permute-start | bytes 98312 | tf_op jit(solution)/shard_map/ppermute | solution.py:20
  119.9 21.3 %collective-permute-start.2 = (bf16[10,4,1024]{2,1,0:T(4,128)(2,1)S(1)}, bf16[10,4,1024]{2,1,0:T(4,128)(2,1)}, u32[]{:S(2)}, u32[]{:S(2)}) collective-permute-start(bf16[10,4,1024]{2,1,0:T(4,128)(2,1)S(1)} %pad_maximum_fusion.3), channel_id=1, source_target_pairs={{0,1},{1,2},{2,3},{3,4},{4,5},{5,6},{6,7},{7,8},{8,9},{9,10},{10,1... | collective-permute-start | bytes 245768 | tf_op jit(solution)/shard_map/ppermute | solution.py:20
  126.4 8.0 %copy-start.9 = (bf16[8,2,1024]{2,1,0:T(2,128)(2,1)S(1)}, bf16[8,2,1024]{2,1,0:T(2,128)(2,1)}, u32[]{:S(2)}) copy-start(bf16[8,2,1024]{2,1,0:T(2,128)(2,1)} %copy-done.8) | copy-start | bytes 98308
  128.5 12.7 %collective-permute-start.3 = (bf16[10,4,1024]{2,1,0:T(4,128)(2,1)S(1)}, bf16[10,4,1024]{2,1,0:T(4,128)(2,1)S(1)}, u32[]{:S(2)}, u32[]{:S(2)}) collective-permute-start(bf16[10,4,1024]{2,1,0:T(4,128)(2,1)S(1)} %pad_maximum_fusion.3), channel_id=1, source_target_pairs={{1,0},{2,1},{3,2},{4,3},{5,4},{6,5},{7,6},{8,7},{9,8},{10,9},{11,1... | collective-permute-start | bytes 245768 | tf_op jit(solution)/shard_map/ppermute | solution.py:20
  137.0 3.6 %copy-start.7 = (bf16[1,4,32,32]{3,2,1,0:T(8,128)(2,1)S(1)}, bf16[1,4,32,32]{3,2,1,0:T(8,128)(2,1)}, u32[]{:S(2)}) copy-start(bf16[1,4,32,32]{3,2,1,0:T(8,128)(2,1)} %copy-done.6) | copy-start | bytes 24580
  137.0 3.6 %copy-start.10 = (bf16[32,32,1,1]{1,0,3,2:T(8,128)(2,1)S(1)}, bf16[32,32,1,1]{1,0,3,2:T(8,128)(2,1)}, u32[]{:S(2)}) copy-start(bf16[32,32,1,1]{1,0,3,2:T(8,128)(2,1)} %fusion.25) | copy-start | bytes 6148
  140.6 2.5 %copy-start.48 = (bf16[4,4]{1,0:T(4,128)(2,1)S(1)}, bf16[4,4]{1,0:T(4,128)(2,1)}, u32[]{:S(2)}) copy-start(bf16[4,4]{1,0:T(4,128)(2,1)} %get-tuple-element.28) | copy-start | bytes 100
  140.6 2.6 %copy-start.47 = (bf16[4,4]{1,0:T(4,128)(2,1)S(1)}, bf16[4,4]{1,0:T(4,128)(2,1)}, u32[]{:S(2)}) copy-start(bf16[4,4]{1,0:T(4,128)(2,1)} %get-tuple-element.26) | copy-start | bytes 100
  140.6 2.7 %copy-start.46 = (bf16[4,4]{1,0:T(4,128)(2,1)S(1)}, bf16[4,4]{1,0:T(4,128)(2,1)}, u32[]{:S(2)}) copy-start(bf16[4,4]{1,0:T(4,128)(2,1)} %get-tuple-element.34) | copy-start | bytes 100
  140.6 2.9 %copy-start.45 = (bf16[4,4]{1,0:T(4,128)(2,1)S(1)}, bf16[4,4]{1,0:T(4,128)(2,1)}, u32[]{:S(2)}) copy-start(bf16[4,4]{1,0:T(4,128)(2,1)} %get-tuple-element.30) | copy-start | bytes 100
  140.6 3.0 %copy-start.44 = (bf16[4,4]{1,0:T(4,128)(2,1)S(1)}, bf16[4,4]{1,0:T(4,128)(2,1)}, u32[]{:S(2)}) copy-start(bf16[4,4]{1,0:T(4,128)(2,1)} %get-tuple-element.27) | copy-start | bytes 100
  140.6 3.1 %copy-start.43 = (bf16[4,4]{1,0:T(4,128)(2,1)S(1)}, bf16[4,4]{1,0:T(4,128)(2,1)}, u32[]{:S(2)}) copy-start(bf16[4,4]{1,0:T(4,128)(2,1)} %get-tuple-element.29) | copy-start | bytes 100
  140.6 3.2 %copy-start.42 = (bf16[4,4]{1,0:T(4,128)(2,1)S(1)}, bf16[4,4]{1,0:T(4,128)(2,1)}, u32[]{:S(2)}) copy-start(bf16[4,4]{1,0:T(4,128)(2,1)} %get-tuple-element.40) | copy-start | bytes 100
  140.7 3.3 %copy-start.41 = (bf16[4,4]{1,0:T(4,128)(2,1)S(1)}, bf16[4,4]{1,0:T(4,128)(2,1)}, u32[]{:S(2)}) copy-start(bf16[4,4]{1,0:T(4,128)(2,1)} %get-tuple-element.16) | copy-start | bytes 100
  141.0 3.1 %copy-start.40 = (bf16[4,4]{1,0:T(4,128)(2,1)S(1)}, bf16[4,4]{1,0:T(4,128)(2,1)}, u32[]{:S(2)}) copy-start(bf16[4,4]{1,0:T(4,128)(2,1)} %get-tuple-element.24) | copy-start | bytes 100
  141.0 3.3 %copy-start.39 = (bf16[4,4]{1,0:T(4,128)(2,1)S(1)}, bf16[4,4]{1,0:T(4,128)(2,1)}, u32[]{:S(2)}) copy-start(bf16[4,4]{1,0:T(4,128)(2,1)} %get-tuple-element.36) | copy-start | bytes 100
  141.1 3.2 %copy-start.38 = (bf16[4,4]{1,0:T(4,128)(2,1)S(1)}, bf16[4,4]{1,0:T(4,128)(2,1)}, u32[]{:S(2)}) copy-start(bf16[4,4]{1,0:T(4,128)(2,1)} %get-tuple-element.32) | copy-start | bytes 100
  141.2 3.4 %copy-start.37 = (bf16[4,4]{1,0:T(4,128)(2,1)S(1)}, bf16[4,4]{1,0:T(4,128)(2,1)}, u32[]{:S(2)}) copy-start(bf16[4,4]{1,0:T(4,128)(2,1)} %get-tuple-element.18) | copy-start | bytes 100
  142.3 2.6 %copy-start.34 = (bf16[4,4]{1,0:T(4,128)(2,1)S(1)}, bf16[4,4]{1,0:T(4,128)(2,1)}, u32[]{:S(2)}) copy-start(bf16[4,4]{1,0:T(4,128)(2,1)} %get-tuple-element.52) | copy-start | bytes 100
  (31 other events, 67.4 us)
where the time goes:
time: 154 us; the launch traced here: 152 us
  starting transfers between devices  93.3 us (61%)
  waiting for transfers between devices  21.4 us (14%)
  matrix products  13.9 us (9%)
  other arithmetic  10.9 us (7%)
  local copies, waits for them, and re-layouts  10.1 us (7%)
  between operations  2.66 us (2%)
    ppermute x24, starting transfers between devices, shifted(): return lax.ppermute(block, axis, route)  79.8 us
    ppermute x24, waiting for transfers between devices, shifted(): return lax.ppermute(block, axis, route)  21.4 us
    unnamed x117, other arithmetic  7.95 us
    ppermute x2, starting transfers between devices, with_halo(): lax.ppermute(lax.slice_in_dim(block, 0, width, axis=dim), axis, backward)  7.91 us
    dot_general x9, matrix products, local(): jnp.einsum('abpq,abqv->abpv', near_blocks[:, :, position], window, prefer...  6.97 us
    ppermute x2, starting transfers between devices, with_halo(): lax.ppermute(lax.slice_in_dim(block, block.shape[dim] - width, None, axis...  5.58 us
  transfers between devices with their start and end apart: 28, of which 5 were waited for; matrix products, arithmetic and copies ran while one was open for 14% of the time, Pallas kernels for 0%

commit v1 on v0

v1 whole, which is shorter than its diff:
```python
import jax
import jax.numpy as jnp
from jax import lax
from jax.experimental import pallas as pl
from jax.experimental.pallas import tpu as pltpu
from jax.sharding import PartitionSpec as P

BF = jnp.bfloat16
F32 = jnp.float32
AXES = ("gx", "gy")
VMEM_BYTES = 48 * 1024 * 1024

OWN_ROW, OWN_COL, OWN_E0, OWN_E1, OWN_E2, OWN_ROWS = 0, 64, 128, 256, 288, 320
FAR_X, FAR_E0, FAR_CORNER, FAR_E1, FAR_E1_SIDE, FAR_E2, FAR_ROWS = 0, 64, 128, 192, 224, 256, 288


def dot(a, b):
    return lax.dot_general(a, b, (((1,), (0,)), ((), ())), preferred_element_type=F32)


def dot_nt(a, b):
    return lax.dot_general(a, b, (((1,), (1,)), ((), ())), preferred_element_type=F32)


def roll(x, lanes):
    lanes = lanes % x.shape[1]
    if lanes == 0:
        return x
    if x.dtype == BF:
        return pltpu.roll(x.astype(F32), lanes, 1).astype(BF)
    return pltpu.roll(x, lanes, 1)


def lane_of(rows, lanes=128):
    return lax.broadcasted_iota(jnp.int32, (rows, lanes), 1)


def slot_of(rows, lanes=128):
    return lane_of(rows, lanes) // 32


def eye(n):
    row = lax.broadcasted_iota(jnp.int32, (n, n), 0)
    return jnp.where(row == lane_of(n, n), 1.0, 0.0).astype(BF)


def place():
    gx, gy = lax.axis_index("gx"), lax.axis_index("gy")
    return gx, gy, lax.rem(gx, 2), lax.rem(gy, 2)


def merge_diagonal(blocks, height):
    slot = slot_of(height)
    out = jnp.zeros((height, 128), F32)
    for b in range(4):
        out = jnp.where(slot == b, blocks[b * height : (b + 1) * height], out)
    return out


def upward_kernel(samples, order, basis, transfer, x_out, msg):
    _, _, pi, pj = place()
    slot = slot_of(64)
    spread = jnp.concatenate([samples[...]] * 4, axis=0)
    lane = lane_of(128)
    xs, e0s = [], []
    for a in range(4):
        picked = []
        for half in range(2):
            g = 2 * a + half
            line = order[g : g + 1, :].astype(F32)
            column = jnp.transpose(jnp.broadcast_to(line, (128, 128))).astype(jnp.int32)
            pick = jnp.concatenate(
                [jnp.where(column == lane + 128 * t, 1.0, 0.0).astype(BF) for t in range(8)],
                axis=1,
            )
            picked.append(dot_nt(pick, spread))
        x = merge_diagonal(jnp.concatenate(picked, axis=0), 64).astype(BF)
        x_out[a * 64 : (a + 1) * 64, :] = x
        e0 = merge_diagonal(dot(basis[a * 128 : (a + 1) * 128, :], x), 32).astype(BF)
        msg[OWN_E0 + a * 32 : OWN_E0 + (a + 1) * 32, :] = e0
        xs.append(x)
        e0s.append(e0)
    msg[OWN_ROW : OWN_ROW + 64, :] = jnp.where(pi == 0, xs[3], xs[0])
    column_slot = jnp.where(pj == 0, 3, 0)
    packed = jnp.zeros((64, 128), BF)
    for a in range(4):
        packed = jnp.where(slot == lax.rem(column_slot + a, 4), roll(xs[a], 32 * a), packed)
    msg[OWN_COL : OWN_COL + 64, :] = packed

    one = eye(32)
    slot = slot_of(32)
    turned = [dot_nt(one, transfer[n * 32 : (n + 1) * 32, :]).astype(BF) for n in range(8)]
    e1 = jnp.zeros((32, 128), F32)
    for x in range(2):
        parts = []
        for j in range(2):
            parts.append(dot(turned[j], e0s[2 * x]) + dot(turned[2 + j], e0s[2 * x + 1]))
        joined = parts[0] + roll(parts[1], -32)
        e1 = jnp.where(slot == 2 * x, roll(joined, 64 * x), e1)
        e1 = jnp.where(slot == 2 * x + 1, roll(joined, 64 * x - 32), e1)
    e1 = e1.astype(BF)
    msg[OWN_E1 : OWN_E1 + 32, :] = e1
    e2 = merge_diagonal(dot(jnp.concatenate(turned[4:], axis=0), e1), 32)
    e2 = e2 + roll(e2, 64)
    e2 = e2 + roll(e2, 32)
    msg[OWN_E2 : OWN_E2 + 32, :] = jnp.where(slot == 2 * pi + pj, e2, 0.0).astype(BF)


def cross_kernel(group, x, send):
    _, _, pi, pj = place()
    me, across_x, across_y = 2 * pi + pj, 2 * (1 - pi) + pj, 2 * pi + 1 - pj
    lane, slot = lane_of(64), slot_of(64)
    near_half = (lane < 64) == (pj == 0)
    e0 = group[me, OWN_E0 : OWN_E0 + 128, :]
    e0_rows = jnp.where(pi == 0, e0[:64], e0[64:])
    x_row = jnp.where(pi == 0, x[0:64, :], x[192:256, :])
    e1 = group[me, OWN_E1 : OWN_E1 + 32, :]
    e2 = group[0, OWN_E2 : OWN_ROWS, :]
    for m in range(1, 4):
        e2 = e2 + group[m, OWN_E2 : OWN_ROWS, :]
    for m in range(4):
        send[m, FAR_E2 : FAR_E2 + 32, :] = e2
        send[m, FAR_E1 : FAR_E1 + 32, :] = e1

    to = 2 * pi + 1 - pj
    send[to, FAR_X : FAR_X + 64, :] = x_row
    send[to, FAR_E0 : FAR_E0 + 64, :] = e0_rows
    column = group[across_y, OWN_COL : OWN_COL + 64, :]
    column = jnp.where(pi == 0, roll(column, 64), roll(column, -32))
    corner_e0 = group[across_y, pl.ds(OWN_E0 + 64 * pi, 64), :]
    send[to, FAR_CORNER : FAR_CORNER + 64, :] = jnp.where(near_half, corner_e0, column)
    send[to, FAR_E1_SIDE : FAR_E1_SIDE + 32, :] = group[across_y, OWN_E1 : OWN_E1 + 32, :]

    to = 2 * (1 - pi) + pj
    column_slot = jnp.where(pj == 0, 0, 3)
    packed = jnp.zeros((64, 128), BF)
    for a in range(4):
        moved = roll(x[a * 64 : (a + 1) * 64, :], 32 * a)
        packed = jnp.where(slot == lax.rem(column_slot + a, 4), moved, packed)
    send[to, FAR_X : FAR_X + 64, :] = packed
    send[to, FAR_E0 : FAR_E0 + 64, :] = jnp.where(near_half, e0[:64], roll(e0[64:], 64))
    corner_x = roll(group[across_x, OWN_ROW : OWN_ROW + 64, :], 64)
    corner_e0 = group[across_x, pl.ds(OWN_E0 + 64 * pi, 64), :]
    send[to, FAR_CORNER : FAR_CORNER + 64, :] = jnp.where(near_half, corner_e0, corner_x)
    send[to, FAR_E1_SIDE : FAR_E1_SIDE + 32, :] = group[across_x, OWN_E1 : OWN_E1 + 32, :]

    to = 2 * pi + pj
    send[to, FAR_X : FAR_X + 64, :] = jnp.zeros((64, 128), BF)
    send[to, FAR_E0 : FAR_E0 + 64, :] = jnp.zeros((64, 128), BF)
    send[to, FAR_CORNER : FAR_CORNER + 64, :] = jnp.where(near_half, e0_rows, roll(x_row, 64))
    send[to, FAR_E1_SIDE : FAR_E1_SIDE + 32, :] = jnp.zeros((32, 128), BF)

    to = 2 * (1 - pi) + 1 - pj
    send[to, 0:FAR_E1, :] = jnp.zeros((FAR_E1, 128), BF)
    send[to, FAR_E1_SIDE : FAR_E1_SIDE + 32, :] = jnp.zeros((32, 128), BF)


def store_row_of_tiles(halo, start, left, middle, right):
    lane = lane_of(32)
    low = lane < 64
    nothing = jnp.zeros((32, 128), BF)
    first = jnp.where(low, middle, roll(right, 64))
    second = jnp.where(low, roll(middle, 64), right)
    halo[pl.ds(start, 32), 0:128] = first
    halo[pl.ds(start, 32), 128:256] = jnp.where(low, nothing, roll(left, 64))
    halo[pl.ds(start + 32, 32), 0:128] = second
    halo[pl.ds(start + 32, 32), 128:256] = jnp.where(low, nothing, left)


def far_row(matrix, window, parity):
    lane = lane_of(224, 224)
    admitted = (lane >= 32 * (1 - parity)) & (lane < 224 - 32 * parity)
    product = dot(jnp.where(admitted, matrix, jnp.zeros((224, 224), BF)), window)
    odd = lax.rem(slot_of(32), 2) == 1
    out = jnp.zeros((32, 128), F32)
    for w in range(-3, 4):
        part = product[(w + 3) * 32 : (w + 4) * 32]
        part = part[:, :128] if w == 0 else pltpu.roll(part, (-32 * w) % 256, 1)[:, :128]
        if w == -3:
            part = jnp.where(odd, part, 0.0)
        if w == 3:
            part = jnp.where(odd, 0.0, part)
        out = out + part
    return out


def downward_kernel(count_x, count_y):
    def body(group, x, cross, shared, near, basis, transfer, coupling, order, out, far, h0, h1, h2):
        gx, gy, pi, pj = place()
        me, across_x, across_y = 2 * pi + pj, 2 * (1 - pi) + pj, 2 * pi + 1 - pj
        across = 2 * (1 - pi) + 1 - pj
        from_x, from_y, from_xy = 2 * pi + 1 - pj, 2 * (1 - pi) + pj, 2 * pi + pj
        has_x = jnp.where(pi == 0, gx > 0, gx < count_x - 1)
        has_y = jnp.where(pj == 0, gy > 0, gy < count_y - 1)
        has_xy = has_x & has_y

        def kept(keep, value):
            return jnp.where(keep, value, jnp.zeros_like(value))

        far[...] = jnp.zeros(far.shape, BF)
        for level in range(3):
            n = 0
            for u in range(-3, 4):
                for w in range(-3, 4):
                    if max(abs(u), abs(w)) >= 2:
                        start = (level * 40 + n) * 32
                        far[level, (w + 3) * 32 : (w + 4) * 32, (u + 3) * 32 : (u + 4) * 32] = (
                            coupling[start : start + 32, :]
                        )
                        n += 1

        lane = lane_of(64)
        near_half = (lane < 64) == (pj == 0)
        h0[0:32, :] = jnp.zeros((32, 256), BF)
        h0[288:320, :] = jnp.zeros((32, 256), BF)
        h0[96:224, 0:128] = group[me, OWN_E0 : OWN_E0 + 128, :]
        strip = kept(has_y, cross[from_y, FAR_E0 : FAR_E0 + 64, :])
        beside = group[across_y, OWN_E0 : OWN_E0 + 128, :]
        h0[96:160, 128:256] = jnp.where(near_half, beside[:64], strip)
        h0[160:224, 128:256] = jnp.where(near_half, beside[64:], roll(strip, 64))
        start = 32 + 192 * (1 - pi)
        h0[pl.ds(start, 64), 0:128] = group[across_x, pl.ds(OWN_E0 + 64 * pi, 64), :]
        h0[pl.ds(start, 64), 128:256] = jnp.where(
            near_half,
            group[across, pl.ds(OWN_E0 + 64 * pi, 64), :],
            kept(has_y, cross[from_y, FAR_CORNER : FAR_CORNER + 64, :]),
        )
        start = 32 + 192 * pi
        h0[pl.ds(start, 64), 0:128] = kept(has_x, cross[from_x, FAR_E0 : FAR_E0 + 64, :])
        h0[pl.ds(start, 64), 128:256] = jnp.where(
            near_half,
            kept(has_x, cross[from_x, FAR_CORNER : FAR_CORNER + 64, :]),
            kept(has_xy, cross[from_xy, FAR_CORNER : FAR_CORNER + 64, :]),
        )

        def store_sides(start, middle, inner, outer):
            left = jnp.where(pj == 0, outer, inner)
            right = jnp.where(pj == 0, inner, outer)
            store_row_of_tiles(h1, start, left, middle, right)

        for halo in (h1, h2):
            halo[0:32, :] = jnp.zeros((32, 256), BF)
            halo[224:256, :] = jnp.zeros((32, 256), BF)
        own_e1 = slice(OWN_E1, OWN_E1 + 32)
        far_e1, side_e1 = slice(FAR_E1, FAR_E1 + 32), slice(FAR_E1_SIDE, FAR_E1_SIDE + 32)
        store_sides(
            96, group[me, own_e1, :], group[across_y, own_e1, :], kept(has_y, cross[from_y, far_e1, :])
        )
        store_sides(
            32 + 128 * (1 - pi),
            group[across_x, own_e1, :],
            group[across, own_e1, :],
            kept(has_y, cross[from_y, side_e1, :]),
        )
        store_sides(
            32 + 128 * pi,
            kept(has_x, cross[from_x, far_e1, :]),
            kept(has_x, cross[from_x, side_e1, :]),
            kept(has_xy, cross[from_xy, far_e1, :]),
        )

        above, below = gx >= 2, gx < count_x - 2
        before, after = gy >= 2, gy < count_y - 2
        e2 = group[0, OWN_E2:OWN_ROWS, :]
        for m in range(1, 4):
            e2 = e2 + group[m, OWN_E2:OWN_ROWS, :]
        store_row_of_tiles(
            h2,
            32,
            kept(above & before, shared[0, 0]),
            kept(above, shared[0, 1]),
            kept(above & after, shared[1, 1]),
        )
        store_row_of_tiles(h2, 96, kept(before, shared[0, 2]), e2, kept(after, shared[1, 3]))
        store_row_of_tiles(
            h2,
            160,
            kept(below & before, shared[2, 2]),
            kept(below, shared[2, 3]),
            kept(below & after, shared[3, 3]),
        )

        slot = slot_of(32)
        local2 = far_row(far[2], h2[pl.ds(32 * pi, 224), :], pi)
        local2 = jnp.where(slot == pj, local2, 0.0)
        local2 = local2 + roll(local2, 64)
        local2 = (local2 + roll(local2, 32)).astype(BF)
        spread = dot(transfer[128:256, :], local2)
        local1 = []
        for i in range(2):
            down = far_row(far[1], h1[32 * i : 32 * i + 224, :], i)
            for j in range(2):
                n = 2 * i + j
                down = down + jnp.where(slot == j, spread[n * 32 : (n + 1) * 32], 0.0)
            down = jnp.where(slot < 2, down, 0.0)
            wide = jnp.where(slot == 0, down, 0.0) + jnp.where(slot == 2, roll(down, 32), 0.0)
            local1.append((wide + roll(wide, 32)).astype(BF))
        local0 = []
        for i in range(4):
            spread = dot(transfer[64 * (i % 2) : 64 * (i % 2) + 64, :], local1[i // 2])
            down = far_row(far[0], h0[32 * i : 32 * i + 224, :], i % 2)
            down = down + jnp.where(lax.rem(slot, 2) == 0, spread[:32], spread[32:])
            local0.append(down.astype(BF))

        slot = slot_of(64)
        column = kept(has_y, cross[from_y, FAR_X : FAR_X + 64, :])
        beside = group[across_y, OWN_COL : OWN_COL + 64, :]
        windows = {}

        def store_windows(a, middle, inner, outer):
            left = jnp.where(pj == 0, outer, inner)
            right = jnp.where(pj == 0, inner, outer)
            windows[a, 0] = middle
            windows[a, -1] = roll(jnp.where(slot == 3, left, middle), 32)
            windows[a, 1] = roll(jnp.where(slot == 0, right, middle), -32)

        for a in range(4):
            store_windows(
                a, x[a * 64 : (a + 1) * 64, :], roll(beside, -32 * a), roll(column, -32 * a)
            )
        inside = (
            group[across_x, OWN_ROW : OWN_ROW + 64, :],
            group[across, OWN_ROW : OWN_ROW + 64, :],
            kept(has_y, roll(cross[from_y, FAR_CORNER : FAR_CORNER + 64, :], 64)),
        )
        outside = (
            kept(has_x, cross[from_x, FAR_X : FAR_X + 64, :]),
            kept(has_x, roll(cross[from_x, FAR_CORNER : FAR_CORNER + 64, :], 64)),
            kept(has_xy, roll(cross[from_xy, FAR_CORNER : FAR_CORNER + 64, :], 64)),
        )
        store_windows(-1, *[jnp.where(pi == 0, o, i) for o, i in zip(outside, inside)])
        store_windows(4, *[jnp.where(pi == 0, i, o) for o, i in zip(outside, inside)])

        row = lax.broadcasted_iota(jnp.int32, (256, 128), 0)
        diagonal = row // 64 == slot_of(256)
        block = lax.broadcasted_iota(jnp.int32, (128, 128), 0) // 32 == slot_of(128)
        leaves = []
        for a in range(4):
            total = jnp.zeros((256, 128), F32)
            for n in range(9):
                r, c = n // 3 - 1, n % 3 - 1
                matrix = near[a, :, n].reshape(256, 64)
                total = total + dot(matrix, windows[a + r, c])
            leaf = jnp.transpose(basis[a * 128 : (a + 1) * 128, :].astype(F32)).astype(BF)
            local = jnp.concatenate([local0[a]] * 4, axis=0)
            lift = dot(leaf, jnp.where(block, local, jnp.zeros_like(local)))
            total = total + jnp.concatenate([lift] * 4, axis=0)
            leaves.append(jnp.where(diagonal, total, 0.0).astype(BF))
        leaves = jnp.concatenate(leaves, axis=0)
        line = jnp.concatenate([order[g : g + 1, :] for g in range(8)], axis=1)
        for t in range(8):
            site = lax.broadcasted_iota(jnp.int32, (128, 1024), 0) + 128 * t
            pick = jnp.where(site == line, 1.0, 0.0).astype(BF)
            done = jnp.transpose(dot(pick, leaves))
            done = (done[:32] + done[32:64]) + (done[64:96] + done[96:])
            out[:, 128 * t : 128 * (t + 1)] = done.astype(BF)

    return body


def call(kernel, shapes, scratch=()):
    return pl.pallas_call(
        kernel,
        out_shape=shapes,
        scratch_shapes=list(scratch),
        compiler_params=pltpu.CompilerParams(vmem_limit_bytes=VMEM_BYTES),
    )


def groups_of_four(count_x, count_y, offset):
    return [
        [
            ((i + di) % count_x) * count_y + (j + dj) % count_y
            for di in range(2)
            for dj in range(2)
        ]
        for i in range(offset, count_x + offset, 2)
        for j in range(offset, count_y + offset, 2)
    ]


def solution(mesh):
    count_x, count_y = mesh.shape["gx"], mesh.shape["gy"]
    aligned = groups_of_four(count_x, count_y, 0)
    shifted = groups_of_four(count_x, count_y, 1)

    def local(samples, site_order, leaf_basis, near_blocks, transfer, coupling):
        samples = samples.T
        order = site_order.reshape(8, 128)
        basis = leaf_basis.transpose(0, 1, 3, 2).reshape(512, 64)
        transfer = transfer.reshape(256, 32)
        coupling = coupling.reshape(3840, 32)
        x, message = call(
            upward_kernel,
            (jax.ShapeDtypeStruct((256, 128), BF), jax.ShapeDtypeStruct((OWN_ROWS, 128), BF)),
        )(samples, order, basis, transfer)
        group = lax.all_gather(message, AXES, axis_index_groups=aligned)
        send = call(cross_kernel, jax.ShapeDtypeStruct((4, FAR_ROWS, 128), BF))(group, x)
        cross = lax.all_to_all(send, AXES, 0, 0, axis_index_groups=shifted)
        shared = lax.all_gather(cross[:, FAR_E2 : FAR_E2 + 32], AXES, axis_index_groups=aligned)
        out = call(
            downward_kernel(count_x, count_y),
            jax.ShapeDtypeStruct((32, 1024), BF),
            (
                pltpu.VMEM((3, 224, 224), BF),
                pltpu.VMEM((320, 256), BF),
                pltpu.VMEM((256, 256), BF),
                pltpu.VMEM((256, 256), BF),
            ),
        )(group, x, cross, shared, near_blocks, basis, transfer, coupling, order)
        return out.T

    return jax.shard_map(
        local,
        mesh=mesh,
        in_specs=(
            P(("gx", "gy"), None),
            P(("gx", "gy")),
            P("gx", "gy", None, None),
            P("gx", "gy", None, None, None),
            P(),
            P(),
        ),
        out_specs=P(("gx", "gy"), None),
        check_vma=False,
    )
```

time: 154 us -> 45.8 us (0.30)
  the two profiles are of different devices: /device:TPU:38 before, /device:TPU:1 now
where the time goes in v1:
time: 45.8 us; the launch traced here: 45.4 us
  blocking collectives  22.1 us (48%)
  starting transfers between devices  7.26 us (16%)
  Pallas kernels  6.31 us (14%)
  local copies, waits for them, and re-layouts  5.89 us (13%)
  waiting for transfers between devices  3.85 us (8%)
    all_gather x1, blocking collectives, local(): group = lax.all_gather(message, AXES, axis_index_groups=aligned)  12.7 us
    all_gather x1, blocking collectives, local(): lax.all_gather(cross[:, FAR_E2:FAR_E2 + 32], AXES, axis_index_groups=alig...  9.38 us
    all_to_all x1, starting transfers between devices, local(): cross = lax.all_to_all(send, AXES, 0, 0, axis_index_groups=shifted)  7.26 us
    unnamed x19, local copies, waits for them, and re-layouts  5.89 us
    all_to_all x1, waiting for transfers between devices, local(): cross = lax.all_to_all(send, AXES, 0, 0, axis_index_groups=shifted)  3.85 us
    pallas_call x1, Pallas kernels, local(): call(downward_kernel(count_x, count_y), jax.ShapeDtypeStruct((32, 1024),...  3.53 us
    pallas_call x1, Pallas kernels, local(): call(upward_kernel, (jax.ShapeDtypeStruct((256, 128), BF), jax.ShapeDtype...  1.95 us
  transfers between devices with their start and end apart: 1, of which 1 were waited for; matrix products, arithmetic and copies ran while one was open for 2% of the time, Pallas kernels for 0%

profile of v1, /device:TPU:1, one launch (start us, length us, event | category | flops | bytes accessed | tf_op | source)
XLA Modules:
  0.0 45.4 jit_solution(11111437406730100726)
XLA Ops:
  0.0 0.0 copy-start.7
  0.0 0.0 copy-start.1
  0.0 0.9 %copy-done.1 = bf16[4,4,64,32]{2,3,1,0:T(8,128)(2,1)S(1)} copy-done((bf16[4,4,64,32]{2,3,1,0:T(8,128)(2,1)S(1)}, bf16[4,4,64,32]{2,3,1,0:T(8,128)(2,1)}, u32[]{:S(2)}) %copy-start.1) | copy-done | bytes 65560
  0.9 0.0 copy-start.3
  0.9 0.8 %copy-done.3 = bf16[2,4,32,32]{3,2,1,0:T(8,128)(2,1)S(1)} copy-done((bf16[2,4,32,32]{3,2,1,0:T(8,128)(2,1)S(1)}, bf16[2,4,32,32]{3,2,1,0:T(8,128)(2,1)}, u32[]{:S(2)}) %copy-start.3) | copy-done | bytes 16408
  1.8 0.0 copy-start.5
  1.8 0.8 %copy-done.5 = bf16[1024,32]{0,1:T(8,128)(2,1)S(1)} copy-done((bf16[1024,32]{0,1:T(8,128)(2,1)S(1)}, bf16[1024,32]{0,1:T(8,128)(2,1)}, u32[]{:S(2)}) %copy-start.5) | copy-done | bytes 65560
  2.6 0.0 copy-start.6
  2.6 0.7 %copy-done.6 = s32[1024]{0:T(1024)S(1)} copy-done((s32[1024]{0:T(1024)S(1)}, s32[1024]{0:T(1024)}, u32[]{:S(2)}) %copy-start.6) | copy-done | bytes 4120
  3.3 0.0 copy-start.8
  3.3 0.0 copy-start.2
  3.3 0.0 copy-start.4
  3.3 2.0 %shard_map.64 = (bf16[256,128]{1,0:T(8,128)(2,1)S(1)}, bf16[320,128]{1,0:T(8,128)(2,1)S(1)}) custom-call(bf16[32,1024]{1,0:T(8,128)(2,1)S(1)} %bitcast.18, s32[8,128]{1,0:T(8,128)S(1)} %bitcast.19, bf16[512,64]{1,0:T(8,128)(2,1)S(1)} %bitcast.14, bf16[256,32]{1,0:T(8,128)(2,1)S(1)} %bitcast.16), custom_call_target="tpu_custom_call" | custom-call | tf_op jit(solution)/shard_map/pallas_call | solution.py:393
  5.2 12.7 %all-gather = bf16[1280,128]{1,0:T(8,128)(2,1)S(1)} all-gather(bf16[320,128]{1,0:T(8,128)(2,1)S(1)} %get-tuple-element.7), channel_id=2, replica_groups={{0,1,32,33},{2,3,34,35},{4,5,36,37},{6,7,38,39},{8,9,40,41},{10,11,42,4..., dimensions={0}, use_global_device_ids=true | all-gather | bytes 409600 | tf_op jit(solution)/shard_map/all_gather | solution.py:397
  17.9 0.8 %shard_map.65 = bf16[4,288,128]{2,1,0:T(8,128)(2,1)} custom-call(bf16[4,320,128]{2,1,0:T(8,128)(2,1)S(1)} %bitcast.11, bf16[256,128]{1,0:T(8,128)(2,1)S(1)} %get-tuple-element.8.x), custom_call_target="tpu_custom_call" | custom-call | tf_op jit(solution)/shard_map/pallas_call | solution.py:398
  18.7 7.3 %all-to-all-start = ((bf16[4,288,128]{2,1,0:T(8,128)(2,1)}), bf16[4,288,128]{2,1,0:T(8,128)(2,1)S(1)}, u32[]{:S(2)}, u32[]{:S(2)}) async-start(bf16[4,288,128]{2,1,0:T(8,128)(2,1)} %shard_map.65), calls=%async_computation | async-start | bytes 589824 | tf_op jit(solution)/shard_map/all_to_all | solution.py:399
  26.0 0.0 copy-done.8
  26.0 0.9 %copy.8 = bf16[3,40,32,32]{3,2,1,0:T(8,128)(2,1)S(1)} copy(bf16[3,40,32,32]{1,3,2,0:T(8,128)(2,1)S(1)} %copy-done.8) | data formatting | bytes 491520 | tf_op args[5]
  27.0 3.8 %all-to-all-done.cross = bf16[4,288,128]{2,1,0:T(8,128)(2,1)S(1)} async-done(((bf16[4,288,128]{2,1,0:T(8,128)(2,1)}), bf16[4,288,128]{2,1,0:T(8,128)(2,1)S(1)}, u32[]{:S(2)}, u32[]{:S(2)}) %all-to-all-start) | async-done | bytes 294944 | tf_op jit(solution)/shard_map/all_to_all | solution.py:399
  30.8 9.4 %all-gather.1 = bf16[16,32,128]{2,1,0:T(8,128)(2,1)S(1)} all-gather(bf16[4,32,128]{2,1,0:T(8,128)(2,1)S(1)} %slice.4), channel_id=3, replica_groups={{0,1,32,33},{2,3,34,35},{4,5,36,37},{6,7,38,39},{8,9,40,41},{10,11,42,4..., dimensions={0}, use_global_device_ids=true | all-gather | bytes 163840 | tf_op jit(solution)/shard_map/all_gather | solution.py:400
  40.2 0.0 copy-done.7
  40.2 0.0 copy-done.2
  40.2 0.0 copy-done.4
  40.2 0.0 copy-start
  40.2 1.7 %copy-done = bf16[4,4,9,64,64]{4,3,2,1,0:T(8,128)(2,1)S(1)} copy-done((bf16[4,4,9,64,64]{4,3,2,1,0:T(8,128)(2,1)S(1)}, bf16[4,4,9,64,64]{4,3,2,1,0:T(8,128)(2,1)}, u32[]{:S(2)}) %copy-start) | copy-done | bytes 1179672
  41.9 3.5 %shard_map.66 = bf16[32,1024]{1,0:T(8,128)(2,1)} custom-call(bf16[4,320,128]{2,1,0:T(8,128)(2,1)S(1)} %bitcast.12, bf16[256,128]{1,0:T(8,128)(2,1)S(1)} %get-tuple-element.8.x, bf16[4,288,128]{2,1,0:T(8,128)(2,1)S(1)} %all-to-all-done.cross, bf16[4,4,32,128]{3,2,1,0:T(8,128)(2,1)S(1)} %bitcast.13, bf16[4,4,9,64,64]{4,3,2,1,0:T(8,128)(2,1)S(1)} %copy-done, ...), custom_call_target="tpu_custom_call" | custom-call | tf_op jit(solution)/shard_map/pallas_call | solution.py:401
  (1 shorter events, 0.0 us)
Async XLA Ops:
  0.0 40.2 %copy-start.7 = (s32[1024]{0:T(1024)S(1)}, s32[1024]{0:T(1024)}, u32[]{:S(2)}) copy-start(s32[1024]{0:T(1024)} %param.7) | copy-start | bytes 12292
  0.0 0.9 %copy-start.1 = (bf16[4,4,64,32]{2,3,1,0:T(8,128)(2,1)S(1)}, bf16[4,4,64,32]{2,3,1,0:T(8,128)(2,1)}, u32[]{:S(2)}) copy-start(bf16[4,4,64,32]{2,3,1,0:T(8,128)(2,1)} %param.8) | copy-start | bytes 196612
  0.9 0.8 %copy-start.3 = (bf16[2,4,32,32]{3,2,1,0:T(8,128)(2,1)S(1)}, bf16[2,4,32,32]{3,2,1,0:T(8,128)(2,1)}, u32[]{:S(2)}) copy-start(bf16[2,4,32,32]{3,2,1,0:T(8,128)(2,1)} %param.10) | copy-start | bytes 49156
  1.8 0.8 %copy-start.5 = (bf16[1024,32]{0,1:T(8,128)(2,1)S(1)}, bf16[1024,32]{0,1:T(8,128)(2,1)}, u32[]{:S(2)}) copy-start(bf16[1024,32]{0,1:T(8,128)(2,1)} %param.6) | copy-start | bytes 196612
  2.6 0.7 %copy-start.6 = (s32[1024]{0:T(1024)S(1)}, s32[1024]{0:T(1024)}, u32[]{:S(2)}) copy-start(s32[1024]{0:T(1024)} %param.7) | copy-start | bytes 12292
  3.3 22.7 %copy-start.8 = (bf16[3,40,32,32]{1,3,2,0:T(8,128)(2,1)S(1)}, bf16[3,40,32,32]{1,3,2,0:T(8,128)(2,1)}, u32[]{:S(2)}) copy-start(bf16[3,40,32,32]{1,3,2,0:T(8,128)(2,1)} %param.11) | copy-start | bytes 737284
  3.3 36.9 %copy-start.2 = (bf16[4,4,64,32]{2,3,1,0:T(8,128)(2,1)S(1)}, bf16[4,4,64,32]{2,3,1,0:T(8,128)(2,1)}, u32[]{:S(2)}) copy-start(bf16[4,4,64,32]{2,3,1,0:T(8,128)(2,1)} %param.8) | copy-start | bytes 196612
  3.3 36.9 %copy-start.4 = (bf16[2,4,32,32]{3,2,1,0:T(8,128)(2,1)S(1)}, bf16[2,4,32,32]{3,2,1,0:T(8,128)(2,1)}, u32[]{:S(2)}) copy-start(bf16[2,4,32,32]{3,2,1,0:T(8,128)(2,1)} %param.10) | copy-start | bytes 49156
  18.7 12.1 %all-to-all-start = ((bf16[4,288,128]{2,1,0:T(8,128)(2,1)}), bf16[4,288,128]{2,1,0:T(8,128)(2,1)S(1)}, u32[]{:S(2)}, u32[]{:S(2)}) async-start(bf16[4,288,128]{2,1,0:T(8,128)(2,1)} %shard_map.65), calls=%async_computation | async-start | bytes 589824 | tf_op jit(solution)/shard_map/all_to_all | solution.py:399
  40.2 1.7 %copy-start = (bf16[4,4,9,64,64]{4,3,2,1,0:T(8,128)(2,1)S(1)}, bf16[4,4,9,64,64]{4,3,2,1,0:T(8,128)(2,1)}, u32[]{:S(2)}) copy-start(bf16[4,4,9,64,64]{4,3,2,1,0:T(8,128)(2,1)} %near.1) | copy-start | bytes 3538948

commit v2 on v1

--- a/solution.py
+++ b/solution.py
@@ -8,7 +8,8 @@
 BF = jnp.bfloat16
 F32 = jnp.float32
 AXES = ("gx", "gy")
-VMEM_BYTES = 48 * 1024 * 1024
+VMEM_BYTES = 32 * 1024 * 1024
+VMEM, FAR_MEMORY = pltpu.VMEM, pltpu.HBM
 
 OWN_ROW, OWN_COL, OWN_E0, OWN_E1, OWN_E2, OWN_ROWS = 0, 64, 128, 256, 288, 320
 FAR_X, FAR_E0, FAR_CORNER, FAR_E1, FAR_E1_SIDE, FAR_E2, FAR_ROWS = 0, 64, 128, 192, 224, 256, 288
@@ -57,8 +58,25 @@
     return out
 
 
-def upward_kernel(samples, order, basis, transfer, x_out, msg):
+def fetch(sources, targets, sems):
+    copies = [
+        pltpu.make_async_copy(source, target, sems.at[n])
+        for n, (source, target) in enumerate(zip(sources, targets))
+    ]
+    for copy in copies:
+        copy.start()
+    return copies
+
+
+def upward_kernel(
+    samples_hbm, order_hbm, basis_hbm, transfer_hbm, x_out, msg, samples, order, basis, transfer, sems
+):
+    copies = fetch(
+        (order_hbm, samples_hbm, basis_hbm, transfer_hbm), (order, samples, basis, transfer), sems
+    )
     _, _, pi, pj = place()
+    copies[0].wait()
+    copies[1].wait()
     slot = slot_of(64)
     spread = jnp.concatenate([samples[...]] * 4, axis=0)
     lane = lane_of(128)
@@ -75,6 +93,8 @@
             )
             picked.append(dot_nt(pick, spread))
         x = merge_diagonal(jnp.concatenate(picked, axis=0), 64).astype(BF)
+        if a == 0:
+            copies[2].wait()
         x_out[a * 64 : (a + 1) * 64, :] = x
         e0 = merge_diagonal(dot(basis[a * 128 : (a + 1) * 128, :], x), 32).astype(BF)
         msg[OWN_E0 + a * 32 : OWN_E0 + (a + 1) * 32, :] = e0
@@ -89,6 +109,7 @@
 
     one = eye(32)
     slot = slot_of(32)
+    copies[3].wait()
     turned = [dot_nt(one, transfer[n * 32 : (n + 1) * 32, :]).astype(BF) for n in range(8)]
     e1 = jnp.zeros((32, 128), F32)
     for x in range(2):
@@ -184,9 +205,67 @@
     return out
 
 
+def inner_kernel(group, x, near_hbm, coupling, near_out, far, near, sems):
+    copies = fetch([near_hbm.at[a] for a in range(4)], [near.at[a] for a in range(4)], sems)
+    _, _, pi, pj = place()
+    across_x, across_y, across = 2 * (1 - pi) + pj, 2 * pi + 1 - pj, 2 * (1 - pi) + 1 - pj
+    far[...] = jnp.zeros(far.shape, BF)
+    for level in range(3):
+        n = 0
+        for u in range(-3, 4):
+            for w in range(-3, 4):
+                if max(abs(u), abs(w)) >= 2:
+                    start = (level * 40 + n) * 32
+                    far[level, (w + 3) * 32 : (w + 4) * 32, (u + 3) * 32 : (u + 4) * 32] = (
+                        coupling[start : start + 32, :]
+                    )
+                    n += 1
+
+
+    slot = slot_of(64)
+    windows = {}
+
+    def store_windows(a, middle, inner):
+        left = jnp.where(pj == 0, jnp.zeros_like(inner), inner)
+        right = jnp.where(pj == 0, inner, jnp.zeros_like(inner))
+        windows[a, 0] = middle
+        windows[a, -1] = roll(jnp.where(slot == 3, left, middle), 32)
+        windows[a, 1] = roll(jnp.where(slot == 0, right, middle), -32)
+
+    beside = group[across_y, OWN_COL : OWN_COL + 64, :]
+    for a in range(4):
+        store_windows(a, x[a * 64 : (a + 1) * 64, :], roll(beside, -32 * a))
+    middle = group[across_x, OWN_ROW : OWN_ROW + 64, :]
+    inner = group[across, OWN_ROW : OWN_ROW + 64, :]
+    nothing = jnp.zeros((64, 128), BF)
+    store_windows(-1, jnp.where(pi == 0, nothing, middle), jnp.where(pi == 0, nothing, inner))
+    store_windows(4, jnp.where(pi == 0, middle, nothing), jnp.where(pi == 0, inner, nothing))
+    for a in range(4):
+        copies[a].wait()
+        total = jnp.zeros((256, 128), F32)
+        for n in range(9):
+            matrix = near[a, :, n].reshape(256, 64)
+            total = total + dot(matrix, windows[a + n // 3 - 1, n % 3 - 1])
+        near_out[a * 64 : (a + 1) * 64, :] = merge_diagonal(total, 64)
+
+
 def downward_kernel(count_x, count_y):
-    def body(group, x, cross, shared, near, basis, transfer, coupling, order, out, far, h0, h1, h2):
+    def body(
+        group, near_part, far, cross, shared, near_hbm, basis_hbm, transfer_hbm, order_hbm, out,
+        h0, h1, h2, near_row, near_col, basis, transfer, order, sems,
+    ):
         gx, gy, pi, pj = place()
+        copies = fetch(
+            (
+                transfer_hbm,
+                near_hbm.at[3 * pi, :, pl.ds(6 * pi, 3)],
+                near_hbm.at[:, 3 * pj],
+                basis_hbm,
+                order_hbm,
+            ),
+            (transfer, near_row, near_col, basis, order),
+            sems,
+        )
         me, across_x, across_y = 2 * pi + pj, 2 * (1 - pi) + pj, 2 * pi + 1 - pj
         across = 2 * (1 - pi) + 1 - pj
         from_x, from_y, from_xy = 2 * pi + 1 - pj, 2 * (1 - pi) + pj, 2 * pi + pj
@@ -196,18 +275,6 @@
 
         def kept(keep, value):
             return jnp.where(keep, value, jnp.zeros_like(value))
-
-        far[...] = jnp.zeros(far.shape, BF)
-        for level in range(3):
-            n = 0
-            for u in range(-3, 4):
-                for w in range(-3, 4):
-                    if max(abs(u), abs(w)) >= 2:
-                        start = (level * 40 + n) * 32
-                        far[level, (w + 3) * 32 : (w + 4) * 32, (u + 3) * 32 : (u + 4) * 32] = (
-                            coupling[start : start + 32, :]
-                        )
-                        n += 1
 
         lane = lane_of(64)
         near_half = (lane < 64) == (pj == 0)
@@ -285,6 +352,7 @@
         local2 = jnp.where(slot == pj, local2, 0.0)
         local2 = local2 + roll(local2, 64)
         local2 = (local2 + roll(local2, 32)).astype(BF)
+        copies[0].wait()
         spread = dot(transfer[128:256, :], local2)
         local1 = []
         for i in range(2):
@@ -302,51 +370,55 @@
             down = down + jnp.where(lax.rem(slot, 2) == 0, spread[:32], spread[32:])
             local0.append(down.astype(BF))
 
+
         slot = slot_of(64)
+        copies[1].wait()
+        copies[2].wait()
         column = kept(has_y, cross[from_y, FAR_X : FAR_X + 64, :])
-        beside = group[across_y, OWN_COL : OWN_COL + 64, :]
-        windows = {}
-
-        def store_windows(a, middle, inner, outer):
-            left = jnp.where(pj == 0, outer, inner)
-            right = jnp.where(pj == 0, inner, outer)
-            windows[a, 0] = middle
-            windows[a, -1] = roll(jnp.where(slot == 3, left, middle), 32)
-            windows[a, 1] = roll(jnp.where(slot == 0, right, middle), -32)
-
-        for a in range(4):
-            store_windows(
-                a, x[a * 64 : (a + 1) * 64, :], roll(beside, -32 * a), roll(column, -32 * a)
-            )
-        inside = (
-            group[across_x, OWN_ROW : OWN_ROW + 64, :],
-            group[across, OWN_ROW : OWN_ROW + 64, :],
-            kept(has_y, roll(cross[from_y, FAR_CORNER : FAR_CORNER + 64, :], 64)),
-        )
-        outside = (
-            kept(has_x, cross[from_x, FAR_X : FAR_X + 64, :]),
-            kept(has_x, roll(cross[from_x, FAR_CORNER : FAR_CORNER + 64, :], 64)),
-            kept(has_xy, roll(cross[from_xy, FAR_CORNER : FAR_CORNER + 64, :], 64)),
-        )
-        store_windows(-1, *[jnp.where(pi == 0, o, i) for o, i in zip(outside, inside)])
-        store_windows(4, *[jnp.where(pi == 0, i, o) for o, i in zip(outside, inside)])
+        corner_in = kept(has_y, roll(cross[from_y, FAR_CORNER : FAR_CORNER + 64, :], 64))
+        corner_out = kept(has_xy, roll(cross[from_xy, FAR_CORNER : FAR_CORNER + 64, :], 64))
+        boxes = {a: roll(column, -32 * a) for a in range(4)}
+        boxes[-1] = jnp.where(pi == 0, corner_out, corner_in)
+        boxes[4] = jnp.where(pi == 0, corner_in, corner_out)
+        edge = slot == 3 * pj
+        for a in boxes:
+            moved = jnp.where(pj == 0, roll(boxes[a], 32), roll(boxes[a], -32))
+            boxes[a] = jnp.where(edge, moved, jnp.zeros_like(moved))
+        middle = kept(has_x, cross[from_x, FAR_X : FAR_X + 64, :])
+        inner = kept(has_x, roll(cross[from_x, FAR_CORNER : FAR_CORNER + 64, :], 64))
+        nothing = jnp.zeros_like(inner)
+        left = jnp.where(pj == 0, nothing, inner)
+        right = jnp.where(pj == 0, inner, nothing)
+        shifts = (
+            roll(jnp.where(slot == 3, left, middle), 32),
+            middle,
+            roll(jnp.where(slot == 0, right, middle), -32),
+        )
+        beyond = jnp.zeros((256, 128), F32)
+        for c in range(3):
+            beyond = beyond + dot(near_row[:, c].reshape(256, 64), shifts[c])
+        beyond = merge_diagonal(beyond, 64)
 
         row = lax.broadcasted_iota(jnp.int32, (256, 128), 0)
         diagonal = row // 64 == slot_of(256)
         block = lax.broadcasted_iota(jnp.int32, (128, 128), 0) // 32 == slot_of(128)
         leaves = []
+        copies[3].wait()
         for a in range(4):
-            total = jnp.zeros((256, 128), F32)
-            for n in range(9):
-                r, c = n // 3 - 1, n % 3 - 1
-                matrix = near[a, :, n].reshape(256, 64)
-                total = total + dot(matrix, windows[a + r, c])
+            total = near_part[a * 64 : (a + 1) * 64, :]
+            if a == 0:
+                total = total + jnp.where(pi == 0, beyond, 0.0)
+            if a == 3:
+                total = total + jnp.where(pi == 0, 0.0, beyond)
+            for r in range(3):
+                total = total + dot(near_col[a, 3 * r + 2 * pj], boxes[a + r - 1])
             leaf = jnp.transpose(basis[a * 128 : (a + 1) * 128, :].astype(F32)).astype(BF)
             local = jnp.concatenate([local0[a]] * 4, axis=0)
-            lift = dot(leaf, jnp.where(block, local, jnp.zeros_like(local)))
-            total = total + jnp.concatenate([lift] * 4, axis=0)
+            total = total + dot(leaf, jnp.where(block, local, jnp.zeros_like(local)))
+            total = jnp.concatenate([total] * 4, axis=0)
             leaves.append(jnp.where(diagonal, total, 0.0).astype(BF))
         leaves = jnp.concatenate(leaves, axis=0)
+        copies[4].wait()
         line = jnp.concatenate([order[g : g + 1, :] for g in range(8)], axis=1)
         for t in range(8):
             site = lax.broadcasted_iota(jnp.int32, (128, 1024), 0) + 128 * t
@@ -358,11 +430,13 @@
     return body
 
 
-def call(kernel, shapes, scratch=()):
+def call(kernel, in_spaces, shapes, scratch=(), flops=10**6):
     return pl.pallas_call(
         kernel,
+        in_specs=[pl.BlockSpec(memory_space=space) for space in in_spaces],
         out_shape=shapes,
         scratch_shapes=list(scratch),
+        cost_estimate=pl.CostEstimate(flops=flops, bytes_accessed=2**20, transcendentals=0),
         compiler_params=pltpu.CompilerParams(vmem_limit_bytes=VMEM_BYTES),
     )
 
@@ -392,22 +466,43 @@
         coupling = coupling.reshape(3840, 32)
         x, message = call(
             upward_kernel,
+            (FAR_MEMORY,) * 4,
             (jax.ShapeDtypeStruct((256, 128), BF), jax.ShapeDtypeStruct((OWN_ROWS, 128), BF)),
+            (
+                pltpu.VMEM((32, 1024), BF),
+                pltpu.VMEM((8, 128), jnp.int32),
+                pltpu.VMEM((512, 64), BF),
+                pltpu.VMEM((256, 32), BF),
+                pltpu.SemaphoreType.DMA((4,)),
+            ),
         )(samples, order, basis, transfer)
         group = lax.all_gather(message, AXES, axis_index_groups=aligned)
-        send = call(cross_kernel, jax.ShapeDtypeStruct((4, FAR_ROWS, 128), BF))(group, x)
+        send = call(cross_kernel, (VMEM,) * 2, jax.ShapeDtypeStruct((4, FAR_ROWS, 128), BF))(group, x)
         cross = lax.all_to_all(send, AXES, 0, 0, axis_index_groups=shifted)
+        near_part, far = call(
+            inner_kernel,
+            (VMEM, VMEM, FAR_MEMORY, VMEM),
+            (jax.ShapeDtypeStruct((256, 128), F32), jax.ShapeDtypeStruct((3, 224, 224), BF)),
+            (pltpu.VMEM((4, 4, 9, 64, 64), BF), pltpu.SemaphoreType.DMA((4,))),
+            flops=10**9,
+        )(group, x, near_blocks, coupling)
         shared = lax.all_gather(cross[:, FAR_E2 : FAR_E2 + 32], AXES, axis_index_groups=aligned)
         out = call(
             downward_kernel(count_x, count_y),
+            (VMEM,) * 5 + (FAR_MEMORY,) * 4,
             jax.ShapeDtypeStruct((32, 1024), BF),
             (
-                pltpu.VMEM((3, 224, 224), BF),
                 pltpu.VMEM((320, 256), BF),
                 pltpu.VMEM((256, 256), BF),
                 pltpu.VMEM((256, 256), BF),
+                pltpu.VMEM((4, 3, 64, 64), BF),
+                pltpu.VMEM((4, 9, 64, 64), BF),
+                pltpu.VMEM((512, 64), BF),
+                pltpu.VMEM((256, 32), BF),
+                pltpu.VMEM((8, 128), jnp.int32),
+                pltpu.SemaphoreType.DMA((5,)),
             ),
-        )(group, x, cross, shared, near_blocks, basis, transfer, coupling, order)
+        )(group, near_part, far, cross, shared, near_blocks, basis, transfer, order)
         return out.T
 
     return jax.shard_map(

time: 45.8 us -> 50.6 us (1.10)
  Pallas kernels: 6.31 us -> 10.3 us
  waiting for transfers between devices: 3.85 us -> 0.01 us
  local copies, waits for them, and re-layouts: 5.89 us -> 9.63 us
  blocking collectives: 22.1 us -> 23 us
    pallas_call x3 -> x4, Pallas kernels: 6.31 us -> 10.3 us  [the longest x1 3.93 us: local(): call(downward_kernel(count_x, count_y), (VMEM,) * 5 + (FAR_MEMORY,) * 4,...]
    all_to_all x1, waiting for transfers between devices: 3.85 us -> 0.01 us  [local(): cross = lax.all_to_all(send, AXES, 0, 0, axis_index_groups=shifted)]
    unnamed x19 -> x27, local copies, waits for them, and re-layouts: 5.89 us -> 9.62 us
    all_gather x1, blocking collectives: 9.38 us -> 10.3 us  [local(): lax.all_gather(cross[:, FAR_E2:FAR_E2 + 32], AXES, axis_index_groups=alig...]
  transfers between devices with their start and end apart: 1 -> 1, of which waited for: 1 -> 0; matrix products, arithmetic and copies ran while one was open for 2% -> 5% of each run, Pallas kernels for 0% -> 6%
where the time goes in v2:
time: 50.6 us; the launch traced here: 50.2 us
  blocking collectives  23 us (45%)
  Pallas kernels  10.3 us (20%)
  local copies, waits for them, and re-layouts  9.63 us (19%)
  starting transfers between devices  7.26 us (14%)
    all_gather x1, blocking collectives, local(): group = lax.all_gather(message, AXES, axis_index_groups=aligned)  12.7 us
    all_gather x1, blocking collectives, local(): lax.all_gather(cross[:, FAR_E2:FAR_E2 + 32], AXES, axis_index_groups=alig...  10.3 us
    unnamed x27, local copies, waits for them, and re-layouts  9.62 us
    all_to_all x1, starting transfers between devices, local(): cross = lax.all_to_all(send, AXES, 0, 0, axis_index_groups=shifted)  7.26 us
    pallas_call x1, Pallas kernels, local(): call(downward_kernel(count_x, count_y), (VMEM,) * 5 + (FAR_MEMORY,) * 4,...  3.93 us
    pallas_call x1, Pallas kernels, local(): call(inner_kernel, (VMEM, VMEM, FAR_MEMORY, VMEM), (jax.ShapeDtypeStruct(...  2.92 us
    pallas_call x1, Pallas kernels, local(): call(upward_kernel, (FAR_MEMORY,) * 4, (jax.ShapeDtypeStruct((256, 128),...  2.56 us
  transfers between devices with their start and end apart: 1, of which 0 were waited for; matrix products, arithmetic and copies ran while one was open for 5% of the time, Pallas kernels for 6%

profile of v2, /device:TPU:1, one launch (start us, length us, event | category | flops | bytes accessed | tf_op | source)
XLA Modules:
  0.0 50.2 jit_solution(823381449258020318)
XLA Ops:
  0.0 0.0 copy-start
  0.0 0.0 copy-start.2
  0.0 1.1 %copy-done.2 = bf16[4,4,64,32]{2,3,1,0:T(8,128)(2,1)S(1)} copy-done((bf16[4,4,64,32]{2,3,1,0:T(8,128)(2,1)S(1)}, bf16[4,4,64,32]{2,3,1,0:T(8,128)(2,1)}, u32[]{:S(2)}) %copy-start.2) | copy-done | bytes 65560
  1.1 0.0 copy-start.4
  1.1 0.8 %copy-done.4 = bf16[2,4,32,32]{3,2,1,0:T(8,128)(2,1)S(1)} copy-done((bf16[2,4,32,32]{3,2,1,0:T(8,128)(2,1)S(1)}, bf16[2,4,32,32]{3,2,1,0:T(8,128)(2,1)}, u32[]{:S(2)}) %copy-start.4) | copy-done | bytes 16408
  1.9 0.0 copy-start.10
  1.9 0.8 %copy-done.10 = bf16[1024,32]{0,1:T(8,128)(2,1)S(1)} copy-done((bf16[1024,32]{0,1:T(8,128)(2,1)S(1)}, bf16[1024,32]{0,1:T(8,128)(2,1)}, u32[]{:S(2)}) %copy-start.10) | copy-done | bytes 65560
  2.7 0.0 copy-start.11
  2.7 0.7 %copy-done.11 = s32[1024]{0:T(1024)S(1)} copy-done((s32[1024]{0:T(1024)S(1)}, s32[1024]{0:T(1024)}, u32[]{:S(2)}) %copy-start.11) | copy-done | bytes 4120
  3.4 2.6 %shard_map.64 = (bf16[256,128]{1,0:T(8,128)(2,1)S(1)}, bf16[320,128]{1,0:T(8,128)(2,1)S(1)}) custom-call(bf16[32,1024]{1,0:T(8,128)(2,1)S(1)} %bitcast.19, s32[8,128]{1,0:T(8,128)S(1)} %bitcast.20, bf16[512,64]{1,0:T(8,128)(2,1)S(1)} %bitcast.15, bf16[256,32]{1,0:T(8,128)(2,1)S(1)} %bitcast.17), custom_call_target="tpu_custom_call" | custom-call | flops 1000000 | bytes 1048576 | tf_op jit(solution)/shard_map/pallas_call | solution.py:467
  6.0 0.0 copy-start.6
  6.0 12.7 %all-gather = bf16[1280,128]{1,0:T(8,128)(2,1)S(1)} all-gather(bf16[320,128]{1,0:T(8,128)(2,1)S(1)} %get-tuple-element.9), channel_id=2, replica_groups={{0,1,32,33},{2,3,34,35},{4,5,36,37},{6,7,38,39},{8,9,40,41},{10,11,42,4..., dimensions={0}, use_global_device_ids=true | all-gather | bytes 409600 | tf_op jit(solution)/shard_map/all_gather | solution.py:479
  18.7 0.0 copy-done.6
  18.7 0.8 %shard_map.66 = bf16[4,288,128]{2,1,0:T(8,128)(2,1)} custom-call(bf16[4,320,128]{2,1,0:T(8,128)(2,1)S(1)} %bitcast.10, bf16[256,128]{1,0:T(8,128)(2,1)S(1)} %get-tuple-element.10.x), custom_call_target="tpu_custom_call" | custom-call | flops 1000000 | bytes 1048576 | tf_op jit(solution)/shard_map/pallas_call | solution.py:480
  19.5 7.3 %all-to-all-start = ((bf16[4,288,128]{2,1,0:T(8,128)(2,1)}), bf16[4,288,128]{2,1,0:T(8,128)(2,1)S(1)}, u32[]{:S(2)}, u32[]{:S(2)}) async-start(bf16[4,288,128]{2,1,0:T(8,128)(2,1)} %shard_map.66), calls=%async_computation | async-start | bytes 589824 | tf_op jit(solution)/shard_map/all_to_all | solution.py:481
  26.8 2.6 %copy.8 = bf16[3,40,32,32]{3,2,1,0:T(8,128)(2,1)} copy(bf16[3,40,32,32]{1,3,2,0:T(8,128)(2,1)} %param.11) | data formatting | bytes 491520 | tf_op args[5]
  29.4 0.0 copy-done
  29.4 0.0 copy-start.1
  29.4 1.2 %copy-done.1 = bf16[3,40,32,32]{3,2,1,0:T(8,128)(2,1)S(1)} copy-done((bf16[3,40,32,32]{3,2,1,0:T(8,128)(2,1)S(1)}, bf16[3,40,32,32]{3,2,1,0:T(8,128)(2,1)}, u32[]{:S(2)}) %copy-start.1) | copy-done | bytes 245784
  30.6 0.0 copy-start.7
  30.6 0.8 %copy-done.7 = bf16[256,128]{1,0:T(8,128)(2,1)S(1)} copy-done((bf16[256,128]{1,0:T(8,128)(2,1)S(1)}, bf16[256,128]{1,0:T(8,128)(2,1)}, u32[]{:S(2)}) %copy-start.7) | copy-done | bytes 65560
  31.4 0.0 copy-start.3
  31.4 0.0 copy-start.5
  31.4 0.0 copy-start.12
  31.4 2.9 %shard_map.65 = (f32[256,128]{1,0:T(8,128)S(1)}, bf16[3,224,224]{2,1,0:T(8,128)(2,1)S(1)}) custom-call(bf16[4,320,128]{2,1,0:T(8,128)(2,1)S(1)} %bitcast.11, bf16[256,128]{1,0:T(8,128)(2,1)S(1)} %copy-done.7, bf16[4,4,9,64,64]{4,3,2,1,0:T(8,128)(2,1)S(1)} %copy-done, bf16[3840,32]{1,0:T(8,128)(2,1)S(1)} %bitcast.13), custom_call_target="tpu_custom_call" | custom-call | flops 1000000000 | bytes 1048576 | tf_op jit(solution)/shard_map/pallas_call | solution.py:482
  34.4 0.0 copy-start.8
  34.4 0.6 %copy-done.8 = f32[256,128]{1,0:T(8,128)} copy-done((f32[256,128]{1,0:T(8,128)}, f32[256,128]{1,0:T(8,128)S(1)}, u32[]{:S(2)}) %copy-start.8) | copy-done | bytes 131096
  35.0 0.0 all-to-all-done.cross
  35.0 10.3 %all-gather.1 = bf16[16,32,128]{2,1,0:T(8,128)(2,1)S(1)} all-gather(bf16[4,32,128]{2,1,0:T(8,128)(2,1)S(1)} %slice.4), channel_id=3, replica_groups={{0,1,32,33},{2,3,34,35},{4,5,36,37},{6,7,38,39},{8,9,40,41},{10,11,42,4..., dimensions={0}, use_global_device_ids=true | all-gather | bytes 163840 | tf_op jit(solution)/shard_map/all_gather | solution.py:489
  45.3 0.0 copy-done.3
  45.3 0.0 copy-done.5
  45.3 0.0 copy-done.12
  45.3 0.0 copy-start.9
  45.3 0.9 %copy-done.9 = f32[256,128]{1,0:T(8,128)S(1)} copy-done((f32[256,128]{1,0:T(8,128)S(1)}, f32[256,128]{1,0:T(8,128)}, u32[]{:S(2)}) %copy-start.9) | copy-done | bytes 131096
  46.2 3.9 %shard_map.67 = bf16[32,1024]{1,0:T(8,128)(2,1)} custom-call(bf16[4,320,128]{2,1,0:T(8,128)(2,1)S(1)} %bitcast.12, f32[256,128]{1,0:T(8,128)S(1)} %copy-done.9, bf16[3,224,224]{2,1,0:T(8,128)(2,1)S(1)} %get-tuple-element.12.far, bf16[4,288,128]{2,1,0:T(8,128)(2,1)S(1)} %all-to-all-done.cross, bf16[4,4,32,128]{3,2,1,0:T(8,128)(2,1)S(1)} %bitcast.14, ...), custom_call_target="tpu_custom_call" | custom-call | flops 1000000 | bytes 1048576 | tf_op jit(solution)/shard_map/pallas_call | solution.py:490
  (1 shorter events, 0.0 us)
Async XLA Ops:
  0.0 29.4 %copy-start = (bf16[4,4,9,64,64]{4,3,2,1,0:T(8,128)(2,1)S(1)}, bf16[4,4,9,64,64]{4,3,2,1,0:T(8,128)(2,1)}, u32[]{:S(2)}) copy-start(bf16[4,4,9,64,64]{4,3,2,1,0:T(8,128)(2,1)} %near_hbm.3) | copy-start | bytes 3538948
  0.0 1.1 %copy-start.2 = (bf16[4,4,64,32]{2,3,1,0:T(8,128)(2,1)S(1)}, bf16[4,4,64,32]{2,3,1,0:T(8,128)(2,1)}, u32[]{:S(2)}) copy-start(bf16[4,4,64,32]{2,3,1,0:T(8,128)(2,1)} %param.8) | copy-start | bytes 196612
  1.1 0.8 %copy-start.4 = (bf16[2,4,32,32]{3,2,1,0:T(8,128)(2,1)S(1)}, bf16[2,4,32,32]{3,2,1,0:T(8,128)(2,1)}, u32[]{:S(2)}) copy-start(bf16[2,4,32,32]{3,2,1,0:T(8,128)(2,1)} %param.10) | copy-start | bytes 49156
  1.9 0.8 %copy-start.10 = (bf16[1024,32]{0,1:T(8,128)(2,1)S(1)}, bf16[1024,32]{0,1:T(8,128)(2,1)}, u32[]{:S(2)}) copy-start(bf16[1024,32]{0,1:T(8,128)(2,1)} %param.6) | copy-start | bytes 196612
  2.7 0.7 %copy-start.11 = (s32[1024]{0:T(1024)S(1)}, s32[1024]{0:T(1024)}, u32[]{:S(2)}) copy-start(s32[1024]{0:T(1024)} %param.7) | copy-start | bytes 12292
  6.0 12.7 %copy-start.6 = (bf16[256,128]{1,0:T(8,128)(2,1)}, bf16[256,128]{1,0:T(8,128)(2,1)S(1)}, u32[]{:S(2)}) copy-start(bf16[256,128]{1,0:T(8,128)(2,1)S(1)} %get-tuple-element.10.x) | copy-start | bytes 196612
  19.5 15.5 %all-to-all-start = ((bf16[4,288,128]{2,1,0:T(8,128)(2,1)}), bf16[4,288,128]{2,1,0:T(8,128)(2,1)S(1)}, u32[]{:S(2)}, u32[]{:S(2)}) async-start(bf16[4,288,128]{2,1,0:T(8,128)(2,1)} %shard_map.66), calls=%async_computation | async-start | bytes 589824 | tf_op jit(solution)/shard_map/all_to_all | solution.py:481
  29.4 1.2 %copy-start.1 = (bf16[3,40,32,32]{3,2,1,0:T(8,128)(2,1)S(1)}, bf16[3,40,32,32]{3,2,1,0:T(8,128)(2,1)}, u32[]{:S(2)}) copy-start(bf16[3,40,32,32]{3,2,1,0:T(8,128)(2,1)} %copy.8) | copy-start | bytes 737284
  30.6 0.8 %copy-start.7 = (bf16[256,128]{1,0:T(8,128)(2,1)S(1)}, bf16[256,128]{1,0:T(8,128)(2,1)}, u32[]{:S(2)}) copy-start(bf16[256,128]{1,0:T(8,128)(2,1)} %copy-done.6) | copy-start | bytes 196612
  31.4 13.9 %copy-start.3 = (bf16[4,4,64,32]{2,3,1,0:T(8,128)(2,1)S(1)}, bf16[4,4,64,32]{2,3,1,0:T(8,128)(2,1)}, u32[]{:S(2)}) copy-start(bf16[4,4,64,32]{2,3,1,0:T(8,128)(2,1)} %param.8) | copy-start | bytes 196612
  31.4 13.9 %copy-start.5 = (bf16[2,4,32,32]{3,2,1,0:T(8,128)(2,1)S(1)}, bf16[2,4,32,32]{3,2,1,0:T(8,128)(2,1)}, u32[]{:S(2)}) copy-start(bf16[2,4,32,32]{3,2,1,0:T(8,128)(2,1)} %param.10) | copy-start | bytes 49156
  31.4 13.9 %copy-start.12 = (s32[1024]{0:T(1024)S(1)}, s32[1024]{0:T(1024)}, u32[]{:S(2)}) copy-start(s32[1024]{0:T(1024)} %param.7) | copy-start | bytes 12292
  34.4 0.7 %copy-start.8 = (f32[256,128]{1,0:T(8,128)}, f32[256,128]{1,0:T(8,128)S(1)}, u32[]{:S(2)}) copy-start(f32[256,128]{1,0:T(8,128)S(1)} %get-tuple-element.11.near_part) | copy-start | bytes 393220
  45.3 0.9 %copy-start.9 = (f32[256,128]{1,0:T(8,128)S(1)}, f32[256,128]{1,0:T(8,128)}, u32[]{:S(2)}) copy-start(f32[256,128]{1,0:T(8,128)} %copy-done.8) | copy-start | bytes 393220

commit v3 on v2

--- a/solution.py
+++ b/solution.py
@@ -9,7 +9,7 @@
 F32 = jnp.float32
 AXES = ("gx", "gy")
 VMEM_BYTES = 32 * 1024 * 1024
-VMEM, FAR_MEMORY = pltpu.VMEM, pltpu.HBM
+VMEM = pltpu.VMEM
 
 OWN_ROW, OWN_COL, OWN_E0, OWN_E1, OWN_E2, OWN_ROWS = 0, 64, 128, 256, 288, 320
 FAR_X, FAR_E0, FAR_CORNER, FAR_E1, FAR_E1_SIDE, FAR_E2, FAR_ROWS = 0, 64, 128, 192, 224, 256, 288
@@ -69,10 +69,13 @@
 
 
 def upward_kernel(
-    samples_hbm, order_hbm, basis_hbm, transfer_hbm, x_out, msg, samples, order, basis, transfer, sems
+    samples_hbm, order_hbm, basis_hbm, transfer_hbm, coupling_hbm, near_hbm,
+    x_out, msg, order, basis, transfer, coupling, near, samples, sems,
 ):
     copies = fetch(
-        (order_hbm, samples_hbm, basis_hbm, transfer_hbm), (order, samples, basis, transfer), sems
+        (order_hbm, samples_hbm, basis_hbm, transfer_hbm, coupling_hbm, near_hbm),
+        (order, samples, basis, transfer, coupling, near),
+        sems,
     )
     _, _, pi, pj = place()
     copies[0].wait()
@@ -125,6 +128,8 @@
     e2 = e2 + roll(e2, 64)
     e2 = e2 + roll(e2, 32)
     msg[OWN_E2 : OWN_E2 + 32, :] = jnp.where(slot == 2 * pi + pj, e2, 0.0).astype(BF)
+    copies[4].wait()
+    copies[5].wait()
 
 
 def cross_kernel(group, x, send):
@@ -205,8 +210,7 @@
     return out
 
 
-def inner_kernel(group, x, near_hbm, coupling, near_out, far, near, sems):
-    copies = fetch([near_hbm.at[a] for a in range(4)], [near.at[a] for a in range(4)], sems)
+def inner_kernel(group, x, near, coupling, basis, order, near_out, far, leaf, pick):
     _, _, pi, pj = place()
     across_x, across_y, across = 2 * (1 - pi) + pj, 2 * pi + 1 - pj, 2 * (1 - pi) + 1 - pj
     far[...] = jnp.zeros(far.shape, BF)
@@ -241,31 +245,24 @@
     store_windows(-1, jnp.where(pi == 0, nothing, middle), jnp.where(pi == 0, nothing, inner))
     store_windows(4, jnp.where(pi == 0, middle, nothing), jnp.where(pi == 0, inner, nothing))
     for a in range(4):
-        copies[a].wait()
         total = jnp.zeros((256, 128), F32)
         for n in range(9):
             matrix = near[a, :, n].reshape(256, 64)
             total = total + dot(matrix, windows[a + n // 3 - 1, n % 3 - 1])
         near_out[a * 64 : (a + 1) * 64, :] = merge_diagonal(total, 64)
+        turned = jnp.transpose(basis[a * 128 : (a + 1) * 128, :].astype(F32))
+        leaf[a * 64 : (a + 1) * 64, :] = turned.astype(BF)
+    line = jnp.concatenate([order[g : g + 1, :] for g in range(8)], axis=1)
+    for t in range(8):
+        site = lax.broadcasted_iota(jnp.int32, (128, 1024), 0) + 128 * t
+        pick[128 * t : 128 * (t + 1), :] = jnp.where(site == line, 1.0, 0.0).astype(BF)
 
 
 def downward_kernel(count_x, count_y):
     def body(
-        group, near_part, far, cross, shared, near_hbm, basis_hbm, transfer_hbm, order_hbm, out,
-        h0, h1, h2, near_row, near_col, basis, transfer, order, sems,
+        group, near_part, far, leaf, pick, cross, shared, near, transfer, out, h0, h1, h2
     ):
         gx, gy, pi, pj = place()
-        copies = fetch(
-            (
-                transfer_hbm,
-                near_hbm.at[3 * pi, :, pl.ds(6 * pi, 3)],
-                near_hbm.at[:, 3 * pj],
-                basis_hbm,
-                order_hbm,
-            ),
-            (transfer, near_row, near_col, basis, order),
-            sems,
-        )
         me, across_x, across_y = 2 * pi + pj, 2 * (1 - pi) + pj, 2 * pi + 1 - pj
         across = 2 * (1 - pi) + 1 - pj
         from_x, from_y, from_xy = 2 * pi + 1 - pj, 2 * (1 - pi) + pj, 2 * pi + pj
@@ -352,7 +349,6 @@
         local2 = jnp.where(slot == pj, local2, 0.0)
         local2 = local2 + roll(local2, 64)
         local2 = (local2 + roll(local2, 32)).astype(BF)
-        copies[0].wait()
         spread = dot(transfer[128:256, :], local2)
         local1 = []
         for i in range(2):
@@ -372,8 +368,6 @@
 
 
         slot = slot_of(64)
-        copies[1].wait()
-        copies[2].wait()
         column = kept(has_y, cross[from_y, FAR_X : FAR_X + 64, :])
         corner_in = kept(has_y, roll(cross[from_y, FAR_CORNER : FAR_CORNER + 64, :], 64))
         corner_out = kept(has_xy, roll(cross[from_xy, FAR_CORNER : FAR_CORNER + 64, :], 64))
@@ -396,14 +390,13 @@
         )
         beyond = jnp.zeros((256, 128), F32)
         for c in range(3):
-            beyond = beyond + dot(near_row[:, c].reshape(256, 64), shifts[c])
+            beyond = beyond + dot(near[3 * pi, :, 6 * pi + c].reshape(256, 64), shifts[c])
         beyond = merge_diagonal(beyond, 64)
 
         row = lax.broadcasted_iota(jnp.int32, (256, 128), 0)
         diagonal = row // 64 == slot_of(256)
         block = lax.broadcasted_iota(jnp.int32, (128, 128), 0) // 32 == slot_of(128)
         leaves = []
-        copies[3].wait()
         for a in range(4):
             total = near_part[a * 64 : (a + 1) * 64, :]
             if a == 0:
@@ -411,34 +404,32 @@
             if a == 3:
                 total = total + jnp.where(pi == 0, 0.0, beyond)
             for r in range(3):
-                total = total + dot(near_col[a, 3 * r + 2 * pj], boxes[a + r - 1])
-            leaf = jnp.transpose(basis[a * 128 : (a + 1) * 128, :].astype(F32)).astype(BF)
+                total = total + dot(near[a, 3 * pj, 3 * r + 2 * pj], boxes[a + r - 1])
             local = jnp.concatenate([local0[a]] * 4, axis=0)
-            total = total + dot(leaf, jnp.where(block, local, jnp.zeros_like(local)))
+            total = total + dot(leaf[a * 64 : (a + 1) * 64, :], jnp.where(block, local, jnp.zeros_like(local)))
             total = jnp.concatenate([total] * 4, axis=0)
             leaves.append(jnp.where(diagonal, total, 0.0).astype(BF))
         leaves = jnp.concatenate(leaves, axis=0)
-        copies[4].wait()
-        line = jnp.concatenate([order[g : g + 1, :] for g in range(8)], axis=1)
         for t in range(8):
-            site = lax.broadcasted_iota(jnp.int32, (128, 1024), 0) + 128 * t
-            pick = jnp.where(site == line, 1.0, 0.0).astype(BF)
-            done = jnp.transpose(dot(pick, leaves))
+            done = jnp.transpose(dot(pick[128 * t : 128 * (t + 1), :], leaves))
             done = (done[:32] + done[32:64]) + (done[64:96] + done[96:])
             out[:, 128 * t : 128 * (t + 1)] = done.astype(BF)
 
     return body
 
 
-def call(kernel, in_spaces, shapes, scratch=(), flops=10**6):
-    return pl.pallas_call(
-        kernel,
-        in_specs=[pl.BlockSpec(memory_space=space) for space in in_spaces],
-        out_shape=shapes,
-        scratch_shapes=list(scratch),
-        cost_estimate=pl.CostEstimate(flops=flops, bytes_accessed=2**20, transcendentals=0),
-        compiler_params=pltpu.CompilerParams(vmem_limit_bytes=VMEM_BYTES),
-    )
+def call(kernel, shapes, scratch=(), inputs=VMEM, flops=10**6):
+    def run(*args):
+        return pl.pallas_call(
+            kernel,
+            out_shape=shapes,
+            in_specs=[pl.BlockSpec(memory_space=inputs)] * len(args),
+            scratch_shapes=list(scratch),
+            cost_estimate=pl.CostEstimate(flops=flops, bytes_accessed=2**20, transcendentals=0),
+            compiler_params=pltpu.CompilerParams(vmem_limit_bytes=VMEM_BYTES),
+        )(*[pltpu.with_memory_space_constraint(arg, inputs) for arg in args])
+
+    return run
 
 
 def groups_of_four(count_x, count_y, offset):
@@ -463,46 +454,41 @@
         order = site_order.reshape(8, 128)
         basis = leaf_basis.transpose(0, 1, 3, 2).reshape(512, 64)
         transfer = transfer.reshape(256, 32)
-        coupling = coupling.reshape(3840, 32)
-        x, message = call(
+        coupling = coupling.transpose(0, 2, 3, 1)
+        x, message, order, basis, transfer, coupling, near = call(
             upward_kernel,
-            (FAR_MEMORY,) * 4,
-            (jax.ShapeDtypeStruct((256, 128), BF), jax.ShapeDtypeStruct((OWN_ROWS, 128), BF)),
             (
-                pltpu.VMEM((32, 1024), BF),
-                pltpu.VMEM((8, 128), jnp.int32),
-                pltpu.VMEM((512, 64), BF),
-                pltpu.VMEM((256, 32), BF),
-                pltpu.SemaphoreType.DMA((4,)),
+                VMEM((256, 128), BF),
+                VMEM((OWN_ROWS, 128), BF),
+                VMEM((8, 128), jnp.int32),
+                VMEM((512, 64), BF),
+                VMEM((256, 32), BF),
+                VMEM((3, 32, 32, 40), BF),
+                VMEM((4, 4, 9, 64, 64), BF),
             ),
-        )(samples, order, basis, transfer)
+            (VMEM((32, 1024), BF), pltpu.SemaphoreType.DMA((6,))),
+            inputs=pltpu.HBM,
+        )(samples, order, basis, transfer, coupling, near_blocks)
         group = lax.all_gather(message, AXES, axis_index_groups=aligned)
-        send = call(cross_kernel, (VMEM,) * 2, jax.ShapeDtypeStruct((4, FAR_ROWS, 128), BF))(group, x)
+        send = call(cross_kernel, VMEM((4, FAR_ROWS, 128), BF))(group, x)
         cross = lax.all_to_all(send, AXES, 0, 0, axis_index_groups=shifted)
-        near_part, far = call(
+        coupling = coupling.transpose(0, 3, 1, 2).reshape(3840, 32)
+        near_part, far, leaf, pick = call(
             inner_kernel,
-            (VMEM, VMEM, FAR_MEMORY, VMEM),
-            (jax.ShapeDtypeStruct((256, 128), F32), jax.ShapeDtypeStruct((3, 224, 224), BF)),
-            (pltpu.VMEM((4, 4, 9, 64, 64), BF), pltpu.SemaphoreType.DMA((4,))),
+            (
+                VMEM((256, 128), F32),
+                VMEM((3, 224, 224), BF),
+                VMEM((256, 128), BF),
+                VMEM((1024, 1024), BF),
+            ),
             flops=10**9,
-        )(group, x, near_blocks, coupling)
+        )(group, x, near, coupling, basis, order)
         shared = lax.all_gather(cross[:, FAR_E2 : FAR_E2 + 32], AXES, axis_index_groups=aligned)
         out = call(
             downward_kernel(count_x, count_y),
-            (VMEM,) * 5 + (FAR_MEMORY,) * 4,
             jax.ShapeDtypeStruct((32, 1024), BF),
-            (
-                pltpu.VMEM((320, 256), BF),
-                pltpu.VMEM((256, 256), BF),
-                pltpu.VMEM((256, 256), BF),
-                pltpu.VMEM((4, 3, 64, 64), BF),
-                pltpu.VMEM((4, 9, 64, 64), BF),
-                pltpu.VMEM((512, 64), BF),
-                pltpu.VMEM((256, 32), BF),
-                pltpu.VMEM((8, 128), jnp.int32),
-                pltpu.SemaphoreType.DMA((5,)),
-            ),
-        )(group, near_part, far, cross, shared, near_blocks, basis, transfer, order)
+            (VMEM((320, 256), BF), VMEM((256, 256), BF), VMEM((256, 256), BF)),
+        )(group, near_part, far, leaf, pick, cross, shared, near, transfer)
         return out.T
 
     return jax.shard_map(

time: 50.6 us -> 50.4 us (level)
  Pallas kernels: 10.3 us -> 8.3 us
  local copies, waits for them, and re-layouts: 9.63 us -> 11.5 us
    transpose x0 -> x1, local copies, waits for them, and re-layouts: none -> 2.6 us  [local(): coupling = coupling.transpose(0, 3, 1, 2).reshape(3840, 32)]
    pallas_call x4, Pallas kernels: 10.3 us -> 8.3 us  [run(): pl.pallas_call(kernel, out_shape=shapes, in_specs=[pl.BlockSpec(memory_sp...]
    unnamed x27 -> x20, local copies, waits for them, and re-layouts: 9.62 us -> 8.89 us
  transfers between devices with their start and end apart: 1 -> 1, of which waited for: 0 -> 0; matrix products, arithmetic and copies ran while one was open for 5% -> 5% of each run, Pallas kernels for 6% -> 3%
where the time goes in v3:
time: 50.4 us; the launch traced here: 50.1 us
  blocking collectives  23 us (46%)
  local copies, waits for them, and re-layouts  11.5 us (23%)
  Pallas kernels  8.3 us (16%)
  starting transfers between devices  7.26 us (14%)
    all_gather x1, blocking collectives, local(): group = lax.all_gather(message, AXES, axis_index_groups=aligned)  12.7 us
    all_gather x1, blocking collectives, local(): lax.all_gather(cross[:, FAR_E2:FAR_E2 + 32], AXES, axis_index_groups=alig...  10.3 us
    unnamed x20, local copies, waits for them, and re-layouts  8.89 us
    pallas_call x4, Pallas kernels, run(): pl.pallas_call(kernel, out_shape=shapes, in_specs=[pl.BlockSpec(memory_sp...  8.3 us
    all_to_all x1, starting transfers between devices, local(): cross = lax.all_to_all(send, AXES, 0, 0, axis_index_groups=shifted)  7.26 us
    transpose x1, local copies, waits for them, and re-layouts, local(): coupling = coupling.transpose(0, 3, 1, 2).reshape(3840, 32)  2.6 us
  transfers between devices with their start and end apart: 1, of which 0 were waited for; matrix products, arithmetic and copies ran while one was open for 5% of the time, Pallas kernels for 3%

profile of v3, /device:TPU:1, one launch (start us, length us, event | category | flops | bytes accessed | tf_op | source)
XLA Modules:
  0.0 50.1 jit_solution(17452288508529062380)
XLA Ops:
  0.0 3.1 %shard_map.64 = (bf16[256,128]{1,0:T(8,128)(2,1)S(1)}, bf16[320,128]{1,0:T(8,128)(2,1)S(1)}, s32[8,128]{1,0:T(8,128)S(1)}, bf16[512,64]{1,0:T(8,128)(2,1)S(1)}, ...) custom-call(bf16[32,1024]{1,0:T(8,128)(2,1)} %bitcast.20, ...), custom_call_target="tpu_custom_call" | custom-call | flops 1000000 | bytes 1048576 | tf_op jit(solution)/shard_map/pallas_call | solution.py:423
  3.1 0.0 copy-start.3
  3.1 0.9 %copy-done.3 = bf16[3,32,32,40]{3,2,1,0:T(8,128)(2,1)} copy-done((bf16[3,32,32,40]{3,2,1,0:T(8,128)(2,1)}, bf16[3,32,32,40]{3,2,1,0:T(8,128)(2,1)S(1)}, u32[]{:S(2)}) %copy-start.3) | copy-done | bytes 245784
  4.0 0.0 copy-start.4
  4.0 0.6 %copy-done.4 = bf16[512,64]{1,0:T(8,128)(2,1)} copy-done((bf16[512,64]{1,0:T(8,128)(2,1)}, bf16[512,64]{1,0:T(8,128)(2,1)S(1)}, u32[]{:S(2)}) %copy-start.4) | copy-done | bytes 65560
  4.7 0.0 copy-start.6
  4.7 12.7 %all-gather = bf16[1280,128]{1,0:T(8,128)(2,1)S(1)} all-gather(bf16[320,128]{1,0:T(8,128)(2,1)S(1)} %get-tuple-element.16), channel_id=2, replica_groups={{0,1,32,33},{2,3,34,35},{4,5,36,37},{6,7,38,39},{8,9,40,41},{10,11,42,4..., dimensions={0}, use_global_device_ids=true | all-gather | bytes 409600 | tf_op jit(solution)/shard_map/all_gather | solution.py:472
  17.4 0.0 copy-done.6
  17.4 0.8 %shard_map.66 = bf16[4,288,128]{2,1,0:T(8,128)(2,1)} custom-call(bf16[4,320,128]{2,1,0:T(8,128)(2,1)S(1)} %bitcast.12, bf16[256,128]{1,0:T(8,128)(2,1)S(1)} %get-tuple-element.17.x), custom_call_target="tpu_custom_call" | custom-call | flops 1000000 | bytes 1048576 | tf_op jit(solution)/shard_map/pallas_call | solution.py:423
  18.2 7.3 %all-to-all-start = ((bf16[4,288,128]{2,1,0:T(8,128)(2,1)}), bf16[4,288,128]{2,1,0:T(8,128)(2,1)S(1)}, u32[]{:S(2)}, u32[]{:S(2)}) async-start(bf16[4,288,128]{2,1,0:T(8,128)(2,1)} %shard_map.66), calls=%async_computation | async-start | bytes 589824 | tf_op jit(solution)/shard_map/all_to_all | solution.py:474
  25.4 2.6 %copy.8 = bf16[3,40,32,32]{3,2,1,0:T(8,128)(2,1)} copy(bf16[3,40,32,32]{1,3,2,0:T(8,128)(2,1)} %bitcast.16) | data formatting | bytes 491520 | tf_op jit(solution)/shard_map/transpose | solution.py:475
  28.1 0.0 copy-start
  28.1 1.2 %copy-done = bf16[3,40,32,32]{3,2,1,0:T(8,128)(2,1)S(1)} copy-done((bf16[3,40,32,32]{3,2,1,0:T(8,128)(2,1)S(1)}, bf16[3,40,32,32]{3,2,1,0:T(8,128)(2,1)}, u32[]{:S(2)}) %copy-start) | copy-done | bytes 245784
  29.3 0.0 copy-start.5
  29.3 0.9 %copy-done.5 = bf16[512,64]{1,0:T(8,128)(2,1)S(1)} copy-done((bf16[512,64]{1,0:T(8,128)(2,1)S(1)}, bf16[512,64]{1,0:T(8,128)(2,1)}, u32[]{:S(2)}) %copy-start.5) | copy-done | bytes 65560
  30.2 1.3 %shard_map.65 = (f32[256,128]{1,0:T(8,128)S(1)}, bf16[3,224,224]{2,1,0:T(8,128)(2,1)S(1)}, bf16[256,128]{1,0:T(8,128)(2,1)S(1)}, bf16[1024,1024]{1,0:T(8,128)(2,1)S(1)}) custom-call(bf16[4,320,128]{2,1,0:T(8,128)(2,1)S(1)} %bitcast.13, bf16[256,128]{1,0:T(8,128)(2,1)S(1)} %get-tuple-element.17.x, bf16[4,4,9,64,64]{4,3,2,1,0:T(8,128)(2,1)S(1)} %get-tuple-element.18.near, ...), custom_call_target="tpu_custom_call" | custom-call | flops 1000000000 | bytes 1048576 | tf_op jit(solution)/shard_map/pallas_call | solution.py:423
  31.5 0.0 copy-start.1
  31.5 1.3 %copy-done.1 = bf16[1024,1024]{1,0:T(8,128)(2,1)} copy-done((bf16[1024,1024]{1,0:T(8,128)(2,1)}, bf16[1024,1024]{1,0:T(8,128)(2,1)S(1)}, u32[]{:S(2)}) %copy-start.1) | copy-done | bytes 2097176
  32.8 0.0 copy-start.8
  32.8 0.6 %copy-done.8 = bf16[256,128]{1,0:T(8,128)(2,1)} copy-done((bf16[256,128]{1,0:T(8,128)(2,1)}, bf16[256,128]{1,0:T(8,128)(2,1)S(1)}, u32[]{:S(2)}) %copy-start.8) | copy-done | bytes 65560
  33.4 0.0 all-to-all-done.cross
  33.4 10.3 %all-gather.1 = bf16[16,32,128]{2,1,0:T(8,128)(2,1)S(1)} all-gather(bf16[4,32,128]{2,1,0:T(8,128)(2,1)S(1)} %slice.4), channel_id=3, replica_groups={{0,1,32,33},{2,3,34,35},{4,5,36,37},{6,7,38,39},{8,9,40,41},{10,11,42,4..., dimensions={0}, use_global_device_ids=true | all-gather | bytes 163840 | tf_op jit(solution)/shard_map/all_gather | solution.py:486
  43.7 0.0 copy-start.2
  43.7 1.6 %copy-done.2 = bf16[1024,1024]{1,0:T(8,128)(2,1)S(1)} copy-done((bf16[1024,1024]{1,0:T(8,128)(2,1)S(1)}, bf16[1024,1024]{1,0:T(8,128)(2,1)}, u32[]{:S(2)}) %copy-start.2) | copy-done | bytes 2097176
  45.3 0.0 copy-start.7
  45.3 0.8 %copy-done.7 = bf16[256,32]{1,0:T(8,128)(2,1)S(1)} copy-done((bf16[256,32]{1,0:T(8,128)(2,1)S(1)}, bf16[256,32]{1,0:T(8,128)(2,1)}, u32[]{:S(2)}) %copy-start.7) | copy-done | bytes 16408
  46.2 0.0 copy-start.9
  46.2 0.8 %copy-done.9 = bf16[256,128]{1,0:T(8,128)(2,1)S(1)} copy-done((bf16[256,128]{1,0:T(8,128)(2,1)S(1)}, bf16[256,128]{1,0:T(8,128)(2,1)}, u32[]{:S(2)}) %copy-start.9) | copy-done | bytes 65560
  47.0 3.1 %shard_map.67 = bf16[32,1024]{1,0:T(8,128)(2,1)} custom-call(bf16[4,320,128]{2,1,0:T(8,128)(2,1)S(1)} %bitcast.14, f32[256,128]{1,0:T(8,128)S(1)} %get-tuple-element.22.near_part, bf16[3,224,224]{2,1,0:T(8,128)(2,1)S(1)} %get-tuple-element.23.far, bf16[256,128]{1,0:T(8,128)(2,1)S(1)} %copy-done.9, bf16[1024,1024]{1,0:T(8,128)(2,1)S(1)} %copy-done.2, ...), custom_call_target="tpu_custom_call" | custom-call | flops 1000000 | bytes 1048576 | tf_op jit(solution)/shard_map/pallas_call | solution.py:423
  (1 shorter events, 0.0 us)
Async XLA Ops:
  3.1 0.9 %copy-start.3 = (bf16[3,32,32,40]{3,2,1,0:T(8,128)(2,1)}, bf16[3,32,32,40]{3,2,1,0:T(8,128)(2,1)S(1)}, u32[]{:S(2)}) copy-start(bf16[3,32,32,40]{3,2,1,0:T(8,128)(2,1)S(1)} %get-tuple-element.19) | copy-start | bytes 737284
  4.0 0.6 %copy-start.4 = (bf16[512,64]{1,0:T(8,128)(2,1)}, bf16[512,64]{1,0:T(8,128)(2,1)S(1)}, u32[]{:S(2)}) copy-start(bf16[512,64]{1,0:T(8,128)(2,1)S(1)} %get-tuple-element.20.basis) | copy-start | bytes 196612
  4.7 12.7 %copy-start.6 = (bf16[256,32]{1,0:T(8,128)(2,1)}, bf16[256,32]{1,0:T(8,128)(2,1)S(1)}, u32[]{:S(2)}) copy-start(bf16[256,32]{1,0:T(8,128)(2,1)S(1)} %get-tuple-element.26.transfer) | copy-start | bytes 49156
  18.2 15.2 %all-to-all-start = ((bf16[4,288,128]{2,1,0:T(8,128)(2,1)}), bf16[4,288,128]{2,1,0:T(8,128)(2,1)S(1)}, u32[]{:S(2)}, u32[]{:S(2)}) async-start(bf16[4,288,128]{2,1,0:T(8,128)(2,1)} %shard_map.66), calls=%async_computation | async-start | bytes 589824 | tf_op jit(solution)/shard_map/all_to_all | solution.py:474
  28.1 1.2 %copy-start = (bf16[3,40,32,32]{3,2,1,0:T(8,128)(2,1)S(1)}, bf16[3,40,32,32]{3,2,1,0:T(8,128)(2,1)}, u32[]{:S(2)}) copy-start(bf16[3,40,32,32]{3,2,1,0:T(8,128)(2,1)} %copy.8) | copy-start | bytes 737284
  29.3 0.9 %copy-start.5 = (bf16[512,64]{1,0:T(8,128)(2,1)S(1)}, bf16[512,64]{1,0:T(8,128)(2,1)}, u32[]{:S(2)}) copy-start(bf16[512,64]{1,0:T(8,128)(2,1)} %copy-done.4) | copy-start | bytes 196612
  31.5 1.3 %copy-start.1 = (bf16[1024,1024]{1,0:T(8,128)(2,1)}, bf16[1024,1024]{1,0:T(8,128)(2,1)S(1)}, u32[]{:S(2)}) copy-start(bf16[1024,1024]{1,0:T(8,128)(2,1)S(1)} %get-tuple-element.25.pick) | copy-start | bytes 6291460
  32.8 0.6 %copy-start.8 = (bf16[256,128]{1,0:T(8,128)(2,1)}, bf16[256,128]{1,0:T(8,128)(2,1)S(1)}, u32[]{:S(2)}) copy-start(bf16[256,128]{1,0:T(8,128)(2,1)S(1)} %get-tuple-element.24.leaf) | copy-start | bytes 196612
  43.7 1.6 %copy-start.2 = (bf16[1024,1024]{1,0:T(8,128)(2,1)S(1)}, bf16[1024,1024]{1,0:T(8,128)(2,1)}, u32[]{:S(2)}) copy-start(bf16[1024,1024]{1,0:T(8,128)(2,1)} %copy-done.1) | copy-start | bytes 6291460
  45.3 0.8 %copy-start.7 = (bf16[256,32]{1,0:T(8,128)(2,1)S(1)}, bf16[256,32]{1,0:T(8,128)(2,1)}, u32[]{:S(2)}) copy-start(bf16[256,32]{1,0:T(8,128)(2,1)} %copy-done.6) | copy-start | bytes 49156
  46.2 0.8 %copy-start.9 = (bf16[256,128]{1,0:T(8,128)(2,1)S(1)}, bf16[256,128]{1,0:T(8,128)(2,1)}, u32[]{:S(2)}) copy-start(bf16[256,128]{1,0:T(8,128)(2,1)} %copy-done.8) | copy-start | bytes 196612

commit v4 on v3

--- a/solution.py
+++ b/solution.py
@@ -1,3 +1,5 @@
+import functools
+
 import jax
 import jax.numpy as jnp
 from jax import lax
@@ -9,7 +11,7 @@
 F32 = jnp.float32
 AXES = ("gx", "gy")
 VMEM_BYTES = 32 * 1024 * 1024
-VMEM = pltpu.VMEM
+VMEM, HBM = pltpu.VMEM, pltpu.HBM
 
 OWN_ROW, OWN_COL, OWN_E0, OWN_E1, OWN_E2, OWN_ROWS = 0, 64, 128, 256, 288, 320
 FAR_X, FAR_E0, FAR_CORNER, FAR_E1, FAR_E1_SIDE, FAR_E2, FAR_ROWS = 0, 64, 128, 192, 224, 256, 288
@@ -48,6 +50,14 @@
 def place():
     gx, gy = lax.axis_index("gx"), lax.axis_index("gy")
     return gx, gy, lax.rem(gx, 2), lax.rem(gy, 2)
+
+
+def swap_of(gx, gy, count_x, count_y):
+    end_x = (gx == 0) | (gx == count_x - 1)
+    end_y = (gy == 0) | (gy == count_y - 1)
+    along_y = jnp.where(lax.rem(gy + 3, 4) >= 2, 2, 0)
+    along_x = jnp.where(lax.rem(gx + 3, 4) >= 2, 1, 0)
+    return jnp.where(end_x & ~end_y, along_y, jnp.where(end_y & ~end_x, along_x, 0))
 
 
 def merge_diagonal(blocks, height):
@@ -69,13 +79,10 @@
 
 
 def upward_kernel(
-    samples_hbm, order_hbm, basis_hbm, transfer_hbm, coupling_hbm, near_hbm,
-    x_out, msg, order, basis, transfer, coupling, near, samples, sems,
+    samples_hbm, order_hbm, basis_hbm, transfer_hbm, x_out, msg, order, samples, basis, transfer, sems
 ):
     copies = fetch(
-        (order_hbm, samples_hbm, basis_hbm, transfer_hbm, coupling_hbm, near_hbm),
-        (order, samples, basis, transfer, coupling, near),
-        sems,
+        (order_hbm, samples_hbm, basis_hbm, transfer_hbm), (order, samples, basis, transfer), sems
     )
     _, _, pi, pj = place()
     copies[0].wait()
@@ -128,12 +135,11 @@
     e2 = e2 + roll(e2, 64)
     e2 = e2 + roll(e2, 32)
     msg[OWN_E2 : OWN_E2 + 32, :] = jnp.where(slot == 2 * pi + pj, e2, 0.0).astype(BF)
-    copies[4].wait()
-    copies[5].wait()
-
-
-def cross_kernel(group, x, send):
-    _, _, pi, pj = place()
+
+
+def cross_kernel(group, x, send, *, count_x, count_y):
+    gx, gy, pi, pj = place()
+    swap = swap_of(gx, gy, count_x, count_y)
     me, across_x, across_y = 2 * pi + pj, 2 * (1 - pi) + pj, 2 * pi + 1 - pj
     lane, slot = lane_of(64), slot_of(64)
     near_half = (lane < 64) == (pj == 0)
@@ -148,7 +154,7 @@
         send[m, FAR_E2 : FAR_E2 + 32, :] = e2
         send[m, FAR_E1 : FAR_E1 + 32, :] = e1
 
-    to = 2 * pi + 1 - pj
+    to = (2 * pi + 1 - pj) ^ swap
     send[to, FAR_X : FAR_X + 64, :] = x_row
     send[to, FAR_E0 : FAR_E0 + 64, :] = e0_rows
     column = group[across_y, OWN_COL : OWN_COL + 64, :]
@@ -157,7 +163,7 @@
     send[to, FAR_CORNER : FAR_CORNER + 64, :] = jnp.where(near_half, corner_e0, column)
     send[to, FAR_E1_SIDE : FAR_E1_SIDE + 32, :] = group[across_y, OWN_E1 : OWN_E1 + 32, :]
 
-    to = 2 * (1 - pi) + pj
+    to = (2 * (1 - pi) + pj) ^ swap
     column_slot = jnp.where(pj == 0, 0, 3)
     packed = jnp.zeros((64, 128), BF)
     for a in range(4):
@@ -170,13 +176,13 @@
     send[to, FAR_CORNER : FAR_CORNER + 64, :] = jnp.where(near_half, corner_e0, corner_x)
     send[to, FAR_E1_SIDE : FAR_E1_SIDE + 32, :] = group[across_x, OWN_E1 : OWN_E1 + 32, :]
 
-    to = 2 * pi + pj
+    to = (2 * pi + pj) ^ swap
     send[to, FAR_X : FAR_X + 64, :] = jnp.zeros((64, 128), BF)
     send[to, FAR_E0 : FAR_E0 + 64, :] = jnp.zeros((64, 128), BF)
     send[to, FAR_CORNER : FAR_CORNER + 64, :] = jnp.where(near_half, e0_rows, roll(x_row, 64))
     send[to, FAR_E1_SIDE : FAR_E1_SIDE + 32, :] = jnp.zeros((32, 128), BF)
 
-    to = 2 * (1 - pi) + 1 - pj
+    to = (2 * (1 - pi) + 1 - pj) ^ swap
     send[to, 0:FAR_E1, :] = jnp.zeros((FAR_E1, 128), BF)
     send[to, FAR_E1_SIDE : FAR_E1_SIDE + 32, :] = jnp.zeros((32, 128), BF)
 
@@ -210,21 +216,61 @@
     return out
 
 
-def inner_kernel(group, x, near, coupling, basis, order, near_out, far, leaf, pick):
+def turn_coupling(coupling, turned, far):
+    row = lax.broadcasted_iota(jnp.int32, (56, 40), 0)
+    number = lane_of(56, 40)
+    u, w = row // 8 - 3, row % 8 - 3
+    outer = (abs(u) >= 2) & (w <= 3)
+    inner = (abs(u) < 2) & (abs(w) >= 2) & (w <= 3)
+    index = jnp.where(u < -1, (u + 3) * 7 + w + 3, 26 + (u - 2) * 7 + w + 3)
+    index = jnp.where(abs(u) < 2, 14 + (u + 1) * 4 + jnp.where(w < 0, w + 3, w), index)
+    choose = jnp.where((outer | inner) & (number == index), 1.0, 0.0).astype(BF)
+    slot = slot_of(8)
+    for level in range(3):
+        for block in range(8):
+            lines = coupling[level, 4 * block : 4 * block + 4].reshape(128, 40)
+            part = dot_nt(choose, lines)
+            moved = [part] + [pltpu.roll(part, 32 * q, 1) for q in range(1, 4)]
+            for q in range(4):
+                i = 4 * block + q
+                for half in range(2):
+                    out = jnp.zeros((8, 128), F32)
+                    for u in range(4 * half, min(4 * half + 4, 7)):
+                        piece = moved[(u - q) % 4][8 * u : 8 * u + 8]
+                        out = jnp.where(slot == u % 4, piece, out)
+                    turned[half][pl.ds(i, 8, stride=32), :] = out
+        for half in range(2):
+            lines = turned[half][0:224, :].astype(BF)
+            far[level, :, 128 * half : 128 * half + 128] = lines
+
+
+def inner_kernel(
+    group, x, near_hbm, coupling_hbm, basis_hbm, order_hbm,
+    near_out, far, leaf_hbm, pick_hbm,
+    near, coupling, basis, order, turned_low, turned_high, leaf, pick, sems,
+):
+    copies = fetch(
+        [order_hbm, basis_hbm, coupling_hbm] + [near_hbm.at[a] for a in range(4)],
+        [order, basis, coupling] + [near.at[a] for a in range(4)],
+        sems,
+    )
     _, _, pi, pj = place()
     across_x, across_y, across = 2 * (1 - pi) + pj, 2 * pi + 1 - pj, 2 * (1 - pi) + 1 - pj
-    far[...] = jnp.zeros(far.shape, BF)
-    for level in range(3):
-        n = 0
-        for u in range(-3, 4):
-            for w in range(-3, 4):
-                if max(abs(u), abs(w)) >= 2:
-                    start = (level * 40 + n) * 32
-                    far[level, (w + 3) * 32 : (w + 4) * 32, (u + 3) * 32 : (u + 4) * 32] = (
-                        coupling[start : start + 32, :]
-                    )
-                    n += 1
-
+    copies[0].wait()
+    line = jnp.concatenate([order[g : g + 1, :] for g in range(8)], axis=1)
+    for t in range(8):
+        site = lax.broadcasted_iota(jnp.int32, (128, 1024), 0) + 128 * t
+        pick[128 * t : 128 * (t + 1), :] = jnp.where(site == line, 1.0, 0.0).astype(BF)
+    pick_copy = pltpu.make_async_copy(pick, pick_hbm, sems.at[7])
+    pick_copy.start()
+    copies[1].wait()
+    for a in range(4):
+        flat = jnp.transpose(basis[a * 128 : (a + 1) * 128, :].astype(F32))
+        leaf[a * 64 : (a + 1) * 64, :] = flat.astype(BF)
+    leaf_copy = pltpu.make_async_copy(leaf, leaf_hbm, sems.at[8])
+    leaf_copy.start()
+    copies[2].wait()
+    turn_coupling(coupling, (turned_low, turned_high), far)
 
     slot = slot_of(64)
     windows = {}
@@ -245,27 +291,38 @@
     store_windows(-1, jnp.where(pi == 0, nothing, middle), jnp.where(pi == 0, nothing, inner))
     store_windows(4, jnp.where(pi == 0, middle, nothing), jnp.where(pi == 0, inner, nothing))
     for a in range(4):
+        copies[3 + a].wait()
         total = jnp.zeros((256, 128), F32)
         for n in range(9):
             matrix = near[a, :, n].reshape(256, 64)
             total = total + dot(matrix, windows[a + n // 3 - 1, n % 3 - 1])
         near_out[a * 64 : (a + 1) * 64, :] = merge_diagonal(total, 64)
-        turned = jnp.transpose(basis[a * 128 : (a + 1) * 128, :].astype(F32))
-        leaf[a * 64 : (a + 1) * 64, :] = turned.astype(BF)
-    line = jnp.concatenate([order[g : g + 1, :] for g in range(8)], axis=1)
-    for t in range(8):
-        site = lax.broadcasted_iota(jnp.int32, (128, 1024), 0) + 128 * t
-        pick[128 * t : 128 * (t + 1), :] = jnp.where(site == line, 1.0, 0.0).astype(BF)
+    pick_copy.wait()
+    leaf_copy.wait()
 
 
 def downward_kernel(count_x, count_y):
     def body(
-        group, near_part, far, leaf, pick, cross, shared, near, transfer, out, h0, h1, h2
+        group, near_part, far, cross, shared, transfer_hbm, near_hbm, leaf_hbm, pick_hbm, out,
+        h0, h1, h2, transfer, near_row, near_col, leaf, pick, sems,
     ):
         gx, gy, pi, pj = place()
+        copies = fetch(
+            (
+                transfer_hbm,
+                near_hbm.at[3 * pi, :, pl.ds(6 * pi, 3)],
+                near_hbm.at[:, 3 * pj],
+                leaf_hbm,
+                pick_hbm,
+            ),
+            (transfer, near_row, near_col, leaf, pick),
+            sems,
+        )
+        swap = swap_of(gx, gy, count_x, count_y)
         me, across_x, across_y = 2 * pi + pj, 2 * (1 - pi) + pj, 2 * pi + 1 - pj
         across = 2 * (1 - pi) + 1 - pj
-        from_x, from_y, from_xy = 2 * pi + 1 - pj, 2 * (1 - pi) + pj, 2 * pi + pj
+        from_x, from_y = (2 * pi + 1 - pj) ^ swap, (2 * (1 - pi) + pj) ^ swap
+        from_xy = (2 * pi + pj) ^ swap
         has_x = jnp.where(pi == 0, gx > 0, gx < count_x - 1)
         has_y = jnp.where(pj == 0, gy > 0, gy < count_y - 1)
         has_xy = has_x & has_y
@@ -328,31 +385,29 @@
         e2 = group[0, OWN_E2:OWN_ROWS, :]
         for m in range(1, 4):
             e2 = e2 + group[m, OWN_E2:OWN_ROWS, :]
+
+        def brought(m, slot, keep):
+            other = swap_of(gx - pi + m // 2, gy - pj + m % 2, count_x, count_y)
+            return kept(keep, shared[m, slot ^ other])
+
         store_row_of_tiles(
-            h2,
-            32,
-            kept(above & before, shared[0, 0]),
-            kept(above, shared[0, 1]),
-            kept(above & after, shared[1, 1]),
-        )
-        store_row_of_tiles(h2, 96, kept(before, shared[0, 2]), e2, kept(after, shared[1, 3]))
+            h2, 32, brought(0, 0, above & before), brought(0, 1, above), brought(1, 1, above & after)
+        )
+        store_row_of_tiles(h2, 96, brought(0, 2, before), e2, brought(1, 3, after))
         store_row_of_tiles(
-            h2,
-            160,
-            kept(below & before, shared[2, 2]),
-            kept(below, shared[2, 3]),
-            kept(below & after, shared[3, 3]),
+            h2, 160, brought(2, 2, below & before), brought(2, 3, below), brought(3, 3, below & after)
         )
 
         slot = slot_of(32)
-        local2 = far_row(far[2], h2[pl.ds(32 * pi, 224), :], pi)
+        local2 = far_row(far[2, :, :224], h2[pl.ds(32 * pi, 224), :], pi)
         local2 = jnp.where(slot == pj, local2, 0.0)
         local2 = local2 + roll(local2, 64)
         local2 = (local2 + roll(local2, 32)).astype(BF)
+        copies[0].wait()
         spread = dot(transfer[128:256, :], local2)
         local1 = []
         for i in range(2):
-            down = far_row(far[1], h1[32 * i : 32 * i + 224, :], i)
+            down = far_row(far[1, :, :224], h1[32 * i : 32 * i + 224, :], i)
             for j in range(2):
                 n = 2 * i + j
                 down = down + jnp.where(slot == j, spread[n * 32 : (n + 1) * 32], 0.0)
@@ -362,12 +417,14 @@
         local0 = []
         for i in range(4):
             spread = dot(transfer[64 * (i % 2) : 64 * (i % 2) + 64, :], local1[i // 2])
-            down = far_row(far[0], h0[32 * i : 32 * i + 224, :], i % 2)
+            down = far_row(far[0, :, :224], h0[32 * i : 32 * i + 224, :], i % 2)
             down = down + jnp.where(lax.rem(slot, 2) == 0, spread[:32], spread[32:])
             local0.append(down.astype(BF))
 
 
         slot = slot_of(64)
+        copies[1].wait()
+        copies[2].wait()
         column = kept(has_y, cross[from_y, FAR_X : FAR_X + 64, :])
         corner_in = kept(has_y, roll(cross[from_y, FAR_CORNER : FAR_CORNER + 64, :], 64))
         corner_out = kept(has_xy, roll(cross[from_xy, FAR_CORNER : FAR_CORNER + 64, :], 64))
@@ -390,13 +447,14 @@
         )
         beyond = jnp.zeros((256, 128), F32)
         for c in range(3):
-            beyond = beyond + dot(near[3 * pi, :, 6 * pi + c].reshape(256, 64), shifts[c])
+            beyond = beyond + dot(near_row[:, c].reshape(256, 64), shifts[c])
         beyond = merge_diagonal(beyond, 64)
 
         row = lax.broadcasted_iota(jnp.int32, (256, 128), 0)
         diagonal = row // 64 == slot_of(256)
         block = lax.broadcasted_iota(jnp.int32, (128, 128), 0) // 32 == slot_of(128)
         leaves = []
+        copies[3].wait()
         for a in range(4):
             total = near_part[a * 64 : (a + 1) * 64, :]
             if a == 0:
@@ -404,12 +462,13 @@
             if a == 3:
                 total = total + jnp.where(pi == 0, 0.0, beyond)
             for r in range(3):
-                total = total + dot(near[a, 3 * pj, 3 * r + 2 * pj], boxes[a + r - 1])
+                total = total + dot(near_col[a, 3 * r + 2 * pj], boxes[a + r - 1])
             local = jnp.concatenate([local0[a]] * 4, axis=0)
             total = total + dot(leaf[a * 64 : (a + 1) * 64, :], jnp.where(block, local, jnp.zeros_like(local)))
             total = jnp.concatenate([total] * 4, axis=0)
             leaves.append(jnp.where(diagonal, total, 0.0).astype(BF))
         leaves = jnp.concatenate(leaves, axis=0)
+        copies[4].wait()
         for t in range(8):
             done = jnp.transpose(dot(pick[128 * t : 128 * (t + 1), :], leaves))
             done = (done[:32] + done[32:64]) + (done[64:96] + done[96:])
@@ -418,36 +477,55 @@
     return body
 
 
-def call(kernel, shapes, scratch=(), inputs=VMEM, flops=10**6):
+def call(kernel, spaces, shapes, scratch=(), flops=10**6):
     def run(*args):
         return pl.pallas_call(
             kernel,
             out_shape=shapes,
-            in_specs=[pl.BlockSpec(memory_space=inputs)] * len(args),
+            in_specs=[pl.BlockSpec(memory_space=space) for space in spaces],
+            out_specs=jax.tree.map(lambda shape: pl.BlockSpec(memory_space=shape.memory_space), shapes),
             scratch_shapes=list(scratch),
             cost_estimate=pl.CostEstimate(flops=flops, bytes_accessed=2**20, transcendentals=0),
             compiler_params=pltpu.CompilerParams(vmem_limit_bytes=VMEM_BYTES),
-        )(*[pltpu.with_memory_space_constraint(arg, inputs) for arg in args])
+        )(*map(pltpu.with_memory_space_constraint, args, spaces))
 
     return run
 
 
-def groups_of_four(count_x, count_y, offset):
+def aligned_groups(count_x, count_y):
     return [
-        [
-            ((i + di) % count_x) * count_y + (j + dj) % count_y
-            for di in range(2)
-            for dj in range(2)
-        ]
-        for i in range(offset, count_x + offset, 2)
-        for j in range(offset, count_y + offset, 2)
+        [(i + di) * count_y + j + dj for di in range(2) for dj in range(2)]
+        for i in range(0, count_x, 2)
+        for j in range(0, count_y, 2)
     ]
+
+
+def shifted_groups(count_x, count_y):
+    last_x, last_y = count_x - 1, count_y - 1
+    groups = [
+        [(i, j), (i, j + 1), (i + 1, j), (i + 1, j + 1)]
+        for i in range(1, last_x, 2)
+        for j in range(1, last_y, 2)
+    ]
+    for i in (0, last_x):
+        for j in range(1, last_y, 4):
+            second = [(i, j + 2), (i, j + 3)] if j + 3 < last_y else [(i, last_y), (i, 0)]
+            first = [(i, j), (i, j + 1)]
+            groups.append(second + first if i == 0 else first + second)
+    for i in range(1, last_x, 4):
+        if i + 3 < last_x:
+            for j in (0, last_y):
+                lanes = (i + 2, i) if j == 0 else (i, i + 2)
+                groups.append([(g + d, j) for d in range(2) for g in lanes])
+        else:
+            groups.append([(i + d, j) for d in range(2) for j in (last_y, 0)])
+    return [[i * count_y + j for i, j in group] for group in groups]
 
 
 def solution(mesh):
     count_x, count_y = mesh.shape["gx"], mesh.shape["gy"]
-    aligned = groups_of_four(count_x, count_y, 0)
-    shifted = groups_of_four(count_x, count_y, 1)
+    aligned = aligned_groups(count_x, count_y)
+    shifted = shifted_groups(count_x, count_y)
 
     def local(samples, site_order, leaf_basis, near_blocks, transfer, coupling):
         samples = samples.T
@@ -455,40 +533,61 @@
         basis = leaf_basis.transpose(0, 1, 3, 2).reshape(512, 64)
         transfer = transfer.reshape(256, 32)
         coupling = coupling.transpose(0, 2, 3, 1)
-        x, message, order, basis, transfer, coupling, near = call(
+        x, message = call(
             upward_kernel,
+            (HBM,) * 4,
+            (VMEM((256, 128), BF), VMEM((OWN_ROWS, 128), BF)),
             (
-                VMEM((256, 128), BF),
-                VMEM((OWN_ROWS, 128), BF),
                 VMEM((8, 128), jnp.int32),
+                VMEM((32, 1024), BF),
                 VMEM((512, 64), BF),
                 VMEM((256, 32), BF),
-                VMEM((3, 32, 32, 40), BF),
-                VMEM((4, 4, 9, 64, 64), BF),
+                pltpu.SemaphoreType.DMA((4,)),
             ),
-            (VMEM((32, 1024), BF), pltpu.SemaphoreType.DMA((6,))),
-            inputs=pltpu.HBM,
-        )(samples, order, basis, transfer, coupling, near_blocks)
+        )(samples, order, basis, transfer)
         group = lax.all_gather(message, AXES, axis_index_groups=aligned)
-        send = call(cross_kernel, VMEM((4, FAR_ROWS, 128), BF))(group, x)
+        cross_body = functools.partial(cross_kernel, count_x=count_x, count_y=count_y)
+        send = call(cross_body, (VMEM,) * 2, VMEM((4, FAR_ROWS, 128), BF))(group, x)
         cross = lax.all_to_all(send, AXES, 0, 0, axis_index_groups=shifted)
-        coupling = coupling.transpose(0, 3, 1, 2).reshape(3840, 32)
         near_part, far, leaf, pick = call(
             inner_kernel,
+            (VMEM,) * 2 + (HBM,) * 4,
             (
                 VMEM((256, 128), F32),
-                VMEM((3, 224, 224), BF),
+                VMEM((3, 224, 256), BF),
+                HBM((256, 128), BF),
+                HBM((1024, 1024), BF),
+            ),
+            (
+                VMEM((4, 4, 9, 64, 64), BF),
+                VMEM((3, 32, 32, 40), BF),
+                VMEM((512, 64), BF),
+                VMEM((8, 128), jnp.int32),
+                VMEM((256, 128), F32),
+                VMEM((256, 128), F32),
                 VMEM((256, 128), BF),
                 VMEM((1024, 1024), BF),
+                pltpu.SemaphoreType.DMA((9,)),
             ),
             flops=10**9,
-        )(group, x, near, coupling, basis, order)
+        )(group, x, near_blocks, coupling, basis, order)
         shared = lax.all_gather(cross[:, FAR_E2 : FAR_E2 + 32], AXES, axis_index_groups=aligned)
         out = call(
             downward_kernel(count_x, count_y),
-            jax.ShapeDtypeStruct((32, 1024), BF),
-            (VMEM((320, 256), BF), VMEM((256, 256), BF), VMEM((256, 256), BF)),
-        )(group, near_part, far, leaf, pick, cross, shared, near, transfer)
+            (VMEM,) * 5 + (HBM,) * 4,
+            VMEM((32, 1024), BF),
+            (
+                VMEM((320, 256), BF),
+                VMEM((256, 256), BF),
+                VMEM((256, 256), BF),
+                VMEM((256, 32), BF),
+                VMEM((4, 3, 64, 64), BF),
+                VMEM((4, 9, 64, 64), BF),
+                VMEM((256, 128), BF),
+                VMEM((1024, 1024), BF),
+                pltpu.SemaphoreType.DMA((5,)),
+            ),
+        )(group, near_part, far, cross, shared, transfer, near_blocks, leaf, pick)
         return out.T
 
     return jax.shard_map(

time: 50.4 us -> 37.2 us (0.74)
  local copies, waits for them, and re-layouts: 11.5 us -> 0.64 us
  starting transfers between devices: 7.26 us -> 3.44 us
  Pallas kernels: 8.3 us -> 11.8 us
  blocking collectives: 23 us -> 21 us
    unnamed x20 -> x1, local copies, waits for them, and re-layouts: 8.89 us -> 0.63 us
    all_to_all x1, starting transfers between devices: 7.26 us -> 3.44 us  [local(): cross = lax.all_to_all(send, AXES, 0, 0, axis_index_groups=shifted)]
    pallas_call x4, Pallas kernels: 8.3 us -> 11.8 us  [run(): pl.pallas_call(kernel, out_shape=shapes, in_specs=[pl.BlockSpec(memory_sp...]
    transpose x1 -> x0, local copies, waits for them, and re-layouts: 2.6 us -> none  [local(): coupling = coupling.transpose(0, 3, 1, 2).reshape(3840, 32)]
    all_gather x1, blocking collectives: 10.3 us -> 8.3 us  [local(): lax.all_gather(cross[:, FAR_E2:FAR_E2 + 32], AXES, axis_index_groups=alig...]
  transfers between devices with their start and end apart: 1 -> 1, of which waited for: 0 -> 0; matrix products, arithmetic and copies ran while one was open for 5% -> 0% of each run, Pallas kernels for 3% -> 12%
where the time goes in v4:
time: 37.2 us; the launch traced here: 36.9 us
  blocking collectives  21 us (56%)
  Pallas kernels  11.8 us (32%)
  starting transfers between devices  3.44 us (9%)
  local copies, waits for them, and re-layouts  0.64 us (2%)
    all_gather x1, blocking collectives, local(): group = lax.all_gather(message, AXES, axis_index_groups=aligned)  12.7 us
    pallas_call x4, Pallas kernels, run(): pl.pallas_call(kernel, out_shape=shapes, in_specs=[pl.BlockSpec(memory_sp...  11.8 us
    all_gather x1, blocking collectives, local(): lax.all_gather(cross[:, FAR_E2:FAR_E2 + 32], AXES, axis_index_groups=alig...  8.3 us
    all_to_all x1, starting transfers between devices, local(): cross = lax.all_to_all(send, AXES, 0, 0, axis_index_groups=shifted)  3.44 us
  transfers between devices with their start and end apart: 1, of which 0 were waited for; matrix products, arithmetic and copies ran while one was open for 0% of the time, Pallas kernels for 12%

profile of v4, /device:TPU:1, one launch (start us, length us, event | category | flops | bytes accessed | tf_op | source)
XLA Modules:
  0.0 36.9 jit_solution(14135158319483296817)
XLA Ops:
  0.0 3.1 %shard_map.64 = (bf16[256,128]{1,0:T(8,128)(2,1)S(1)}, bf16[320,128]{1,0:T(8,128)(2,1)S(1)}) custom-call(bf16[32,1024]{1,0:T(8,128)(2,1)} %bitcast.19, s32[8,128]{1,0:T(8,128)} %bitcast.20, bf16[512,64]{1,0:T(8,128)(2,1)} %bitcast.17, bf16[256,32]{1,0:T(8,128)(2,1)} %bitcast.15), custom_call_target="tpu_custom_call" | custom-call | flops 1000000 | bytes 1048576 | tf_op jit(solution)/shard_map/pallas_call | solution.py:482
  3.1 12.7 %all-gather = bf16[1280,128]{1,0:T(8,128)(2,1)S(1)} all-gather(bf16[320,128]{1,0:T(8,128)(2,1)S(1)} %get-tuple-element.11), channel_id=2, replica_groups={{0,1,32,33},{2,3,34,35},{4,5,36,37},{6,7,38,39},{8,9,40,41},{10,11,42,4..., dimensions={0}, use_global_device_ids=true | all-gather | bytes 409600 | tf_op jit(solution)/shard_map/all_gather | solution.py:548
  15.8 0.8 %shard_map.66 = bf16[4,288,128]{2,1,0:T(8,128)(2,1)} custom-call(bf16[4,320,128]{2,1,0:T(8,128)(2,1)S(1)} %bitcast.11, bf16[256,128]{1,0:T(8,128)(2,1)S(1)} %get-tuple-element.12.x), custom_call_target="tpu_custom_call" | custom-call | flops 1000000 | bytes 1048576 | tf_op jit(solution)/shard_map/pallas_call | solution.py:482
  16.6 3.4 %all-to-all-start = ((bf16[4,288,128]{2,1,0:T(8,128)(2,1)}), bf16[4,288,128]{2,1,0:T(8,128)(2,1)S(1)}, u32[]{:S(2)}, u32[]{:S(2)}) async-start(bf16[4,288,128]{2,1,0:T(8,128)(2,1)} %shard_map.66), calls=%async_computation | async-start | bytes 589824 | tf_op jit(solution)/shard_map/all_to_all | solution.py:551
  20.1 4.3 %shard_map.65 = (f32[256,128]{1,0:T(8,128)S(1)}, bf16[3,224,256]{2,1,0:T(8,128)(2,1)S(1)}, bf16[256,128]{1,0:T(8,128)(2,1)}, bf16[1024,1024]{1,0:T(8,128)(2,1)}) custom-call(bf16[4,320,128]{2,1,0:T(8,128)(2,1)S(1)} %bitcast.12, bf16[256,128]{1,0:T(8,128)(2,1)S(1)} %get-tuple-element.12.x, bf16[4,4,9,64,64]{4,3,2,1,0:T(8,128)(2,1)} %near_hbm.3, ...), custom_call_target="tpu_custom_call" | custom-call | flops 1000000000 | bytes 1048576 | tf_op jit(solution)/shard_map/pallas_call | solution.py:482
  24.3 0.0 all-to-all-done.cross
  24.4 8.3 %all-gather.1 = bf16[16,32,128]{2,1,0:T(8,128)(2,1)S(1)} all-gather(bf16[4,32,128]{2,1,0:T(8,128)(2,1)S(1)} %slice.4), channel_id=3, replica_groups={{0,1,32,33},{2,3,34,35},{4,5,36,37},{6,7,38,39},{8,9,40,41},{10,11,42,4..., dimensions={0}, use_global_device_ids=true | all-gather | bytes 163840 | tf_op jit(solution)/shard_map/all_gather | solution.py:574
  32.7 3.6 %shard_map.67 = bf16[32,1024]{1,0:T(8,128)(2,1)S(1)} custom-call(bf16[4,320,128]{2,1,0:T(8,128)(2,1)S(1)} %bitcast.13, f32[256,128]{1,0:T(8,128)S(1)} %get-tuple-element.13.near_part, bf16[3,224,256]{2,1,0:T(8,128)(2,1)S(1)} %get-tuple-element.14.far, bf16[4,288,128]{2,1,0:T(8,128)(2,1)S(1)} %all-to-all-done.cross, bf16[4,4,32,128]{3,2,1,0:T(8,128)(2,1)S(1)} %bitcast.14, ...), custom_call_target="tpu_custom_call" | custom-call | flops 1000000 | bytes 1048576 | tf_op jit(solution)/shard_map/pallas_call | solution.py:482
  36.3 0.6 %copy.7 = bf16[1024,32]{0,1:T(8,128)(2,1)} copy(bf16[1024,32]{0,1:T(8,128)(2,1)S(1)} %bitcast.10) | data formatting | bytes 131072
  (1 shorter events, 0.0 us)
Async XLA Ops:
  16.6 7.7 %all-to-all-start = ((bf16[4,288,128]{2,1,0:T(8,128)(2,1)}), bf16[4,288,128]{2,1,0:T(8,128)(2,1)S(1)}, u32[]{:S(2)}, u32[]{:S(2)}) async-start(bf16[4,288,128]{2,1,0:T(8,128)(2,1)} %shard_map.66), calls=%async_computation | async-start | bytes 589824 | tf_op jit(solution)/shard_map/all_to_all | solution.py:551

commit v5 on v4

--- a/solution.py
+++ b/solution.py
@@ -55,7 +55,7 @@
 def swap_of(gx, gy, count_x, count_y):
     end_x = (gx == 0) | (gx == count_x - 1)
     end_y = (gy == 0) | (gy == count_y - 1)
-    along_y = jnp.where(lax.rem(gy + 3, 4) >= 2, 2, 0)
+    along_y = jnp.where((lax.rem(gy + 3, 4) < 2) & (gy > 2), 2, 0)
     along_x = jnp.where(lax.rem(gx + 3, 4) >= 2, 1, 0)
     return jnp.where(end_x & ~end_y, along_y, jnp.where(end_y & ~end_x, along_x, 0))
 
@@ -66,6 +66,26 @@
     for b in range(4):
         out = jnp.where(slot == b, blocks[b * height : (b + 1) * height], out)
     return out
+
+
+def split_order(order):
+    lane = lane_of(1)
+    lines = []
+    for pair in range(2):
+        for b in range(4):
+            low = order[4 * pair + b // 2 : 4 * pair + b // 2 + 1, :]
+            high = order[4 * pair + 2 + b // 2 : 4 * pair + 3 + b // 2, :]
+            if b % 2 == 0:
+                lines.append(jnp.where(lane < 64, low, pltpu.roll(high, 64, 1)))
+            else:
+                lines.append(jnp.where(lane < 64, pltpu.roll(low, 64, 1), high))
+    lines = jnp.concatenate(lines, axis=0)
+    return lines // 128, lines % 128
+
+
+def pick_sites(within):
+    row = lax.broadcasted_iota(jnp.int32, (128, 128), 0)
+    return jnp.where(within == row, 1.0, 0.0).astype(BF)
 
 
 def fetch(sources, targets, sems):
@@ -86,29 +106,30 @@
     )
     _, _, pi, pj = place()
     copies[0].wait()
+    block, within = split_order(order[...])
+    picks = [pick_sites(within[n : n + 1, :]) for n in range(8)]
     copies[1].wait()
+    table = jnp.concatenate([samples[:, 128 * t : 128 * t + 128] for t in range(8)], axis=0)
+    xs, e0s = [], []
+    for pair in range(2):
+        columns = []
+        for b in range(4):
+            n = 4 * pair + b
+            found = dot(table, picks[n])
+            columns.append(
+                sum(
+                    jnp.where(block[n : n + 1, :] == t, found[32 * t : 32 * t + 32], 0.0)
+                    for t in range(8)
+                )
+            )
+        both = jnp.transpose(jnp.concatenate(columns, axis=0)).astype(BF)
+        x_out[128 * pair : 128 * pair + 128, :] = both
+        xs += [both[:64], both[64:]]
     slot = slot_of(64)
-    spread = jnp.concatenate([samples[...]] * 4, axis=0)
-    lane = lane_of(128)
-    xs, e0s = [], []
+    copies[2].wait()
     for a in range(4):
-        picked = []
-        for half in range(2):
-            g = 2 * a + half
-            line = order[g : g + 1, :].astype(F32)
-            column = jnp.transpose(jnp.broadcast_to(line, (128, 128))).astype(jnp.int32)
-            pick = jnp.concatenate(
-                [jnp.where(column == lane + 128 * t, 1.0, 0.0).astype(BF) for t in range(8)],
-                axis=1,
-            )
-            picked.append(dot_nt(pick, spread))
-        x = merge_diagonal(jnp.concatenate(picked, axis=0), 64).astype(BF)
-        if a == 0:
-            copies[2].wait()
-        x_out[a * 64 : (a + 1) * 64, :] = x
-        e0 = merge_diagonal(dot(basis[a * 128 : (a + 1) * 128, :], x), 32).astype(BF)
+        e0 = merge_diagonal(dot(basis[a * 128 : (a + 1) * 128, :], xs[a]), 32).astype(BF)
         msg[OWN_E0 + a * 32 : OWN_E0 + (a + 1) * 32, :] = e0
-        xs.append(x)
         e0s.append(e0)
     msg[OWN_ROW : OWN_ROW + 64, :] = jnp.where(pi == 0, xs[3], xs[0])
     column_slot = jnp.where(pj == 0, 3, 0)
@@ -245,31 +266,24 @@
 
 
 def inner_kernel(
-    group, x, near_hbm, coupling_hbm, basis_hbm, order_hbm,
-    near_out, far, leaf_hbm, pick_hbm,
-    near, coupling, basis, order, turned_low, turned_high, leaf, pick, sems,
+    group, x, near_hbm, coupling_hbm, basis_hbm,
+    near_out, far, leaf_hbm,
+    near, coupling, basis, turned_low, turned_high, leaf, sems,
 ):
     copies = fetch(
-        [order_hbm, basis_hbm, coupling_hbm] + [near_hbm.at[a] for a in range(4)],
-        [order, basis, coupling] + [near.at[a] for a in range(4)],
+        [basis_hbm, coupling_hbm] + [near_hbm.at[a] for a in range(4)],
+        [basis, coupling] + [near.at[a] for a in range(4)],
         sems,
     )
     _, _, pi, pj = place()
     across_x, across_y, across = 2 * (1 - pi) + pj, 2 * pi + 1 - pj, 2 * (1 - pi) + 1 - pj
     copies[0].wait()
-    line = jnp.concatenate([order[g : g + 1, :] for g in range(8)], axis=1)
-    for t in range(8):
-        site = lax.broadcasted_iota(jnp.int32, (128, 1024), 0) + 128 * t
-        pick[128 * t : 128 * (t + 1), :] = jnp.where(site == line, 1.0, 0.0).astype(BF)
-    pick_copy = pltpu.make_async_copy(pick, pick_hbm, sems.at[7])
-    pick_copy.start()
-    copies[1].wait()
     for a in range(4):
         flat = jnp.transpose(basis[a * 128 : (a + 1) * 128, :].astype(F32))
         leaf[a * 64 : (a + 1) * 64, :] = flat.astype(BF)
-    leaf_copy = pltpu.make_async_copy(leaf, leaf_hbm, sems.at[8])
+    leaf_copy = pltpu.make_async_copy(leaf, leaf_hbm, sems.at[6])
     leaf_copy.start()
-    copies[2].wait()
+    copies[1].wait()
     turn_coupling(coupling, (turned_low, turned_high), far)
 
     slot = slot_of(64)
@@ -291,20 +305,19 @@
     store_windows(-1, jnp.where(pi == 0, nothing, middle), jnp.where(pi == 0, nothing, inner))
     store_windows(4, jnp.where(pi == 0, middle, nothing), jnp.where(pi == 0, inner, nothing))
     for a in range(4):
-        copies[3 + a].wait()
+        copies[2 + a].wait()
         total = jnp.zeros((256, 128), F32)
         for n in range(9):
             matrix = near[a, :, n].reshape(256, 64)
             total = total + dot(matrix, windows[a + n // 3 - 1, n % 3 - 1])
         near_out[a * 64 : (a + 1) * 64, :] = merge_diagonal(total, 64)
-    pick_copy.wait()
     leaf_copy.wait()
 
 
 def downward_kernel(count_x, count_y):
     def body(
-        group, near_part, far, cross, shared, transfer_hbm, near_hbm, leaf_hbm, pick_hbm, out,
-        h0, h1, h2, transfer, near_row, near_col, leaf, pick, sems,
+        group, near_part, far, cross, shared, transfer_hbm, near_hbm, leaf_hbm, order_hbm, out_hbm,
+        h0, h1, h2, transfer, near_row, near_col, leaf, order, out, sems,
     ):
         gx, gy, pi, pj = place()
         copies = fetch(
@@ -313,9 +326,9 @@
                 near_hbm.at[3 * pi, :, pl.ds(6 * pi, 3)],
                 near_hbm.at[:, 3 * pj],
                 leaf_hbm,
-                pick_hbm,
+                order_hbm,
             ),
-            (transfer, near_row, near_col, leaf, pick),
+            (transfer, near_row, near_col, leaf, order),
             sems,
         )
         swap = swap_of(gx, gy, count_x, count_y)
@@ -450,9 +463,10 @@
             beyond = beyond + dot(near_row[:, c].reshape(256, 64), shifts[c])
         beyond = merge_diagonal(beyond, 64)
 
-        row = lax.broadcasted_iota(jnp.int32, (256, 128), 0)
-        diagonal = row // 64 == slot_of(256)
         block = lax.broadcasted_iota(jnp.int32, (128, 128), 0) // 32 == slot_of(128)
+        copies[4].wait()
+        part, within = split_order(order[...])
+        pick = jnp.concatenate([pick_sites(within[n : n + 1, :]) for n in range(8)], axis=1)
         leaves = []
         copies[3].wait()
         for a in range(4):
@@ -465,14 +479,21 @@
                 total = total + dot(near_col[a, 3 * r + 2 * pj], boxes[a + r - 1])
             local = jnp.concatenate([local0[a]] * 4, axis=0)
             total = total + dot(leaf[a * 64 : (a + 1) * 64, :], jnp.where(block, local, jnp.zeros_like(local)))
-            total = jnp.concatenate([total] * 4, axis=0)
-            leaves.append(jnp.where(diagonal, total, 0.0).astype(BF))
-        leaves = jnp.concatenate(leaves, axis=0)
-        copies[4].wait()
+            leaves.append(total)
+        spread = []
+        for pair in range(2):
+            turned = jnp.transpose(jnp.concatenate(leaves[2 * pair : 2 * pair + 2], axis=0))
+            for b in range(4):
+                n = 4 * pair + b
+                line = turned[32 * b : 32 * b + 32]
+                parts = [jnp.where(part[n : n + 1, :] == t, line, 0.0) for t in range(8)]
+                spread.append(jnp.concatenate(parts, axis=0).astype(BF))
+        done = dot_nt(jnp.concatenate(spread, axis=1), pick).astype(BF)
         for t in range(8):
-            done = jnp.transpose(dot(pick[128 * t : 128 * (t + 1), :], leaves))
-            done = (done[:32] + done[32:64]) + (done[64:96] + done[96:])
-            out[:, 128 * t : 128 * (t + 1)] = done.astype(BF)
+            out[:, 128 * t : 128 * (t + 1)] = done[32 * t : 32 * t + 32]
+        last = pltpu.make_async_copy(out, out_hbm, sems.at[5])
+        last.start()
+        last.wait()
 
     return body
 
@@ -508,9 +529,11 @@
         for j in range(1, last_y, 2)
     ]
     for i in (0, last_x):
-        for j in range(1, last_y, 4):
-            second = [(i, j + 2), (i, j + 3)] if j + 3 < last_y else [(i, last_y), (i, 0)]
-            first = [(i, j), (i, j + 1)]
+        for j in range(-1, last_y, 4):
+            first = [(i, j), (i, j + 1)] if j > 0 else [(i, last_y), (i, 0)]
+            second = [(i, j + 2), (i, j + 3)]
+            if j < 0:
+                first, second = second, first
             groups.append(second + first if i == 0 else first + second)
     for i in range(1, last_x, 4):
         if i + 3 < last_x:
@@ -522,6 +545,65 @@
     return [[i * count_y + j for i, j in group] for group in groups]
 
 
+def run_upward(samples, order, basis, transfer):
+    return call(
+        upward_kernel,
+        (HBM,) * 4,
+        (VMEM((256, 128), BF), VMEM((OWN_ROWS, 128), BF)),
+        (
+            VMEM((8, 128), jnp.int32),
+            VMEM((32, 1024), BF),
+            VMEM((512, 64), BF),
+            VMEM((256, 32), BF),
+            pltpu.SemaphoreType.DMA((4,)),
+        ),
+    )(samples, order, basis, transfer)
+
+
+def run_cross(group, x, count_x, count_y):
+    body = functools.partial(cross_kernel, count_x=count_x, count_y=count_y)
+    return call(body, (VMEM,) * 2, VMEM((4, FAR_ROWS, 128), BF))(group, x)
+
+
+def run_inner(group, x, near_blocks, coupling, basis):
+    return call(
+        inner_kernel,
+        (VMEM,) * 2 + (HBM,) * 3,
+        (VMEM((256, 128), F32), VMEM((3, 224, 256), BF), HBM((256, 128), BF)),
+        (
+            VMEM((4, 4, 9, 64, 64), BF),
+            VMEM((3, 32, 32, 40), BF),
+            VMEM((512, 64), BF),
+            VMEM((256, 128), F32),
+            VMEM((256, 128), F32),
+            VMEM((256, 128), BF),
+            pltpu.SemaphoreType.DMA((7,)),
+        ),
+        flops=10**9,
+    )(group, x, near_blocks, coupling, basis)
+
+
+def run_downward(group, inner, cross, shared, transfer, near_blocks, order, count_x, count_y):
+    near_part, far, leaf = inner
+    return call(
+        downward_kernel(count_x, count_y),
+        (VMEM,) * 5 + (HBM,) * 4,
+        HBM((32, 1024), BF),
+        (
+            VMEM((320, 256), BF),
+            VMEM((256, 256), BF),
+            VMEM((256, 256), BF),
+            VMEM((256, 32), BF),
+            VMEM((4, 3, 64, 64), BF),
+            VMEM((4, 9, 64, 64), BF),
+            VMEM((256, 128), BF),
+            VMEM((8, 128), jnp.int32),
+            VMEM((32, 1024), BF),
+            pltpu.SemaphoreType.DMA((6,)),
+        ),
+    )(group, near_part, far, cross, shared, transfer, near_blocks, leaf, order)
+
+
 def solution(mesh):
     count_x, count_y = mesh.shape["gx"], mesh.shape["gy"]
     aligned = aligned_groups(count_x, count_y)
@@ -533,61 +615,15 @@
         basis = leaf_basis.transpose(0, 1, 3, 2).reshape(512, 64)
         transfer = transfer.reshape(256, 32)
         coupling = coupling.transpose(0, 2, 3, 1)
-        x, message = call(
-            upward_kernel,
-            (HBM,) * 4,
-            (VMEM((256, 128), BF), VMEM((OWN_ROWS, 128), BF)),
-            (
-                VMEM((8, 128), jnp.int32),
-                VMEM((32, 1024), BF),
-                VMEM((512, 64), BF),
-                VMEM((256, 32), BF),
-                pltpu.SemaphoreType.DMA((4,)),
-            ),
-        )(samples, order, basis, transfer)
+        x, message = run_upward(samples, order, basis, transfer)
         group = lax.all_gather(message, AXES, axis_index_groups=aligned)
-        cross_body = functools.partial(cross_kernel, count_x=count_x, count_y=count_y)
-        send = call(cross_body, (VMEM,) * 2, VMEM((4, FAR_ROWS, 128), BF))(group, x)
+        send = run_cross(group, x, count_x, count_y)
         cross = lax.all_to_all(send, AXES, 0, 0, axis_index_groups=shifted)
-        near_part, far, leaf, pick = call(
-            inner_kernel,
-            (VMEM,) * 2 + (HBM,) * 4,
-            (
-                VMEM((256, 128), F32),
-                VMEM((3, 224, 256), BF),
-                HBM((256, 128), BF),
-                HBM((1024, 1024), BF),
-            ),
-            (
-                VMEM((4, 4, 9, 64, 64), BF),
-                VMEM((3, 32, 32, 40), BF),
-                VMEM((512, 64), BF),
-                VMEM((8, 128), jnp.int32),
-                VMEM((256, 128), F32),
-                VMEM((256, 128), F32),
-                VMEM((256, 128), BF),
-                VMEM((1024, 1024), BF),
-                pltpu.SemaphoreType.DMA((9,)),
-            ),
-            flops=10**9,
-        )(group, x, near_blocks, coupling, basis, order)
+        inner = run_inner(group, x, near_blocks, coupling, basis)
         shared = lax.all_gather(cross[:, FAR_E2 : FAR_E2 + 32], AXES, axis_index_groups=aligned)
-        out = call(
-            downward_kernel(count_x, count_y),
-            (VMEM,) * 5 + (HBM,) * 4,
-            VMEM((32, 1024), BF),
-            (
-                VMEM((320, 256), BF),
-                VMEM((256, 256), BF),
-                VMEM((256, 256), BF),
-                VMEM((256, 32), BF),
-                VMEM((4, 3, 64, 64), BF),
-                VMEM((4, 9, 64, 64), BF),
-                VMEM((256, 128), BF),
-                VMEM((1024, 1024), BF),
-                pltpu.SemaphoreType.DMA((5,)),
-            ),
-        )(group, near_part, far, cross, shared, transfer, near_blocks, leaf, pick)
+        out = run_downward(
+            group, inner, cross, shared, transfer, near_blocks, order, count_x, count_y
+        )
         return out.T
 
     return jax.shard_map(

time: 37.2 us -> 35.7 us (0.960)
  starting transfers between devices: 3.44 us -> 6.14 us
  blocking collectives: 21 us -> 18.3 us
  Pallas kernels: 11.8 us -> 11 us
  local copies, waits for them, and re-layouts: 0.64 us -> 0.01 us
    all_to_all x1, starting transfers between devices: 3.44 us -> 6.14 us  [local(): cross = lax.all_to_all(send, AXES, 0, 0, axis_index_groups=shifted)]
    all_gather x1, blocking collectives: 8.3 us -> 5.62 us  [local(): lax.all_gather(cross[:, FAR_E2:FAR_E2 + 32], AXES, axis_index_groups=alig...]
    pallas_call x4, Pallas kernels: 11.8 us -> 11 us  [run(): pl.pallas_call(kernel, out_shape=shapes, in_specs=[pl.BlockSpec(memory_sp...]
    unnamed x1 -> x0, local copies, waits for them, and re-layouts: 0.63 us -> none
where the time goes in v5:
time: 35.7 us; the launch traced here: 35.5 us
  blocking collectives  18.3 us (51%)
  Pallas kernels  11 us (31%)
  starting transfers between devices  6.14 us (17%)
    all_gather x1, blocking collectives, local(): group = lax.all_gather(message, AXES, axis_index_groups=aligned)  12.7 us
    pallas_call x4, Pallas kernels, run(): pl.pallas_call(kernel, out_shape=shapes, in_specs=[pl.BlockSpec(memory_sp...  11 us
    all_to_all x1, starting transfers between devices, local(): cross = lax.all_to_all(send, AXES, 0, 0, axis_index_groups=shifted)  6.14 us
    all_gather x1, blocking collectives, local(): lax.all_gather(cross[:, FAR_E2:FAR_E2 + 32], AXES, axis_index_groups=alig...  5.62 us
  transfers between devices with their start and end apart: 1, of which 0 were waited for; matrix products, arithmetic and copies ran while one was open for 0% of the time, Pallas kernels for 12%

profile of v5, /device:TPU:1, one launch (start us, length us, event | category | flops | bytes accessed | tf_op | source)
XLA Modules:
  0.0 35.5 jit_solution(3855387563413591068)
XLA Ops:
  0.0 2.1 %shard_map.64 = (bf16[256,128]{1,0:T(8,128)(2,1)S(1)}, bf16[320,128]{1,0:T(8,128)(2,1)S(1)}) custom-call(bf16[32,1024]{1,0:T(8,128)(2,1)} %bitcast.18, s32[8,128]{1,0:T(8,128)} %bitcast.19, bf16[512,64]{1,0:T(8,128)(2,1)} %bitcast.16, bf16[256,32]{1,0:T(8,128)(2,1)} %bitcast.14), custom_call_target="tpu_custom_call" | custom-call | flops 1000000 | bytes 1048576 | tf_op jit(solution)/shard_map/pallas_call | solution.py:503
  2.1 12.7 %all-gather = bf16[1280,128]{1,0:T(8,128)(2,1)S(1)} all-gather(bf16[320,128]{1,0:T(8,128)(2,1)S(1)} %get-tuple-element.10), channel_id=2, replica_groups={{0,1,32,33},{2,3,34,35},{4,5,36,37},{6,7,38,39},{8,9,40,41},{10,11,42,4..., dimensions={0}, use_global_device_ids=true | all-gather | bytes 409600 | tf_op jit(solution)/shard_map/all_gather | solution.py:619
  14.8 0.8 %shard_map.66 = bf16[4,288,128]{2,1,0:T(8,128)(2,1)} custom-call(bf16[4,320,128]{2,1,0:T(8,128)(2,1)S(1)} %bitcast.10, bf16[256,128]{1,0:T(8,128)(2,1)S(1)} %get-tuple-element.11.x), custom_call_target="tpu_custom_call" | custom-call | flops 1000000 | bytes 1048576 | tf_op jit(solution)/shard_map/pallas_call | solution.py:503
  15.7 6.1 %all-to-all-start = ((bf16[4,288,128]{2,1,0:T(8,128)(2,1)}), bf16[4,288,128]{2,1,0:T(8,128)(2,1)S(1)}, u32[]{:S(2)}, u32[]{:S(2)}) async-start(bf16[4,288,128]{2,1,0:T(8,128)(2,1)} %shard_map.66), calls=%async_computation | async-start | bytes 589824 | tf_op jit(solution)/shard_map/all_to_all | solution.py:621
  21.8 4.2 %shard_map.65 = (f32[256,128]{1,0:T(8,128)S(1)}, bf16[3,224,256]{2,1,0:T(8,128)(2,1)S(1)}, bf16[256,128]{1,0:T(8,128)(2,1)}) custom-call(bf16[4,320,128]{2,1,0:T(8,128)(2,1)S(1)} %bitcast.11, bf16[256,128]{1,0:T(8,128)(2,1)S(1)} %get-tuple-element.11.x, bf16[4,4,9,64,64]{4,3,2,1,0:T(8,128)(2,1)} %near_hbm.3, bf16[3,32,32,40]{3,2,1,0:T(8,128)(2,1)} %bitcast.21, ...), custom_call_target="tpu_custom_call" | custom-call | flops 1000000000 | bytes 1048576 | tf_op jit(solution)/shard_map/pallas_call | solution.py:503
  26.0 0.0 all-to-all-done.cross
  26.1 5.6 %all-gather.1 = bf16[16,32,128]{2,1,0:T(8,128)(2,1)S(1)} all-gather(bf16[4,32,128]{2,1,0:T(8,128)(2,1)S(1)} %slice.4), channel_id=3, replica_groups={{0,1,32,33},{2,3,34,35},{4,5,36,37},{6,7,38,39},{8,9,40,41},{10,11,42,4..., dimensions={0}, use_global_device_ids=true | all-gather | bytes 163840 | tf_op jit(solution)/shard_map/all_gather | solution.py:623
  31.7 3.8 %shard_map.67 = bf16[32,1024]{1,0:T(8,128)(2,1)} custom-call(bf16[4,320,128]{2,1,0:T(8,128)(2,1)S(1)} %bitcast.12, f32[256,128]{1,0:T(8,128)S(1)} %get-tuple-element.12.near_part, bf16[3,224,256]{2,1,0:T(8,128)(2,1)S(1)} %get-tuple-element.13.far, bf16[4,288,128]{2,1,0:T(8,128)(2,1)S(1)} %all-to-all-done.cross, bf16[4,4,32,128]{3,2,1,0:T(8,128)(2,1)S(1)} %bitcast.13, ...), custom_call_target="tpu_custom_call" | custom-call | flops 1000000 | bytes 1048576 | tf_op jit(solution)/shard_map/pallas_call | solution.py:503
  (1 shorter events, 0.0 us)
Async XLA Ops:
  15.7 10.4 %all-to-all-start = ((bf16[4,288,128]{2,1,0:T(8,128)(2,1)}), bf16[4,288,128]{2,1,0:T(8,128)(2,1)S(1)}, u32[]{:S(2)}, u32[]{:S(2)}) async-start(bf16[4,288,128]{2,1,0:T(8,128)(2,1)} %shard_map.66), calls=%async_computation | async-start | bytes 589824 | tf_op jit(solution)/shard_map/all_to_all | solution.py:621

commit v6 on v5

--- a/solution.py
+++ b/solution.py
@@ -10,6 +10,7 @@
 BF = jnp.bfloat16
 F32 = jnp.float32
 AXES = ("gx", "gy")
+LEAF, TABLE_ROWS = 672, 928
 VMEM_BYTES = 32 * 1024 * 1024
 VMEM, HBM = pltpu.VMEM, pltpu.HBM
 
@@ -55,7 +56,7 @@
 def swap_of(gx, gy, count_x, count_y):
     end_x = (gx == 0) | (gx == count_x - 1)
     end_y = (gy == 0) | (gy == count_y - 1)
-    along_y = jnp.where((lax.rem(gy + 3, 4) < 2) & (gy > 2), 2, 0)
+    along_y = jnp.where((lax.rem(gy + 3, 4) < 2) == (gx == 0), 2, 0)
     along_x = jnp.where(lax.rem(gx + 3, 4) >= 2, 1, 0)
     return jnp.where(end_x & ~end_y, along_y, jnp.where(end_y & ~end_x, along_x, 0))
 
@@ -99,10 +100,13 @@
 
 
 def upward_kernel(
-    samples_hbm, order_hbm, basis_hbm, transfer_hbm, x_out, msg, order, samples, basis, transfer, sems
+    samples_hbm, order_hbm, basis_hbm, transfer_hbm, near_hbm,
+    x_out, msg, near, order, samples, basis, transfer, sems,
 ):
     copies = fetch(
-        (order_hbm, samples_hbm, basis_hbm, transfer_hbm), (order, samples, basis, transfer), sems
+        (order_hbm, samples_hbm, basis_hbm, transfer_hbm, near_hbm.at[0:2]),
+        (order, samples, basis, transfer, near),
+        sems,
     )
     _, _, pi, pj = place()
     copies[0].wait()
@@ -156,6 +160,7 @@
     e2 = e2 + roll(e2, 64)
     e2 = e2 + roll(e2, 32)
     msg[OWN_E2 : OWN_E2 + 32, :] = jnp.where(slot == 2 * pi + pj, e2, 0.0).astype(BF)
+    copies[4].wait()
 
 
 def cross_kernel(group, x, send, *, count_x, count_y):
@@ -237,7 +242,7 @@
     return out
 
 
-def turn_coupling(coupling, turned, far):
+def turn_coupling(coupling, turned, tables):
     row = lax.broadcasted_iota(jnp.int32, (56, 40), 0)
     number = lane_of(56, 40)
     u, w = row // 8 - 3, row % 8 - 3
@@ -262,30 +267,21 @@
                     turned[half][pl.ds(i, 8, stride=32), :] = out
         for half in range(2):
             lines = turned[half][0:224, :].astype(BF)
-            far[level, :, 128 * half : 128 * half + 128] = lines
+            tables[224 * level : 224 * level + 224, 128 * half : 128 * half + 128] = lines
 
 
 def inner_kernel(
-    group, x, near_hbm, coupling_hbm, basis_hbm,
-    near_out, far, leaf_hbm,
-    near, coupling, basis, turned_low, turned_high, leaf, sems,
+    group, x, near_low, near_hbm, coupling_hbm, basis_hbm, transfer_hbm, order_hbm,
+    near_out, tables, edges,
+    near_high, coupling, basis, transfer, order, turned_low, turned_high, sems,
 ):
     copies = fetch(
-        [basis_hbm, coupling_hbm] + [near_hbm.at[a] for a in range(4)],
-        [basis, coupling] + [near.at[a] for a in range(4)],
+        (coupling_hbm, near_hbm.at[2:4], basis_hbm, transfer_hbm, order_hbm),
+        (coupling, near_high, basis, transfer, order),
         sems,
     )
     _, _, pi, pj = place()
     across_x, across_y, across = 2 * (1 - pi) + pj, 2 * pi + 1 - pj, 2 * (1 - pi) + 1 - pj
-    copies[0].wait()
-    for a in range(4):
-        flat = jnp.transpose(basis[a * 128 : (a + 1) * 128, :].astype(F32))
-        leaf[a * 64 : (a + 1) * 64, :] = flat.astype(BF)
-    leaf_copy = pltpu.make_async_copy(leaf, leaf_hbm, sems.at[6])
-    leaf_copy.start()
-    copies[1].wait()
-    turn_coupling(coupling, (turned_low, turned_high), far)
-
     slot = slot_of(64)
     windows = {}
 
@@ -304,33 +300,39 @@
     nothing = jnp.zeros((64, 128), BF)
     store_windows(-1, jnp.where(pi == 0, nothing, middle), jnp.where(pi == 0, nothing, inner))
     store_windows(4, jnp.where(pi == 0, middle, nothing), jnp.where(pi == 0, inner, nothing))
-    for a in range(4):
-        copies[2 + a].wait()
+    def add_near(a):
+        near = near_low if a < 2 else near_high
         total = jnp.zeros((256, 128), F32)
         for n in range(9):
-            matrix = near[a, :, n].reshape(256, 64)
+            matrix = near[a % 2, :, n].reshape(256, 64)
             total = total + dot(matrix, windows[a + n // 3 - 1, n % 3 - 1])
         near_out[a * 64 : (a + 1) * 64, :] = merge_diagonal(total, 64)
-    leaf_copy.wait()
+        for r in range(3):
+            row = 768 + 64 * (3 * a + r)
+            edges[row : row + 64, :] = near[a % 2, 3 * pj, 3 * r + 2 * pj]
+
+    add_near(0)
+    add_near(1)
+    copies[0].wait()
+    turn_coupling(coupling, (turned_low, turned_high), tables)
+    copies[1].wait()
+    add_near(2)
+    add_near(3)
+    for c in range(3):
+        above, below = near_low[0, :, c], near_high[1, :, 6 + c]
+        edges[256 * c : 256 * c + 256, :] = jnp.where(pi == 0, above, below).reshape(256, 64)
+    for copy in copies[2:]:
+        copy.wait()
+    for a in range(4):
+        flat = jnp.transpose(basis[a * 128 : (a + 1) * 128, :].astype(F32))
+        tables[LEAF + a * 64 : LEAF + (a + 1) * 64, 0:128] = flat.astype(BF)
+    tables[LEAF : LEAF + 256, 128:160] = transfer[...]
+    near_out[256:264, :] = order[...].astype(F32)
 
 
 def downward_kernel(count_x, count_y):
-    def body(
-        group, near_part, far, cross, shared, transfer_hbm, near_hbm, leaf_hbm, order_hbm, out_hbm,
-        h0, h1, h2, transfer, near_row, near_col, leaf, order, out, sems,
-    ):
+    def body(group, near_part, tables, edges, cross, shared, out_hbm, h0, h1, h2, out, sem):
         gx, gy, pi, pj = place()
-        copies = fetch(
-            (
-                transfer_hbm,
-                near_hbm.at[3 * pi, :, pl.ds(6 * pi, 3)],
-                near_hbm.at[:, 3 * pj],
-                leaf_hbm,
-                order_hbm,
-            ),
-            (transfer, near_row, near_col, leaf, order),
-            sems,
-        )
         swap = swap_of(gx, gy, count_x, count_y)
         me, across_x, across_y = 2 * pi + pj, 2 * (1 - pi) + pj, 2 * pi + 1 - pj
         across = 2 * (1 - pi) + 1 - pj
@@ -412,15 +414,15 @@
         )
 
         slot = slot_of(32)
-        local2 = far_row(far[2, :, :224], h2[pl.ds(32 * pi, 224), :], pi)
+        local2 = far_row(tables[448 : 672, 0:224], h2[pl.ds(32 * pi, 224), :], pi)
         local2 = jnp.where(slot == pj, local2, 0.0)
         local2 = local2 + roll(local2, 64)
         local2 = (local2 + roll(local2, 32)).astype(BF)
-        copies[0].wait()
-        spread = dot(transfer[128:256, :], local2)
+        transfer = tables[LEAF : LEAF + 256, 128:160]
+        spread = dot(transfer[128:256], local2)
         local1 = []
         for i in range(2):
-            down = far_row(far[1, :, :224], h1[32 * i : 32 * i + 224, :], i)
+            down = far_row(tables[224 : 448, 0:224], h1[32 * i : 32 * i + 224, :], i)
             for j in range(2):
                 n = 2 * i + j
                 down = down + jnp.where(slot == j, spread[n * 32 : (n + 1) * 32], 0.0)
@@ -429,15 +431,13 @@
             local1.append((wide + roll(wide, 32)).astype(BF))
         local0 = []
         for i in range(4):
-            spread = dot(transfer[64 * (i % 2) : 64 * (i % 2) + 64, :], local1[i // 2])
-            down = far_row(far[0, :, :224], h0[32 * i : 32 * i + 224, :], i % 2)
+            spread = dot(transfer[64 * (i % 2) : 64 * (i % 2) + 64], local1[i // 2])
+            down = far_row(tables[0 : 224, 0:224], h0[32 * i : 32 * i + 224, :], i % 2)
             down = down + jnp.where(lax.rem(slot, 2) == 0, spread[:32], spread[32:])
             local0.append(down.astype(BF))
 
 
         slot = slot_of(64)
-        copies[1].wait()
-        copies[2].wait()
         column = kept(has_y, cross[from_y, FAR_X : FAR_X + 64, :])
         corner_in = kept(has_y, roll(cross[from_y, FAR_CORNER : FAR_CORNER + 64, :], 64))
         corner_out = kept(has_xy, roll(cross[from_xy, FAR_CORNER : FAR_CORNER + 64, :], 64))
@@ -460,15 +460,13 @@
         )
         beyond = jnp.zeros((256, 128), F32)
         for c in range(3):
-            beyond = beyond + dot(near_row[:, c].reshape(256, 64), shifts[c])
+            beyond = beyond + dot(edges[256 * c : 256 * c + 256, :], shifts[c])
         beyond = merge_diagonal(beyond, 64)
 
         block = lax.broadcasted_iota(jnp.int32, (128, 128), 0) // 32 == slot_of(128)
-        copies[4].wait()
-        part, within = split_order(order[...])
+        part, within = split_order(near_part[256:264, :].astype(jnp.int32))
         pick = jnp.concatenate([pick_sites(within[n : n + 1, :]) for n in range(8)], axis=1)
         leaves = []
-        copies[3].wait()
         for a in range(4):
             total = near_part[a * 64 : (a + 1) * 64, :]
             if a == 0:
@@ -476,9 +474,11 @@
             if a == 3:
                 total = total + jnp.where(pi == 0, 0.0, beyond)
             for r in range(3):
-                total = total + dot(near_col[a, 3 * r + 2 * pj], boxes[a + r - 1])
+                row = 768 + 64 * (3 * a + r)
+                total = total + dot(edges[row : row + 64, :], boxes[a + r - 1])
+            leaf = tables[LEAF + a * 64 : LEAF + (a + 1) * 64, 0:128]
             local = jnp.concatenate([local0[a]] * 4, axis=0)
-            total = total + dot(leaf[a * 64 : (a + 1) * 64, :], jnp.where(block, local, jnp.zeros_like(local)))
+            total = total + dot(leaf, jnp.where(block, local, jnp.zeros_like(local)))
             leaves.append(total)
         spread = []
         for pair in range(2):
@@ -491,7 +491,7 @@
         done = dot_nt(jnp.concatenate(spread, axis=1), pick).astype(BF)
         for t in range(8):
             out[:, 128 * t : 128 * (t + 1)] = done[32 * t : 32 * t + 32]
-        last = pltpu.make_async_copy(out, out_hbm, sems.at[5])
+        last = pltpu.make_async_copy(out, out_hbm, sem)
         last.start()
         last.wait()
 
@@ -529,12 +529,8 @@
         for j in range(1, last_y, 2)
     ]
     for i in (0, last_x):
-        for j in range(-1, last_y, 4):
-            first = [(i, j), (i, j + 1)] if j > 0 else [(i, last_y), (i, 0)]
-            second = [(i, j + 2), (i, j + 3)]
-            if j < 0:
-                first, second = second, first
-            groups.append(second + first if i == 0 else first + second)
+        groups.append([(i, 1), (i, 2), (i, last_y), (i, 0)])
+        groups += [[(i, j + d) for d in (2, 3, 0, 1)] for j in range(3, last_y, 4)]
     for i in range(1, last_x, 4):
         if i + 3 < last_x:
             for j in (0, last_y):
@@ -545,19 +541,19 @@
     return [[i * count_y + j for i, j in group] for group in groups]
 
 
-def run_upward(samples, order, basis, transfer):
+def run_upward(samples, order, basis, transfer, near_blocks):
     return call(
         upward_kernel,
-        (HBM,) * 4,
-        (VMEM((256, 128), BF), VMEM((OWN_ROWS, 128), BF)),
+        (HBM,) * 5,
+        (VMEM((256, 128), BF), VMEM((OWN_ROWS, 128), BF), VMEM((2, 4, 9, 64, 64), BF)),
         (
             VMEM((8, 128), jnp.int32),
             VMEM((32, 1024), BF),
             VMEM((512, 64), BF),
             VMEM((256, 32), BF),
-            pltpu.SemaphoreType.DMA((4,)),
+            pltpu.SemaphoreType.DMA((5,)),
         ),
-    )(samples, order, basis, transfer)
+    )(samples, order, basis, transfer, near_blocks)
 
 
 def run_cross(group, x, count_x, count_y):
@@ -565,43 +561,38 @@
     return call(body, (VMEM,) * 2, VMEM((4, FAR_ROWS, 128), BF))(group, x)
 
 
-def run_inner(group, x, near_blocks, coupling, basis):
+def run_inner(group, x, near, near_blocks, coupling, basis, transfer, order):
     return call(
         inner_kernel,
-        (VMEM,) * 2 + (HBM,) * 3,
-        (VMEM((256, 128), F32), VMEM((3, 224, 256), BF), HBM((256, 128), BF)),
+        (VMEM,) * 3 + (HBM,) * 5,
+        (VMEM((264, 128), F32), VMEM((TABLE_ROWS, 256), BF), VMEM((1536, 64), BF)),
         (
-            VMEM((4, 4, 9, 64, 64), BF),
+            VMEM((2, 4, 9, 64, 64), BF),
             VMEM((3, 32, 32, 40), BF),
             VMEM((512, 64), BF),
+            VMEM((256, 32), BF),
+            VMEM((8, 128), jnp.int32),
             VMEM((256, 128), F32),
             VMEM((256, 128), F32),
-            VMEM((256, 128), BF),
-            pltpu.SemaphoreType.DMA((7,)),
+            pltpu.SemaphoreType.DMA((5,)),
         ),
         flops=10**9,
-    )(group, x, near_blocks, coupling, basis)
-
-
-def run_downward(group, inner, cross, shared, transfer, near_blocks, order, count_x, count_y):
-    near_part, far, leaf = inner
+    )(group, x, near, near_blocks, coupling, basis, transfer, order)
+
+
+def run_downward(group, inner, cross, shared, count_x, count_y):
     return call(
         downward_kernel(count_x, count_y),
-        (VMEM,) * 5 + (HBM,) * 4,
+        (VMEM,) * 6,
         HBM((32, 1024), BF),
         (
             VMEM((320, 256), BF),
             VMEM((256, 256), BF),
             VMEM((256, 256), BF),
-            VMEM((256, 32), BF),
-            VMEM((4, 3, 64, 64), BF),
-            VMEM((4, 9, 64, 64), BF),
-            VMEM((256, 128), BF),
-            VMEM((8, 128), jnp.int32),
             VMEM((32, 1024), BF),
-            pltpu.SemaphoreType.DMA((6,)),
+            pltpu.SemaphoreType.DMA,
         ),
-    )(group, near_part, far, cross, shared, transfer, near_blocks, leaf, order)
+    )(group, *inner, cross, shared)
 
 
 def solution(mesh):
@@ -615,15 +606,15 @@
         basis = leaf_basis.transpose(0, 1, 3, 2).reshape(512, 64)
         transfer = transfer.reshape(256, 32)
         coupling = coupling.transpose(0, 2, 3, 1)
-        x, message = run_upward(samples, order, basis, transfer)
+        x, message, near = run_upward(samples, order, basis, transfer, near_blocks)
         group = lax.all_gather(message, AXES, axis_index_groups=aligned)
         send = run_cross(group, x, count_x, count_y)
         cross = lax.all_to_all(send, AXES, 0, 0, axis_index_groups=shifted)
-        inner = run_inner(group, x, near_blocks, coupling, basis)
+        inner = run_inner(
+            group, x, near, near_blocks, coupling, basis, transfer, order
+        )
         shared = lax.all_gather(cross[:, FAR_E2 : FAR_E2 + 32], AXES, axis_index_groups=aligned)
-        out = run_downward(
-            group, inner, cross, shared, transfer, near_blocks, order, count_x, count_y
-        )
+        out = run_downward(group, inner, cross, shared, count_x, count_y)
         return out.T
 
     return jax.shard_map(

time: 35.7 us -> 34.3 us (0.961)
  waiting for transfers between devices: 0.01 us -> 5.13 us
  starting transfers between devices: 6.14 us -> 3.45 us
  Pallas kernels: 11 us -> 8.47 us
  blocking collectives: 18.3 us -> 17 us
    all_to_all x1, waiting for transfers between devices: 0.01 us -> 5.13 us  [local(): cross = lax.all_to_all(send, AXES, 0, 0, axis_index_groups=shifted)]
    all_to_all x1, starting transfers between devices: 6.14 us -> 3.45 us  [local(): cross = lax.all_to_all(send, AXES, 0, 0, axis_index_groups=shifted)]
    pallas_call x4, Pallas kernels: 11 us -> 8.47 us  [run(): pl.pallas_call(kernel, out_shape=shapes, in_specs=[pl.BlockSpec(memory_sp...]
    all_gather x1, blocking collectives: 5.62 us -> 4.35 us  [local(): lax.all_gather(cross[:, FAR_E2:FAR_E2 + 32], AXES, axis_index_groups=alig...]
  transfers between devices with their start and end apart: 1 -> 1, of which waited for: 0 -> 1; matrix products, arithmetic and copies ran while one was open for 0% -> 0% of each run, Pallas kernels for 12% -> 9%
where the time goes in v6:
time: 34.3 us; the launch traced here: 34.1 us
  blocking collectives  17 us (50%)
  Pallas kernels  8.47 us (25%)
  waiting for transfers between devices  5.13 us (15%)
  starting transfers between devices  3.45 us (10%)
    all_gather x1, blocking collectives, local(): group = lax.all_gather(message, AXES, axis_index_groups=aligned)  12.7 us
    pallas_call x4, Pallas kernels, run(): pl.pallas_call(kernel, out_shape=shapes, in_specs=[pl.BlockSpec(memory_sp...  8.47 us
    all_to_all x1, waiting for transfers between devices, local(): cross = lax.all_to_all(send, AXES, 0, 0, axis_index_groups=shifted)  5.13 us
    all_gather x1, blocking collectives, local(): lax.all_gather(cross[:, FAR_E2:FAR_E2 + 32], AXES, axis_index_groups=alig...  4.35 us
    all_to_all x1, starting transfers between devices, local(): cross = lax.all_to_all(send, AXES, 0, 0, axis_index_groups=shifted)  3.45 us
  transfers between devices with their start and end apart: 1, of which 1 were waited for; matrix products, arithmetic and copies ran while one was open for 0% of the time, Pallas kernels for 9%

profile of v6, /device:TPU:1, one launch (start us, length us, event | category | flops | bytes accessed | tf_op | source)
XLA Modules:
  0.0 34.1 jit_solution(1127711498656817907)
XLA Ops:
  0.0 2.1 %shard_map.64 = (bf16[256,128]{1,0:T(8,128)(2,1)S(1)}, bf16[320,128]{1,0:T(8,128)(2,1)S(1)}, bf16[2,4,9,64,64]{4,3,2,1,0:T(8,128)(2,1)S(1)}) custom-call(bf16[32,1024]{1,0:T(8,128)(2,1)} %bitcast.19, s32[8,128]{1,0:T(8,128)} %bitcast.20, bf16[512,64]{1,0:T(8,128)(2,1)} %bitcast.15, bf16[256,32]{1,0:T(8,128)(2,1)} %bitcast.17, bf16[4,4,9,64,64]{4,3,2,1,0:T(8,128)(2,1)} %near_hbm.3), custom_call_target="tpu_custom_call" | custom-call | flops 1000000 | bytes 1048576 | tf_op jit(solution)/shard_map/pallas_call | solution.py:503
  2.1 12.7 %all-gather = bf16[1280,128]{1,0:T(8,128)(2,1)S(1)} all-gather(bf16[320,128]{1,0:T(8,128)(2,1)S(1)} %get-tuple-element.11), channel_id=2, replica_groups={{0,1,32,33},{2,3,34,35},{4,5,36,37},{6,7,38,39},{8,9,40,41},{10,11,42,4..., dimensions={0}, use_global_device_ids=true | all-gather | bytes 409600 | tf_op jit(solution)/shard_map/all_gather | solution.py:610
  14.8 0.8 %shard_map.66 = bf16[4,288,128]{2,1,0:T(8,128)(2,1)} custom-call(bf16[4,320,128]{2,1,0:T(8,128)(2,1)S(1)} %bitcast.10, bf16[256,128]{1,0:T(8,128)(2,1)S(1)} %get-tuple-element.12.x), custom_call_target="tpu_custom_call" | custom-call | flops 1000000 | bytes 1048576 | tf_op jit(solution)/shard_map/pallas_call | solution.py:503
  15.7 3.5 %all-to-all-start = ((bf16[4,288,128]{2,1,0:T(8,128)(2,1)}), bf16[4,288,128]{2,1,0:T(8,128)(2,1)S(1)}, u32[]{:S(2)}, u32[]{:S(2)}) async-start(bf16[4,288,128]{2,1,0:T(8,128)(2,1)} %shard_map.66), calls=%async_computation | async-start | bytes 589824 | tf_op jit(solution)/shard_map/all_to_all | solution.py:612
  19.1 3.1 %shard_map.65 = (f32[264,128]{1,0:T(8,128)S(1)}, bf16[928,256]{1,0:T(8,128)(2,1)S(1)}, bf16[1536,64]{1,0:T(8,128)(2,1)S(1)}) custom-call(bf16[4,320,128]{2,1,0:T(8,128)(2,1)S(1)} %bitcast.11, bf16[256,128]{1,0:T(8,128)(2,1)S(1)} %get-tuple-element.12.x, bf16[2,4,9,64,64]{4,3,2,1,0:T(8,128)(2,1)S(1)} %get-tuple-element.13.near_low, ...), custom_call_target="tpu_custom_call" | custom-call | flops 1000000000 | bytes 1048576 | tf_op jit(solution)/shard_map/pallas_call | solution.py:503
  22.3 5.1 %all-to-all-done.cross = bf16[4,288,128]{2,1,0:T(8,128)(2,1)S(1)} async-done(((bf16[4,288,128]{2,1,0:T(8,128)(2,1)}), bf16[4,288,128]{2,1,0:T(8,128)(2,1)S(1)}, u32[]{:S(2)}, u32[]{:S(2)}) %all-to-all-start) | async-done | bytes 294944 | tf_op jit(solution)/shard_map/all_to_all | solution.py:612
  27.4 4.4 %all-gather.1 = bf16[16,32,128]{2,1,0:T(8,128)(2,1)S(1)} all-gather(bf16[4,32,128]{2,1,0:T(8,128)(2,1)S(1)} %slice.4), channel_id=3, replica_groups={{0,1,32,33},{2,3,34,35},{4,5,36,37},{6,7,38,39},{8,9,40,41},{10,11,42,4..., dimensions={0}, use_global_device_ids=true | all-gather | bytes 163840 | tf_op jit(solution)/shard_map/all_gather | solution.py:616
  31.8 2.4 %shard_map.67 = bf16[32,1024]{1,0:T(8,128)(2,1)} custom-call(bf16[4,320,128]{2,1,0:T(8,128)(2,1)S(1)} %bitcast.12, f32[264,128]{1,0:T(8,128)S(1)} %get-tuple-element.14.near_part, bf16[928,256]{1,0:T(8,128)(2,1)S(1)} %get-tuple-element.15.tables, bf16[1536,64]{1,0:T(8,128)(2,1)S(1)} %get-tuple-element.16.edges, bf16[4,288,128]{2,1,0:T(8,128)(2,1)S(1)} %all-to-all-done.cross, ...), custom_call_target="tpu_custom_call" | custom-call | flops 1000000 | bytes 1048576 | tf_op jit(solution)/shard_map/pallas_call | solution.py:503
  (1 shorter events, 0.0 us)
Async XLA Ops:
  15.7 11.7 %all-to-all-start = ((bf16[4,288,128]{2,1,0:T(8,128)(2,1)}), bf16[4,288,128]{2,1,0:T(8,128)(2,1)S(1)}, u32[]{:S(2)}, u32[]{:S(2)}) async-start(bf16[4,288,128]{2,1,0:T(8,128)(2,1)} %shard_map.66), calls=%async_computation | async-start | bytes 589824 | tf_op jit(solution)/shard_map/all_to_all | solution.py:612

commit v7 on v6

--- a/solution.py
+++ b/solution.py
@@ -14,7 +14,7 @@
 VMEM_BYTES = 32 * 1024 * 1024
 VMEM, HBM = pltpu.VMEM, pltpu.HBM
 
-OWN_ROW, OWN_COL, OWN_E0, OWN_E1, OWN_E2, OWN_ROWS = 0, 64, 128, 256, 288, 320
+OWN_ROW, OWN_COL, OWN_E0, OWN_ROWS = 0, 64, 128, 256
 FAR_X, FAR_E0, FAR_CORNER, FAR_E1, FAR_E1_SIDE, FAR_E2, FAR_ROWS = 0, 64, 128, 192, 224, 256, 288
 
 
@@ -53,10 +53,17 @@
     return gx, gy, lax.rem(gx, 2), lax.rem(gy, 2)
 
 
+def corner_pair(count_y):
+    return (count_y - 8) // 2 if count_y > 8 else 0
+
+
 def swap_of(gx, gy, count_x, count_y):
     end_x = (gx == 0) | (gx == count_x - 1)
     end_y = (gy == 0) | (gy == count_y - 1)
-    along_y = jnp.where((lax.rem(gy + 3, 4) < 2) == (gx == 0), 2, 0)
+    corner = corner_pair(count_y)
+    pair = lax.div(gy + 1, 2) - 1
+    first = (pair == corner) | (lax.rem(jnp.where(pair > corner, pair + 1, pair), 2) == 0)
+    along_y = jnp.where(first == (gx == 0), 2, 0)
     along_x = jnp.where(lax.rem(gx + 3, 4) >= 2, 1, 0)
     return jnp.where(end_x & ~end_y, along_y, jnp.where(end_y & ~end_x, along_x, 0))
 
@@ -101,7 +108,7 @@
 
 def upward_kernel(
     samples_hbm, order_hbm, basis_hbm, transfer_hbm, near_hbm,
-    x_out, msg, near, order, samples, basis, transfer, sems,
+    x_out, msg, near, turned, order, samples, basis, transfer, sems,
 ):
     copies = fetch(
         (order_hbm, samples_hbm, basis_hbm, transfer_hbm, near_hbm.at[0:2]),
@@ -143,27 +150,44 @@
     msg[OWN_COL : OWN_COL + 64, :] = packed
 
     one = eye(32)
-    slot = slot_of(32)
     copies[3].wait()
-    turned = [dot_nt(one, transfer[n * 32 : (n + 1) * 32, :]).astype(BF) for n in range(8)]
-    e1 = jnp.zeros((32, 128), F32)
+    for n in range(8):
+        block = slice(n * 32, (n + 1) * 32)
+        turned[block, :] = dot_nt(one, transfer[block, :]).astype(BF)
+    copies[4].wait()
+
+
+def lift(group, turned, tiles):
+    slot = lax.rem(slot_of(32, 512), 4)
+    lines = [
+        jnp.concatenate(
+            [group[m, OWN_E0 + 32 * x : OWN_E0 + 32 * x + 32, :] for m in range(4)], axis=1
+        )
+        for x in range(4)
+    ]
+    matrices = [turned[32 * n : 32 * n + 32, :] for n in range(4)]
+    e1 = jnp.zeros((32, 512), F32)
     for x in range(2):
         parts = []
         for j in range(2):
-            parts.append(dot(turned[j], e0s[2 * x]) + dot(turned[2 + j], e0s[2 * x + 1]))
+            parts.append(dot(matrices[j], lines[2 * x]) + dot(matrices[2 + j], lines[2 * x + 1]))
         joined = parts[0] + roll(parts[1], -32)
         e1 = jnp.where(slot == 2 * x, roll(joined, 64 * x), e1)
         e1 = jnp.where(slot == 2 * x + 1, roll(joined, 64 * x - 32), e1)
     e1 = e1.astype(BF)
-    msg[OWN_E1 : OWN_E1 + 32, :] = e1
-    e2 = merge_diagonal(dot(jnp.concatenate(turned[4:], axis=0), e1), 32)
-    e2 = e2 + roll(e2, 64)
-    e2 = e2 + roll(e2, 32)
-    msg[OWN_E2 : OWN_E2 + 32, :] = jnp.where(slot == 2 * pi + pj, e2, 0.0).astype(BF)
-    copies[4].wait()
-
-
-def cross_kernel(group, x, send, *, count_x, count_y):
+    product = dot(turned[128:256, :], e1)
+    slot = slot_of(32)
+    top = jnp.zeros((32, 128), F32)
+    for m in range(4):
+        tiles[m] = e1[:, 128 * m : 128 * m + 128]
+        e2 = merge_diagonal(product[:, 128 * m : 128 * m + 128], 32)
+        e2 = e2 + roll(e2, 64)
+        e2 = e2 + roll(e2, 32)
+        top = jnp.where(slot == m, e2, top)
+    tiles[4] = top.astype(BF)
+
+
+def cross_kernel(group, x, turned, send_hbm, tiles, send, sems, *, count_x, count_y):
     gx, gy, pi, pj = place()
     swap = swap_of(gx, gy, count_x, count_y)
     me, across_x, across_y = 2 * pi + pj, 2 * (1 - pi) + pj, 2 * pi + 1 - pj
@@ -172,14 +196,6 @@
     e0 = group[me, OWN_E0 : OWN_E0 + 128, :]
     e0_rows = jnp.where(pi == 0, e0[:64], e0[64:])
     x_row = jnp.where(pi == 0, x[0:64, :], x[192:256, :])
-    e1 = group[me, OWN_E1 : OWN_E1 + 32, :]
-    e2 = group[0, OWN_E2 : OWN_ROWS, :]
-    for m in range(1, 4):
-        e2 = e2 + group[m, OWN_E2 : OWN_ROWS, :]
-    for m in range(4):
-        send[m, FAR_E2 : FAR_E2 + 32, :] = e2
-        send[m, FAR_E1 : FAR_E1 + 32, :] = e1
-
     to = (2 * pi + 1 - pj) ^ swap
     send[to, FAR_X : FAR_X + 64, :] = x_row
     send[to, FAR_E0 : FAR_E0 + 64, :] = e0_rows
@@ -187,7 +203,7 @@
     column = jnp.where(pi == 0, roll(column, 64), roll(column, -32))
     corner_e0 = group[across_y, pl.ds(OWN_E0 + 64 * pi, 64), :]
     send[to, FAR_CORNER : FAR_CORNER + 64, :] = jnp.where(near_half, corner_e0, column)
-    send[to, FAR_E1_SIDE : FAR_E1_SIDE + 32, :] = group[across_y, OWN_E1 : OWN_E1 + 32, :]
+    side_y = to
 
     to = (2 * (1 - pi) + pj) ^ swap
     column_slot = jnp.where(pj == 0, 0, 3)
@@ -200,17 +216,30 @@
     corner_x = roll(group[across_x, OWN_ROW : OWN_ROW + 64, :], 64)
     corner_e0 = group[across_x, pl.ds(OWN_E0 + 64 * pi, 64), :]
     send[to, FAR_CORNER : FAR_CORNER + 64, :] = jnp.where(near_half, corner_e0, corner_x)
-    send[to, FAR_E1_SIDE : FAR_E1_SIDE + 32, :] = group[across_x, OWN_E1 : OWN_E1 + 32, :]
+    side_x = to
 
     to = (2 * pi + pj) ^ swap
-    send[to, FAR_X : FAR_X + 64, :] = jnp.zeros((64, 128), BF)
-    send[to, FAR_E0 : FAR_E0 + 64, :] = jnp.zeros((64, 128), BF)
+    send[to, 0:FAR_CORNER, :] = jnp.zeros((FAR_CORNER, 128), BF)
     send[to, FAR_CORNER : FAR_CORNER + 64, :] = jnp.where(near_half, e0_rows, roll(x_row, 64))
-    send[to, FAR_E1_SIDE : FAR_E1_SIDE + 32, :] = jnp.zeros((32, 128), BF)
-
-    to = (2 * (1 - pi) + 1 - pj) ^ swap
-    send[to, 0:FAR_E1, :] = jnp.zeros((FAR_E1, 128), BF)
-    send[to, FAR_E1_SIDE : FAR_E1_SIDE + 32, :] = jnp.zeros((32, 128), BF)
+    send[(2 * (1 - pi) + 1 - pj) ^ swap, 0:FAR_E1, :] = jnp.zeros((FAR_E1, 128), BF)
+    strips = pltpu.make_async_copy(
+        send.at[:, 0:FAR_E1, :], send_hbm.at[:, 0:FAR_E1, :], sems.at[0]
+    )
+    strips.start()
+
+    lift(group, turned, tiles)
+    for m in range(4):
+        send[m, FAR_E1 : FAR_E1 + 32, :] = tiles[me]
+        send[m, FAR_E1_SIDE : FAR_E1_SIDE + 32, :] = jnp.zeros((32, 128), BF)
+        send[m, FAR_E2 : FAR_E2 + 32, :] = tiles[4]
+    send[side_y, FAR_E1_SIDE : FAR_E1_SIDE + 32, :] = tiles[across_y]
+    send[side_x, FAR_E1_SIDE : FAR_E1_SIDE + 32, :] = tiles[across_x]
+    levels = pltpu.make_async_copy(
+        send.at[:, FAR_E1:FAR_ROWS, :], send_hbm.at[:, FAR_E1:FAR_ROWS, :], sems.at[1]
+    )
+    levels.start()
+    strips.wait()
+    levels.wait()
 
 
 def store_row_of_tiles(halo, start, left, middle, right):
@@ -331,7 +360,7 @@
 
 
 def downward_kernel(count_x, count_y):
-    def body(group, near_part, tables, edges, cross, shared, out_hbm, h0, h1, h2, out, sem):
+    def body(group, tiles, near_part, tables, edges, cross, shared, out_hbm, h0, h1, h2, out, sem):
         gx, gy, pi, pj = place()
         swap = swap_of(gx, gy, count_x, count_y)
         me, across_x, across_y = 2 * pi + pj, 2 * (1 - pi) + pj, 2 * pi + 1 - pj
@@ -377,15 +406,14 @@
         for halo in (h1, h2):
             halo[0:32, :] = jnp.zeros((32, 256), BF)
             halo[224:256, :] = jnp.zeros((32, 256), BF)
-        own_e1 = slice(OWN_E1, OWN_E1 + 32)
         far_e1, side_e1 = slice(FAR_E1, FAR_E1 + 32), slice(FAR_E1_SIDE, FAR_E1_SIDE + 32)
         store_sides(
-            96, group[me, own_e1, :], group[across_y, own_e1, :], kept(has_y, cross[from_y, far_e1, :])
+            96, tiles[me], tiles[across_y], kept(has_y, cross[from_y, far_e1, :])
         )
         store_sides(
             32 + 128 * (1 - pi),
-            group[across_x, own_e1, :],
-            group[across, own_e1, :],
+            tiles[across_x],
+            tiles[across],
             kept(has_y, cross[from_y, side_e1, :]),
         )
         store_sides(
@@ -397,9 +425,6 @@
 
         above, below = gx >= 2, gx < count_x - 2
         before, after = gy >= 2, gy < count_y - 2
-        e2 = group[0, OWN_E2:OWN_ROWS, :]
-        for m in range(1, 4):
-            e2 = e2 + group[m, OWN_E2:OWN_ROWS, :]
 
         def brought(m, slot, keep):
             other = swap_of(gx - pi + m // 2, gy - pj + m % 2, count_x, count_y)
@@ -408,7 +433,7 @@
         store_row_of_tiles(
             h2, 32, brought(0, 0, above & before), brought(0, 1, above), brought(1, 1, above & after)
         )
-        store_row_of_tiles(h2, 96, brought(0, 2, before), e2, brought(1, 3, after))
+        store_row_of_tiles(h2, 96, brought(0, 2, before), tiles[4], brought(1, 3, after))
         store_row_of_tiles(
             h2, 160, brought(2, 2, below & before), brought(2, 3, below), brought(3, 3, below & after)
         )
@@ -529,8 +554,9 @@
         for j in range(1, last_y, 2)
     ]
     for i in (0, last_x):
-        groups.append([(i, 1), (i, 2), (i, last_y), (i, 0)])
-        groups += [[(i, j + d) for d in (2, 3, 0, 1)] for j in range(3, last_y, 4)]
+        pairs = [[(i, j), (i, j + 1)] for j in range(1, last_y, 2)]
+        groups.append(pairs.pop(corner_pair(count_y)) + [(i, last_y), (i, 0)])
+        groups += [pairs[n] + pairs[n + 1] for n in range(0, len(pairs), 2)]
     for i in range(1, last_x, 4):
         if i + 3 < last_x:
             for j in (0, last_y):
@@ -545,7 +571,7 @@
     return call(
         upward_kernel,
         (HBM,) * 5,
-        (VMEM((256, 128), BF), VMEM((OWN_ROWS, 128), BF), VMEM((2, 4, 9, 64, 64), BF)),
+        (VMEM((256, 128), BF), VMEM((OWN_ROWS, 128), BF), VMEM((2, 4, 9, 64, 64), BF), VMEM((256, 32), BF)),
         (
             VMEM((8, 128), jnp.int32),
             VMEM((32, 1024), BF),
@@ -556,9 +582,14 @@
     )(samples, order, basis, transfer, near_blocks)
 
 
-def run_cross(group, x, count_x, count_y):
+def run_cross(group, x, turned, count_x, count_y):
     body = functools.partial(cross_kernel, count_x=count_x, count_y=count_y)
-    return call(body, (VMEM,) * 2, VMEM((4, FAR_ROWS, 128), BF))(group, x)
+    return call(
+        body,
+        (VMEM,) * 3,
+        (HBM((4, FAR_ROWS, 128), BF), VMEM((5, 32, 128), BF)),
+        (VMEM((4, FAR_ROWS, 128), BF), pltpu.SemaphoreType.DMA((2,))),
+    )(group, x, turned)
 
 
 def run_inner(group, x, near, near_blocks, coupling, basis, transfer, order):
@@ -580,10 +611,10 @@
     )(group, x, near, near_blocks, coupling, basis, transfer, order)
 
 
-def run_downward(group, inner, cross, shared, count_x, count_y):
+def run_downward(group, tiles, inner, cross, shared, count_x, count_y):
     return call(
         downward_kernel(count_x, count_y),
-        (VMEM,) * 6,
+        (VMEM,) * 7,
         HBM((32, 1024), BF),
         (
             VMEM((320, 256), BF),
@@ -592,7 +623,7 @@
             VMEM((32, 1024), BF),
             pltpu.SemaphoreType.DMA,
         ),
-    )(group, *inner, cross, shared)
+    )(group, tiles, *inner, cross, shared)
 
 
 def solution(mesh):
@@ -606,15 +637,15 @@
         basis = leaf_basis.transpose(0, 1, 3, 2).reshape(512, 64)
         transfer = transfer.reshape(256, 32)
         coupling = coupling.transpose(0, 2, 3, 1)
-        x, message, near = run_upward(samples, order, basis, transfer, near_blocks)
+        x, message, near, turned = run_upward(samples, order, basis, transfer, near_blocks)
         group = lax.all_gather(message, AXES, axis_index_groups=aligned)
-        send = run_cross(group, x, count_x, count_y)
+        send, tiles = run_cross(group, x, turned, count_x, count_y)
         cross = lax.all_to_all(send, AXES, 0, 0, axis_index_groups=shifted)
         inner = run_inner(
             group, x, near, near_blocks, coupling, basis, transfer, order
         )
         shared = lax.all_gather(cross[:, FAR_E2 : FAR_E2 + 32], AXES, axis_index_groups=aligned)
-        out = run_downward(group, inner, cross, shared, count_x, count_y)
+        out = run_downward(group, tiles, inner, cross, shared, count_x, count_y)
         return out.T
 
     return jax.shard_map(

time: 34.3 us -> 33.9 us (0.988)
  waiting for transfers between devices: 5.13 us -> 2.51 us
  blocking collectives: 17 us -> 19.1 us
    all_to_all x1, waiting for transfers between devices: 5.13 us -> 2.51 us  [local(): cross = lax.all_to_all(send, AXES, 0, 0, axis_index_groups=shifted)]
    all_gather x1, blocking collectives: 4.35 us -> 6.61 us  [local(): lax.all_gather(cross[:, FAR_E2:FAR_E2 + 32], AXES, axis_index_groups=alig...]
where the time goes in v7:
time: 33.9 us; the launch traced here: 33.6 us
  blocking collectives  19.1 us (56%)
  Pallas kernels  8.51 us (25%)
  starting transfers between devices  3.46 us (10%)
  waiting for transfers between devices  2.51 us (7%)
    all_gather x1, blocking collectives, local(): group = lax.all_gather(message, AXES, axis_index_groups=aligned)  12.5 us
    pallas_call x4, Pallas kernels, run(): pl.pallas_call(kernel, out_shape=shapes, in_specs=[pl.BlockSpec(memory_sp...  8.51 us
    all_gather x1, blocking collectives, local(): lax.all_gather(cross[:, FAR_E2:FAR_E2 + 32], AXES, axis_index_groups=alig...  6.61 us
    all_to_all x1, starting transfers between devices, local(): cross = lax.all_to_all(send, AXES, 0, 0, axis_index_groups=shifted)  3.46 us
    all_to_all x1, waiting for transfers between devices, local(): cross = lax.all_to_all(send, AXES, 0, 0, axis_index_groups=shifted)  2.51 us
  transfers between devices with their start and end apart: 1, of which 1 were waited for; matrix products, arithmetic and copies ran while one was open for 0% of the time, Pallas kernels for 9%

profile of v7, /device:TPU:1, one launch (start us, length us, event | category | flops | bytes accessed | tf_op | source)
XLA Modules:
  0.0 33.6 jit_solution(5061275824893193000)
XLA Ops:
  0.0 1.6 %shard_map.64 = (bf16[256,128]{1,0:T(8,128)(2,1)S(1)}, bf16[256,128]{1,0:T(8,128)(2,1)S(1)}, bf16[2,4,9,64,64]{4,3,2,1,0:T(8,128)(2,1)S(1)}, bf16[256,32]{1,0:T(8,128)(2,1)S(1)}) custom-call(bf16[32,1024]{1,0:T(8,128)(2,1)} %bitcast.19, s32[8,128]{1,0:T(8,128)} %bitcast.20, bf16[512,64]{1,0:T(8,128)(2,1)} %bitcast.15, bf16[256,32]{1,0:T(8,128)(2,1)} %bitcast.17, ...), custom_call_target="tpu_custom_call" | custom-call | flops 1000000 | bytes 1048576 | tf_op jit(solution)/shard_map/pallas_call | solution.py:528
  1.6 12.5 %all-gather = bf16[1024,128]{1,0:T(8,128)(2,1)S(1)} all-gather(bf16[256,128]{1,0:T(8,128)(2,1)S(1)} %get-tuple-element.14), channel_id=2, replica_groups={{0,1,32,33},{2,3,34,35},{4,5,36,37},{6,7,38,39},{8,9,40,41},{10,11,42,4..., dimensions={0}, use_global_device_ids=true | all-gather | bytes 327680 | tf_op jit(solution)/shard_map/all_gather | solution.py:641
  14.1 1.4 %shard_map.65 = (bf16[4,288,128]{2,1,0:T(8,128)(2,1)}, bf16[5,32,128]{2,1,0:T(8,128)(2,1)S(1)}) custom-call(bf16[4,256,128]{2,1,0:T(8,128)(2,1)S(1)} %bitcast.10, bf16[256,128]{1,0:T(8,128)(2,1)S(1)} %get-tuple-element.15.x, bf16[256,32]{1,0:T(8,128)(2,1)S(1)} %get-tuple-element.16.turned), custom_call_target="tpu_custom_call" | custom-call | flops 1000000 | bytes 1048576 | tf_op jit(solution)/shard_map/pallas_call | solution.py:528
  15.5 3.5 %all-to-all-start = ((bf16[4,288,128]{2,1,0:T(8,128)(2,1)}), bf16[4,288,128]{2,1,0:T(8,128)(2,1)S(1)}, u32[]{:S(2)}, u32[]{:S(2)}) async-start(bf16[4,288,128]{2,1,0:T(8,128)(2,1)} %get-tuple-element.22), calls=%async_computation | async-start | bytes 589824 | tf_op jit(solution)/shard_map/all_to_all | solution.py:643
  19.0 3.1 %shard_map.66 = (f32[264,128]{1,0:T(8,128)S(1)}, bf16[928,256]{1,0:T(8,128)(2,1)S(1)}, bf16[1536,64]{1,0:T(8,128)(2,1)S(1)}) custom-call(bf16[4,256,128]{2,1,0:T(8,128)(2,1)S(1)} %bitcast.11, bf16[256,128]{1,0:T(8,128)(2,1)S(1)} %get-tuple-element.15.x, bf16[2,4,9,64,64]{4,3,2,1,0:T(8,128)(2,1)S(1)} %get-tuple-element.18.near_low, ...), custom_call_target="tpu_custom_call" | custom-call | flops 1000000000 | bytes 1048576 | tf_op jit(solution)/shard_map/pallas_call | solution.py:528
  22.1 2.5 %all-to-all-done.cross = bf16[4,288,128]{2,1,0:T(8,128)(2,1)S(1)} async-done(((bf16[4,288,128]{2,1,0:T(8,128)(2,1)}), bf16[4,288,128]{2,1,0:T(8,128)(2,1)S(1)}, u32[]{:S(2)}, u32[]{:S(2)}) %all-to-all-start) | async-done | bytes 294944 | tf_op jit(solution)/shard_map/all_to_all | solution.py:643
  24.7 6.6 %all-gather.1 = bf16[16,32,128]{2,1,0:T(8,128)(2,1)S(1)} all-gather(bf16[4,32,128]{2,1,0:T(8,128)(2,1)S(1)} %slice.4), channel_id=3, replica_groups={{0,1,32,33},{2,3,34,35},{4,5,36,37},{6,7,38,39},{8,9,40,41},{10,11,42,4..., dimensions={0}, use_global_device_ids=true | all-gather | bytes 163840 | tf_op jit(solution)/shard_map/all_gather | solution.py:647
  31.3 2.4 %shard_map.67 = bf16[32,1024]{1,0:T(8,128)(2,1)} custom-call(bf16[4,256,128]{2,1,0:T(8,128)(2,1)S(1)} %bitcast.12, bf16[5,32,128]{2,1,0:T(8,128)(2,1)S(1)} %get-tuple-element.17.tiles, f32[264,128]{1,0:T(8,128)S(1)} %get-tuple-element.19.near_part, bf16[928,256]{1,0:T(8,128)(2,1)S(1)} %get-tuple-element.20.tables, ...), custom_call_target="tpu_custom_call" | custom-call | flops 1000000 | bytes 1048576 | tf_op jit(solution)/shard_map/pallas_call | solution.py:528
  (1 shorter events, 0.0 us)
Async XLA Ops:
  15.5 9.1 %all-to-all-start = ((bf16[4,288,128]{2,1,0:T(8,128)(2,1)}), bf16[4,288,128]{2,1,0:T(8,128)(2,1)S(1)}, u32[]{:S(2)}, u32[]{:S(2)}) async-start(bf16[4,288,128]{2,1,0:T(8,128)(2,1)} %get-tuple-element.22), calls=%async_computation | async-start | bytes 589824 | tf_op jit(solution)/shard_map/all_to_all | solution.py:643

commit v8 on v7

--- a/solution.py
+++ b/solution.py
@@ -151,31 +151,26 @@
 
     one = eye(32)
     copies[3].wait()
-    for n in range(8):
-        block = slice(n * 32, (n + 1) * 32)
-        turned[block, :] = dot_nt(one, transfer[block, :]).astype(BF)
+    blocks = [dot_nt(one, transfer[n * 32 : (n + 1) * 32, :]).astype(BF) for n in range(8)]
+    for j in range(2):
+        turned[32 * j : 32 * j + 32, :] = jnp.concatenate([blocks[j], blocks[2 + j]], axis=1)
+    for n in range(4):
+        turned[64 + 32 * n : 96 + 32 * n, 0:32] = blocks[4 + n]
     copies[4].wait()
 
 
 def lift(group, turned, tiles):
     slot = lax.rem(slot_of(32, 512), 4)
-    lines = [
-        jnp.concatenate(
-            [group[m, OWN_E0 + 32 * x : OWN_E0 + 32 * x + 32, :] for m in range(4)], axis=1
-        )
-        for x in range(4)
-    ]
-    matrices = [turned[32 * n : 32 * n + 32, :] for n in range(4)]
     e1 = jnp.zeros((32, 512), F32)
     for x in range(2):
-        parts = []
-        for j in range(2):
-            parts.append(dot(matrices[j], lines[2 * x]) + dot(matrices[2 + j], lines[2 * x + 1]))
-        joined = parts[0] + roll(parts[1], -32)
+        rows = slice(OWN_E0 + 64 * x, OWN_E0 + 64 * x + 64)
+        lines = jnp.concatenate([group[m, rows, :] for m in range(4)], axis=1)
+        parts = dot(turned[0:64, :], lines)
+        joined = parts[:32] + roll(parts[32:], -32)
         e1 = jnp.where(slot == 2 * x, roll(joined, 64 * x), e1)
         e1 = jnp.where(slot == 2 * x + 1, roll(joined, 64 * x - 32), e1)
     e1 = e1.astype(BF)
-    product = dot(turned[128:256, :], e1)
+    product = dot(turned[64:192, 0:32], e1)
     slot = slot_of(32)
     top = jnp.zeros((32, 128), F32)
     for m in range(4):
@@ -571,7 +566,7 @@
     return call(
         upward_kernel,
         (HBM,) * 5,
-        (VMEM((256, 128), BF), VMEM((OWN_ROWS, 128), BF), VMEM((2, 4, 9, 64, 64), BF), VMEM((256, 32), BF)),
+        (VMEM((256, 128), BF), VMEM((OWN_ROWS, 128), BF), VMEM((2, 4, 9, 64, 64), BF), VMEM((192, 64), BF)),
         (
             VMEM((8, 128), jnp.int32),
             VMEM((32, 1024), BF),

time: 33.9 us -> 33.8 us (level)
  no operation moved by 1% of the time
where the time goes in v8:
time: 33.8 us; the launch traced here: 33.6 us
  blocking collectives  19.1 us (57%)
  Pallas kernels  8.51 us (25%)
  starting transfers between devices  3.46 us (10%)
  waiting for transfers between devices  2.51 us (7%)
    all_gather x1, blocking collectives, local(): group = lax.all_gather(message, AXES, axis_index_groups=aligned)  12.5 us
    pallas_call x4, Pallas kernels, run(): pl.pallas_call(kernel, out_shape=shapes, in_specs=[pl.BlockSpec(memory_sp...  8.51 us
    all_gather x1, blocking collectives, local(): lax.all_gather(cross[:, FAR_E2:FAR_E2 + 32], AXES, axis_index_groups=alig...  6.6 us
    all_to_all x1, starting transfers between devices, local(): cross = lax.all_to_all(send, AXES, 0, 0, axis_index_groups=shifted)  3.46 us
    all_to_all x1, waiting for transfers between devices, local(): cross = lax.all_to_all(send, AXES, 0, 0, axis_index_groups=shifted)  2.51 us
  transfers between devices with their start and end apart: 1, of which 1 were waited for; matrix products, arithmetic and copies ran while one was open for 0% of the time, Pallas kernels for 9%

profile of v8, /device:TPU:1, one launch (start us, length us, event | category | flops | bytes accessed | tf_op | source)
XLA Modules:
  0.0 33.6 jit_solution(2495129837729253846)
XLA Ops:
  0.0 1.6 %shard_map.64 = (bf16[256,128]{1,0:T(8,128)(2,1)S(1)}, bf16[256,128]{1,0:T(8,128)(2,1)S(1)}, bf16[2,4,9,64,64]{4,3,2,1,0:T(8,128)(2,1)S(1)}, bf16[192,64]{1,0:T(8,128)(2,1)S(1)}) custom-call(bf16[32,1024]{1,0:T(8,128)(2,1)} %bitcast.19, s32[8,128]{1,0:T(8,128)} %bitcast.20, bf16[512,64]{1,0:T(8,128)(2,1)} %bitcast.15, bf16[256,32]{1,0:T(8,128)(2,1)} %bitcast.17, ...), custom_call_target="tpu_custom_call" | custom-call | flops 1000000 | bytes 1048576 | tf_op jit(solution)/shard_map/pallas_call | solution.py:523
  1.6 12.5 %all-gather = bf16[1024,128]{1,0:T(8,128)(2,1)S(1)} all-gather(bf16[256,128]{1,0:T(8,128)(2,1)S(1)} %get-tuple-element.14), channel_id=2, replica_groups={{0,1,32,33},{2,3,34,35},{4,5,36,37},{6,7,38,39},{8,9,40,41},{10,11,42,4..., dimensions={0}, use_global_device_ids=true | all-gather | bytes 327680 | tf_op jit(solution)/shard_map/all_gather | solution.py:636
  14.1 1.4 %shard_map.65 = (bf16[4,288,128]{2,1,0:T(8,128)(2,1)}, bf16[5,32,128]{2,1,0:T(8,128)(2,1)S(1)}) custom-call(bf16[4,256,128]{2,1,0:T(8,128)(2,1)S(1)} %bitcast.10, bf16[256,128]{1,0:T(8,128)(2,1)S(1)} %get-tuple-element.15.x, bf16[192,64]{1,0:T(8,128)(2,1)S(1)} %get-tuple-element.16.turned), custom_call_target="tpu_custom_call" | custom-call | flops 1000000 | bytes 1048576 | tf_op jit(solution)/shard_map/pallas_call | solution.py:523
  15.5 3.5 %all-to-all-start = ((bf16[4,288,128]{2,1,0:T(8,128)(2,1)}), bf16[4,288,128]{2,1,0:T(8,128)(2,1)S(1)}, u32[]{:S(2)}, u32[]{:S(2)}) async-start(bf16[4,288,128]{2,1,0:T(8,128)(2,1)} %get-tuple-element.22), calls=%async_computation | async-start | bytes 589824 | tf_op jit(solution)/shard_map/all_to_all | solution.py:638
  19.0 3.1 %shard_map.66 = (f32[264,128]{1,0:T(8,128)S(1)}, bf16[928,256]{1,0:T(8,128)(2,1)S(1)}, bf16[1536,64]{1,0:T(8,128)(2,1)S(1)}) custom-call(bf16[4,256,128]{2,1,0:T(8,128)(2,1)S(1)} %bitcast.11, bf16[256,128]{1,0:T(8,128)(2,1)S(1)} %get-tuple-element.15.x, bf16[2,4,9,64,64]{4,3,2,1,0:T(8,128)(2,1)S(1)} %get-tuple-element.18.near_low, ...), custom_call_target="tpu_custom_call" | custom-call | flops 1000000000 | bytes 1048576 | tf_op jit(solution)/shard_map/pallas_call | solution.py:523
  22.2 2.5 %all-to-all-done.cross = bf16[4,288,128]{2,1,0:T(8,128)(2,1)S(1)} async-done(((bf16[4,288,128]{2,1,0:T(8,128)(2,1)}), bf16[4,288,128]{2,1,0:T(8,128)(2,1)S(1)}, u32[]{:S(2)}, u32[]{:S(2)}) %all-to-all-start) | async-done | bytes 294944 | tf_op jit(solution)/shard_map/all_to_all | solution.py:638
  24.7 6.6 %all-gather.1 = bf16[16,32,128]{2,1,0:T(8,128)(2,1)S(1)} all-gather(bf16[4,32,128]{2,1,0:T(8,128)(2,1)S(1)} %slice.4), channel_id=3, replica_groups={{0,1,32,33},{2,3,34,35},{4,5,36,37},{6,7,38,39},{8,9,40,41},{10,11,42,4..., dimensions={0}, use_global_device_ids=true | all-gather | bytes 163840 | tf_op jit(solution)/shard_map/all_gather | solution.py:642
  31.3 2.4 %shard_map.67 = bf16[32,1024]{1,0:T(8,128)(2,1)} custom-call(bf16[4,256,128]{2,1,0:T(8,128)(2,1)S(1)} %bitcast.12, bf16[5,32,128]{2,1,0:T(8,128)(2,1)S(1)} %get-tuple-element.17.tiles, f32[264,128]{1,0:T(8,128)S(1)} %get-tuple-element.19.near_part, bf16[928,256]{1,0:T(8,128)(2,1)S(1)} %get-tuple-element.20.tables, ...), custom_call_target="tpu_custom_call" | custom-call | flops 1000000 | bytes 1048576 | tf_op jit(solution)/shard_map/pallas_call | solution.py:523
  (1 shorter events, 0.0 us)
Async XLA Ops:
  15.5 9.1 %all-to-all-start = ((bf16[4,288,128]{2,1,0:T(8,128)(2,1)}), bf16[4,288,128]{2,1,0:T(8,128)(2,1)S(1)}, u32[]{:S(2)}, u32[]{:S(2)}) async-start(bf16[4,288,128]{2,1,0:T(8,128)(2,1)} %get-tuple-element.22), calls=%async_computation | async-start | bytes 589824 | tf_op jit(solution)/shard_map/all_to_all | solution.py:638

commit v9 on v7

--- a/solution.py
+++ b/solution.py
@@ -222,11 +222,6 @@
     send[to, 0:FAR_CORNER, :] = jnp.zeros((FAR_CORNER, 128), BF)
     send[to, FAR_CORNER : FAR_CORNER + 64, :] = jnp.where(near_half, e0_rows, roll(x_row, 64))
     send[(2 * (1 - pi) + 1 - pj) ^ swap, 0:FAR_E1, :] = jnp.zeros((FAR_E1, 128), BF)
-    strips = pltpu.make_async_copy(
-        send.at[:, 0:FAR_E1, :], send_hbm.at[:, 0:FAR_E1, :], sems.at[0]
-    )
-    strips.start()
-
     lift(group, turned, tiles)
     for m in range(4):
         send[m, FAR_E1 : FAR_E1 + 32, :] = tiles[me]
@@ -234,12 +229,9 @@
         send[m, FAR_E2 : FAR_E2 + 32, :] = tiles[4]
     send[side_y, FAR_E1_SIDE : FAR_E1_SIDE + 32, :] = tiles[across_y]
     send[side_x, FAR_E1_SIDE : FAR_E1_SIDE + 32, :] = tiles[across_x]
-    levels = pltpu.make_async_copy(
-        send.at[:, FAR_E1:FAR_ROWS, :], send_hbm.at[:, FAR_E1:FAR_ROWS, :], sems.at[1]
-    )
-    levels.start()
-    strips.wait()
-    levels.wait()
+    whole = pltpu.make_async_copy(send, send_hbm, sems.at[0])
+    whole.start()
+    whole.wait()
 
 
 def store_row_of_tiles(halo, start, left, middle, right):

time: 33.9 us -> 33.9 us (level)
  no operation moved by 1% of the time
where the time goes in v9:
time: 33.9 us; the launch traced here: 33.6 us
  blocking collectives  19.1 us (56%)
  Pallas kernels  8.52 us (25%)
  starting transfers between devices  3.46 us (10%)
  waiting for transfers between devices  2.51 us (7%)
    all_gather x1, blocking collectives, local(): group = lax.all_gather(message, AXES, axis_index_groups=aligned)  12.5 us
    pallas_call x4, Pallas kernels, run(): pl.pallas_call(kernel, out_shape=shapes, in_specs=[pl.BlockSpec(memory_sp...  8.52 us
    all_gather x1, blocking collectives, local(): lax.all_gather(cross[:, FAR_E2:FAR_E2 + 32], AXES, axis_index_groups=alig...  6.61 us
    all_to_all x1, starting transfers between devices, local(): cross = lax.all_to_all(send, AXES, 0, 0, axis_index_groups=shifted)  3.46 us
    all_to_all x1, waiting for transfers between devices, local(): cross = lax.all_to_all(send, AXES, 0, 0, axis_index_groups=shifted)  2.51 us
  transfers between devices with their start and end apart: 1, of which 1 were waited for; matrix products, arithmetic and copies ran while one was open for 0% of the time, Pallas kernels for 9%

profile of v9, /device:TPU:1, one launch (start us, length us, event | category | flops | bytes accessed | tf_op | source)
XLA Modules:
  0.0 33.6 jit_solution(17699618485125917160)
XLA Ops:
  0.0 1.6 %shard_map.64 = (bf16[256,128]{1,0:T(8,128)(2,1)S(1)}, bf16[256,128]{1,0:T(8,128)(2,1)S(1)}, bf16[2,4,9,64,64]{4,3,2,1,0:T(8,128)(2,1)S(1)}, bf16[256,32]{1,0:T(8,128)(2,1)S(1)}) custom-call(bf16[32,1024]{1,0:T(8,128)(2,1)} %bitcast.19, s32[8,128]{1,0:T(8,128)} %bitcast.20, bf16[512,64]{1,0:T(8,128)(2,1)} %bitcast.15, bf16[256,32]{1,0:T(8,128)(2,1)} %bitcast.17, ...), custom_call_target="tpu_custom_call" | custom-call | flops 1000000 | bytes 1048576 | tf_op jit(solution)/shard_map/pallas_call | solution.py:520
  1.6 12.5 %all-gather = bf16[1024,128]{1,0:T(8,128)(2,1)S(1)} all-gather(bf16[256,128]{1,0:T(8,128)(2,1)S(1)} %get-tuple-element.14), channel_id=2, replica_groups={{0,1,32,33},{2,3,34,35},{4,5,36,37},{6,7,38,39},{8,9,40,41},{10,11,42,4..., dimensions={0}, use_global_device_ids=true | all-gather | bytes 327680 | tf_op jit(solution)/shard_map/all_gather | solution.py:633
  14.1 1.4 %shard_map.65 = (bf16[4,288,128]{2,1,0:T(8,128)(2,1)}, bf16[5,32,128]{2,1,0:T(8,128)(2,1)S(1)}) custom-call(bf16[4,256,128]{2,1,0:T(8,128)(2,1)S(1)} %bitcast.10, bf16[256,128]{1,0:T(8,128)(2,1)S(1)} %get-tuple-element.15.x, bf16[256,32]{1,0:T(8,128)(2,1)S(1)} %get-tuple-element.16.turned), custom_call_target="tpu_custom_call" | custom-call | flops 1000000 | bytes 1048576 | tf_op jit(solution)/shard_map/pallas_call | solution.py:520
  15.5 3.5 %all-to-all-start = ((bf16[4,288,128]{2,1,0:T(8,128)(2,1)}), bf16[4,288,128]{2,1,0:T(8,128)(2,1)S(1)}, u32[]{:S(2)}, u32[]{:S(2)}) async-start(bf16[4,288,128]{2,1,0:T(8,128)(2,1)} %get-tuple-element.22), calls=%async_computation | async-start | bytes 589824 | tf_op jit(solution)/shard_map/all_to_all | solution.py:635
  19.0 3.1 %shard_map.66 = (f32[264,128]{1,0:T(8,128)S(1)}, bf16[928,256]{1,0:T(8,128)(2,1)S(1)}, bf16[1536,64]{1,0:T(8,128)(2,1)S(1)}) custom-call(bf16[4,256,128]{2,1,0:T(8,128)(2,1)S(1)} %bitcast.11, bf16[256,128]{1,0:T(8,128)(2,1)S(1)} %get-tuple-element.15.x, bf16[2,4,9,64,64]{4,3,2,1,0:T(8,128)(2,1)S(1)} %get-tuple-element.18.near_low, ...), custom_call_target="tpu_custom_call" | custom-call | flops 1000000000 | bytes 1048576 | tf_op jit(solution)/shard_map/pallas_call | solution.py:520
  22.2 2.5 %all-to-all-done.cross = bf16[4,288,128]{2,1,0:T(8,128)(2,1)S(1)} async-done(((bf16[4,288,128]{2,1,0:T(8,128)(2,1)}), bf16[4,288,128]{2,1,0:T(8,128)(2,1)S(1)}, u32[]{:S(2)}, u32[]{:S(2)}) %all-to-all-start) | async-done | bytes 294944 | tf_op jit(solution)/shard_map/all_to_all | solution.py:635
  24.7 6.6 %all-gather.1 = bf16[16,32,128]{2,1,0:T(8,128)(2,1)S(1)} all-gather(bf16[4,32,128]{2,1,0:T(8,128)(2,1)S(1)} %slice.4), channel_id=3, replica_groups={{0,1,32,33},{2,3,34,35},{4,5,36,37},{6,7,38,39},{8,9,40,41},{10,11,42,4..., dimensions={0}, use_global_device_ids=true | all-gather | bytes 163840 | tf_op jit(solution)/shard_map/all_gather | solution.py:639
  31.3 2.4 %shard_map.67 = bf16[32,1024]{1,0:T(8,128)(2,1)} custom-call(bf16[4,256,128]{2,1,0:T(8,128)(2,1)S(1)} %bitcast.12, bf16[5,32,128]{2,1,0:T(8,128)(2,1)S(1)} %get-tuple-element.17.tiles, f32[264,128]{1,0:T(8,128)S(1)} %get-tuple-element.19.near_part, bf16[928,256]{1,0:T(8,128)(2,1)S(1)} %get-tuple-element.20.tables, ...), custom_call_target="tpu_custom_call" | custom-call | flops 1000000 | bytes 1048576 | tf_op jit(solution)/shard_map/pallas_call | solution.py:520
  (1 shorter events, 0.0 us)
Async XLA Ops:
  15.5 9.1 %all-to-all-start = ((bf16[4,288,128]{2,1,0:T(8,128)(2,1)}), bf16[4,288,128]{2,1,0:T(8,128)(2,1)S(1)}, u32[]{:S(2)}, u32[]{:S(2)}) async-start(bf16[4,288,128]{2,1,0:T(8,128)(2,1)} %get-tuple-element.22), calls=%async_computation | async-start | bytes 589824 | tf_op jit(solution)/shard_map/all_to_all | solution.py:635
